TPU v7x, 128 devices: a whole 4x4x4 slice. The times are simulated.
128 devices in a mesh: blk: 16 (over z, y), pair: 8 (over x, core).
Axes of the slice: x: 4, y: 4, z: 4, core: 2. Of those that a mesh axis runs over, the one named last changes fastest.
Arguments:
- amplitudes: bfloat16 [128, 524288], P('pair', 'blk'), may hold values from -6 to 6
- integrals: bfloat16 [10240, 4, 128, 128], P(('blk', 'pair')), may hold values from -0.25 to 0.25
- block_irrep: int32 [4096], replicated, may hold values from 0 to 7
- slab_blocks: int32 [32], replicated, may hold values from 0 to 4095, as said below
- owner: int32 [4096], replicated, may hold values from 0 to 127, as said below
- partner: int32 [4096], replicated, may hold values from 0 to 4095, as said below
- sign: int32 [4096], replicated, may hold values from -1 to 1, as said below
Outputs:
- ladder: bfloat16 [128, 524288], P('pair', 'blk')
Inputs may be any that keep to these rules, and one draw needn't show every extreme that they name: Distinct blocks; block_irrep[slab_blocks[g * 4 + k]] = g. `owner`: flat device index (blk index times the pair axis's size plus pair index). For each blk index t, of the blocks t * 256 to t * 256 + 255 exactly 256 divided by the pair axis's size are stored on each pair index, at most 5 on any one device, and some device stores exactly 5 of them for every t. Integral rows not named by any block are read by no output. An involution without fixed points; for any blk indices t and t2, equal or not, exactly 256 divided by the blk axis's size of the blocks of t have their partner among the blocks of t2. `sign`: each entry is -1 or 1.
All inputs are finite; a program needn't handle non-finite values.
Results may differ from a plain program's by a relative error of at most 0.001.
Values may be sent and summed in bfloat16 or wider, within the bound.
No kernel may reach another device: no remote copies, remote signals or barrier semaphores. Data moves between devices by JAX's collectives and lax.ppermute only.
A program may use at most 128 MiB of HBM per device.

v0:
```python
import jax
import jax.numpy as jnp
from jax import lax
from jax.sharding import PartitionSpec as P


def partner_2(value, axis, distance):
    mask = 2**distance
    pairs = [(source, source ^ mask) for source in range(lax.axis_size(axis))]
    return lax.ppermute(value, axis, pairs)


def earlier_matches(labels):
    span_length = labels.shape[1]
    position_ids = jnp.arange(span_length, dtype=jnp.int32)
    earlier_mask = position_ids[None, :] < position_ids[:, None]
    same_label = labels[:, :, None] == labels[:, None, :]
    return jnp.sum(jnp.logical_and(same_label, earlier_mask[None]), axis=2)


def slot_products(slab_grouped, my_irrep, tile_matrix, blk_count, capacity):
    total_pairs, irrep_count, inner_depth = slab_grouped.shape
    tile_width = tile_matrix.shape[2]
    irrep_groups = my_irrep.reshape(blk_count, capacity)
    tile_groups = tile_matrix.reshape(blk_count, capacity, inner_depth, tile_width)

    def one_group(operands):
        group_irreps, group_tiles = operands
        chosen = jnp.take(slab_grouped, group_irreps, axis=1)
        return jnp.einsum("psk,skw->spw", chosen, group_tiles, preferred_element_type=jnp.float32)

    return lax.map(one_group, (irrep_groups, tile_groups))


def local(amplitudes, integrals, block_irrep, slab_blocks, owner, partner, sign):
    ij_rows, columns = amplitudes.shape
    slot_count = integrals.shape[0]
    per_irrep = integrals.shape[1]
    tile_width = integrals.shape[3]
    blk_count = lax.axis_size("blk")
    pair_count = lax.axis_size("pair")
    block_span = columns // tile_width
    total_pairs = ij_rows * pair_count
    capacity = slot_count // blk_count
    group_len = block_span // pair_count
    inner_depth = per_irrep * tile_width
    irrep_count = slab_blocks.shape[0] // per_irrep
    block_index = lax.axis_index("blk")
    pair_index = lax.axis_index("pair")
    device_index = block_index * pair_count + pair_index
    local_ids = block_index * block_span + jnp.arange(block_span, dtype=jnp.int32)
    picker = (local_ids[:, None] == slab_blocks[None, :]).astype(jnp.bfloat16)
    amp_blocks = amplitudes.reshape(ij_rows, block_span, tile_width)
    picked = jnp.einsum("rbw,bn->rnw", amp_blocks, picker, preferred_element_type=jnp.float32)
    picked = picked.reshape(ij_rows, slab_blocks.shape[0] * tile_width)
    slab_part = lax.psum(picked.astype(jnp.bfloat16), "blk")
    slab_matrix = lax.all_gather(slab_part, "pair", axis=0, tiled=True)
    block_ranks = earlier_matches(owner.reshape(blk_count, block_span)).reshape(-1)
    all_ids = jnp.arange(owner.shape[0], dtype=jnp.int32)
    slot_ids = owner * slot_count + all_ids // block_span * capacity + block_ranks
    slot_irrep = (
        jnp.zeros((blk_count * pair_count * slot_count,), jnp.int32).at[slot_ids].set(block_irrep)
    )
    my_irrep = lax.dynamic_slice_in_dim(slot_irrep, device_index * slot_count, slot_count)
    slab_grouped = slab_matrix.reshape(total_pairs, irrep_count, inner_depth)
    tile_matrix = integrals.reshape(slot_count, inner_depth, tile_width)
    my_owner = lax.dynamic_slice_in_dim(owner, block_index * block_span, block_span)
    my_ranks = lax.dynamic_slice_in_dim(block_ranks, block_index * block_span, block_span)
    products = slot_products(slab_grouped, my_irrep, tile_matrix, blk_count, capacity)
    products = products.reshape(slot_count, total_pairs, tile_width)
    arrived = lax.all_to_all(products, "blk", split_axis=0, concat_axis=0, tiled=True)
    stored_pair = my_owner % pair_count
    pair_ranks = earlier_matches(stored_pair[None, :])[0]
    first_position = my_owner // pair_count * capacity + my_ranks
    target_slot = jnp.where(stored_pair == pair_index, pair_ranks, group_len)
    pick_index = jnp.zeros((group_len,), jnp.int32).at[target_slot].set(first_position, mode="drop")
    gathered = jnp.take(arrived, pick_index, axis=0)
    split_rows = gathered.reshape(group_len, pair_count, ij_rows, tile_width)
    rows_arrived = lax.all_to_all(split_rows, "pair", split_axis=1, concat_axis=0, tiled=True)
    rows_arrived = rows_arrived.reshape(-1, ij_rows, tile_width)
    own_products = jnp.take(rows_arrived, stored_pair * group_len + pair_ranks, axis=0)
    my_partner = lax.dynamic_slice_in_dim(partner, block_index * block_span, block_span)
    send_order = jnp.argsort(my_partner // block_span, stable=True)
    outgoing = jnp.take(own_products, send_order, axis=0)
    incoming = lax.all_to_all(outgoing, "blk", split_axis=0, concat_axis=0, tiled=True)
    arrival_order = jnp.argsort(my_partner, stable=True)
    inverse = jnp.argsort(arrival_order, stable=True)
    facing = jnp.take(incoming, inverse, axis=0)
    high_bit = pair_count.bit_length() - 2
    mirrored = partner_2(facing, "pair", high_bit)
    my_sign = lax.dynamic_slice_in_dim(sign, block_index * block_span, block_span).astype(
        jnp.float32
    )
    summed = own_products + my_sign[:, None, None] * mirrored
    result = summed.astype(jnp.bfloat16)
    return jnp.transpose(result, (1, 0, 2)).reshape(ij_rows, columns)


def solution(mesh):
    placed = (P("pair", "blk"), P(("blk", "pair"), None, None, None), P(), P(), P(), P(), P())
    return jax.shard_map(
        local, mesh=mesh, in_specs=placed, out_specs=P("pair", "blk"), check_vma=False
    )
```

profile of v0, /device:TPU:0, one launch (start us, length us, event | category | flops | bytes accessed | tf_op | source)
XLA Modules:
  0.0 399.8 jit_solution(17845784036686425707)
XLA Ops:
  9.1 86.4 %all-reduce.2.cloned.1.call-done = bf16[16,4096]{1,0:T(8,128)(2,1)} async-done(((bf16[16,4096]{1,0:T(8,128)(2,1)}), bf16[16,4096]{1,0:T(8,128)(2,1)}) %all-reduce.2.cloned.1.call-update) | async-done | bytes 131088 | tf_op jit(solution)/shard_map/psum | solution.py:56
  96.9 15.7 %scatter_custom_fusion.1 = s32[10240]{0:T(1024)S(1)} fusion(s32[4096]{0:T(1024)S(1)} %compare_select_fusion.2, s32[4096]{0:T(1024)} %param.13, s32[]{:T(128)} %constant.111.clone.1), kind=kCustom, calls=%fused_computation.44 | custom fusion | bytes 41472 | tf_op jit(solution)/shard_map/scatter | solution.py:62
  112.8 7.1 %all-gather.2.cloned.1.call-done = bf16[128,4096]{1,0:T(8,128)(2,1)} async-done(((bf16[16,4096]{1,0:T(8,128)(2,1)}), bf16[128,4096]{1,0:T(8,128)(2,1)}) %all-gather.2.cloned.1.call-update) | async-done | bytes 1048592 | tf_op jit(solution)/shard_map/all_gather | solution.py:57
  122.1 45.4 %while.10 = (s32[]{:T(128)}, f32[16,5,128,128]{3,2,1,0:T(8,128)}, s32[16,5]{1,0:T(8,128)S(1)}, bf16[128,8,512]{2,0,1:T(8,128)(2,1)S(1)}, bf16[16,5,512,128]{3,2,1,0:T(8,128)(2,1)}, /*index=5*/s32[]{:T(128)}) while((s32[]{:T(128)}, f32[16,5,128,128]{3,2,1,0:T(8,128)}, s32[16,5]{1,0:T(8,128)S(1)}, bf16[128,8,512]{2,0,1:T(8,128)(2,1)S(1)}, ...), condition=%wide.region_6.7_spmd, body=%wide.region_5.6_spmd.sunk | while | flops 84214832 | bytes 2954427 | solution.py:32
  125.6 2.2 fusion.35
  128.4 2.2 fusion.35
  131.2 2.2 fusion.35
  134.1 2.2 fusion.35
  139.7 2.2 fusion.35
  142.6 2.2 fusion.35
  145.4 2.2 fusion.35
  148.2 2.2 fusion.35
  151.1 2.2 fusion.35
  156.8 2.2 fusion.35
  162.4 2.2 fusion.35
  165.2 2.2 fusion.35
  167.5 7.0 %all-to-all-start = ((f32[80,128,128]{2,1,0:T(8,128)}), f32[80,128,128]{2,1,0:T(8,128)}, u32[]{:S(2)}, u32[]{:S(2)}) async-start(f32[80,128,128]{2,1,0:T(8,128)} %bitcast.58), calls=%async_computation | async-start | bytes 10485760 | tf_op jit(solution)/shard_map/all_to_all | solution.py:71
  176.9 76.5 %all-to-all-done = f32[80,128,128]{2,1,0:T(8,128)} async-done(((f32[80,128,128]{2,1,0:T(8,128)}), f32[80,128,128]{2,1,0:T(8,128)}, u32[]{:S(2)}, u32[]{:S(2)}) %all-to-all-start) | async-done | bytes 5242912 | tf_op jit(solution)/shard_map/all_to_all | solution.py:71
  253.4 3.2 gather_fusion.1
  258.3 3.6 all-to-all-start.1
  261.9 3.2 sort.45
  265.1 23.9 %all-to-all-done.1 = f32[32,8,16,128]{3,2,0,1:T(8,128)S(1)} async-done(((f32[32,8,16,128]{3,2,0,1:T(8,128)}), f32[32,8,16,128]{3,2,0,1:T(8,128)S(1)}, u32[]{:S(2)}, u32[]{:S(2)}) %all-to-all-start.1) | async-done | bytes 2097184 | tf_op jit(solution)/shard_map/all_to_all | solution.py:79
  290.4 2.3 gather_fusion.2
  294.4 3.6 gather_fusion.3
  298.0 3.2 broadcast_select_fusion.1
  301.3 5.3 %all-to-all-start.2 = ((f32[256,16,128]{2,1,0:T(8,128)}), f32[256,16,128]{2,1,0:T(8,128)}, u32[]{:S(2)}, u32[]{:S(2)}) async-start(f32[256,16,128]{2,1,0:T(8,128)} %broadcast_select_fusion.1), calls=%async_computation.2 | async-start | bytes 4194304 | tf_op jit(solution)/shard_map/all_to_all | solution.py:85
  306.6 3.2 sort.46
  309.8 3.2 sort.47
  313.0 24.8 %all-to-all-done.2 = f32[256,16,128]{2,1,0:T(8,128)} async-done(((f32[256,16,128]{2,1,0:T(8,128)}), f32[256,16,128]{2,1,0:T(8,128)}, u32[]{:S(2)}, u32[]{:S(2)}) %all-to-all-start.2) | async-done | bytes 2097184 | tf_op jit(solution)/shard_map/all_to_all | solution.py:85
  337.8 3.6 gather_fusion.4
  345.2 45.5 %collective-permute-done = f32[256,16,128]{2,1,0:T(8,128)S(1)} collective-permute-done((f32[256,16,128]{2,1,0:T(8,128)S(1)}, f32[256,16,128]{2,1,0:T(8,128)S(1)}, u32[]{:S(2)}, u32[]{:S(2)}) %collective-permute-start) | collective-permute-done | bytes 2097184 | tf_op jit(solution)/shard_map/ppermute | solution.py:10
  390.6 2.4 copy_bitcast_fusion
  (116 shorter events, 35.8 us)
Async XLA Ops:
  6.5 1.4 copy-start.2
  6.5 89.0 %copy-start.1 = (s32[4096]{0:T(1024)S(1)}, s32[4096]{0:T(1024)}, u32[]{:S(2)}) copy-start(s32[4096]{0:T(1024)} %param.15) | copy-start | bytes 49156
  6.5 88.9 %all-reduce.2.cloned.1.call-start = ((), (), s32[]{:S(2)}) async-start(), calls=%async_computation.3 | async-start | bytes 262144 | tf_op jit(solution)/shard_map/psum | solution.py:56
  9.0 110.9 %all-gather.2.cloned.1.call-start = ((), (), s32[]{:S(2)}) async-start(), calls=%async_computation.4 | async-start | bytes 1179648 | tf_op jit(solution)/shard_map/all_gather | solution.py:57
  167.5 85.9 %all-to-all-start = ((f32[80,128,128]{2,1,0:T(8,128)}), f32[80,128,128]{2,1,0:T(8,128)}, u32[]{:S(2)}, u32[]{:S(2)}) async-start(f32[80,128,128]{2,1,0:T(8,128)} %bitcast.58), calls=%async_computation | async-start | bytes 10485760 | tf_op jit(solution)/shard_map/all_to_all | solution.py:71
  258.3 30.7 %all-to-all-start.1 = ((f32[32,8,16,128]{3,2,0,1:T(8,128)}), f32[32,8,16,128]{3,2,0,1:T(8,128)S(1)}, u32[]{:S(2)}, u32[]{:S(2)}) async-start(f32[32,8,16,128]{3,2,0,1:T(8,128)} %copy.19), calls=%async_computation.1 | async-start | bytes 4194304 | tf_op jit(solution)/shard_map/all_to_all | solution.py:79
  289.0 1.4 copy-start
  301.3 36.5 %all-to-all-start.2 = ((f32[256,16,128]{2,1,0:T(8,128)}), f32[256,16,128]{2,1,0:T(8,128)}, u32[]{:S(2)}, u32[]{:S(2)}) async-start(f32[256,16,128]{2,1,0:T(8,128)} %broadcast_select_fusion.1), calls=%async_computation.2 | async-start | bytes 4194304 | tf_op jit(solution)/shard_map/all_to_all | solution.py:85
  343.3 47.3 %collective-permute-start = (f32[256,16,128]{2,1,0:T(8,128)S(1)}, f32[256,16,128]{2,1,0:T(8,128)S(1)}, u32[]{:S(2)}, u32[]{:S(2)}) collective-permute-start(f32[256,16,128]{2,1,0:T(8,128)S(1)} %broadcast_select_fusion), channel_id=1, source_target_pairs={{0,4},{1,5},{2,6},{3,7},{4,0},{5,1},{6,2},{7,3},{8,12},{9,13},{10,... | collective-permute-start | bytes 6291464 | tf_op jit(solution)/shard_map/ppermute | solution.py:10
Sparse Core Ops, SparseCore 0:
  10.6 84.8 all-reduce.1
  97.3 22.5 all-gather.1
where the time goes:
time: 401 us; the launch traced here: 400 us
  waiting for transfers between devices  264 us (66%)
  local copies, waits for them, and re-layouts  46.6 us (12%)
  matrix products  35.5 us (9%)
  other arithmetic  22.6 us (6%)
  starting transfers between devices  17 us (4%)
  between operations  13.7 us (3%)
    psum x1, waiting for transfers between devices, local(): slab_part = lax.psum(picked.astype(jnp.bfloat16), 'blk')  86.4 us
    all_to_all x1, waiting for transfers between devices, local(): lax.all_to_all(products, 'blk', split_axis=0, concat_axis=0, tiled=True)  76.5 us
    ppermute x1, waiting for transfers between devices, partner_2(): return lax.ppermute(value, axis, pairs)  45.5 us
    dot_general x16, matrix products, one_group(): jnp.einsum('psk,skw->spw', chosen, group_tiles, preferred_element_type=jn...  35.2 us
    all_to_all x1, waiting for transfers between devices, local(): lax.all_to_all(outgoing, 'blk', split_axis=0, concat_axis=0, tiled=True)  24.8 us
    all_to_all x1, waiting for transfers between devices, local(): lax.all_to_all(split_rows, 'pair', split_axis=1, concat_axis=0, tiled=True)  23.9 us
    scatter x1, local copies, waits for them, and re-layouts, local(): jnp.zeros((blk_count * pair_count * slot_count,), jnp.int32).at[slot_ids]  15.7 us
    gather x16, local copies, waits for them, and re-layouts, one_group(): chosen = jnp.take(slab_grouped, group_irreps, axis=1)  9.4 us
  transfers between devices with their start and end apart: 6, of which 6 were waited for; matrix products, arithmetic and copies ran while one was open for 7% of the time, Pallas kernels for 0%

commit v1 on v0

v1 whole, which is shorter than its diff:
```python
import jax
import jax.numpy as jnp
from jax import lax
from jax.experimental import pallas as pl
from jax.experimental.pallas import tpu as pltpu
from jax.sharding import PartitionSpec as P

BOTH = ("blk", "pair")
TOP = 32760.0
STEPS = 64.0
LN2 = 0.6931471805599453
MIB = 1 << 20


def call(body, grid, prefetch, ins, outs, shapes, scratch, vmem, cost):
    spec = pltpu.PrefetchScalarGridSpec(
        num_scalar_prefetch=prefetch, grid=grid, in_specs=ins, out_specs=outs, scratch_shapes=scratch
    )
    return pl.pallas_call(
        body,
        grid_spec=spec,
        out_shape=shapes,
        compiler_params=pltpu.CompilerParams(vmem_limit_bytes=vmem),
        cost_estimate=pl.CostEstimate(flops=cost[0], bytes_accessed=cost[1], transcendentals=0),
    )


def whole(shape):
    return pl.BlockSpec(shape, lambda i, *_: (0,) * len(shape))


def extract_body(where_ref, amp_ref, out_ref):
    for n in range(32):
        place = where_ref[n]
        start = pl.multiple_of(jnp.maximum(place, 0) * 128, 128)
        tile = amp_ref[:, pl.ds(start, 128)]
        held = jnp.where(place >= 0, tile, jnp.zeros_like(tile))
        out_ref[n // 2, :, (n % 2) * 128 : (n % 2) * 128 + 128] = held


def merge_body(in_ref, out_ref):
    total = in_ref[0].astype(jnp.float32)
    for s in range(1, 16):
        total += in_ref[s].astype(jnp.float32)
    part = total.astype(jnp.bfloat16)
    for s in range(64):
        out_ref[s] = part


def row_tiles(p):
    return (2 * p, 2 * p + 8) if p < 4 else (2 * (p - 4) + 9, 2 * (p - 4) + 1)


def product_body(irrep_ref, core_ref, mine_ref, other_ref, tile_ref, out_ref, slab, prod, peak, code):
    step = pl.program_id(0)

    @pl.when(step == 0)
    def _():
        core = core_ref[0]
        for source, shift in ((mine_ref, core), (other_ref, 1 - core)):
            for c in range(16):
                for x in range(4):
                    rows = pl.ds(pl.multiple_of((2 * x + shift) * 16, 16), 16)
                    slab[c // 2, rows, (c % 2) * 256 : (c % 2) * 256 + 256] = source[c * 4 + x]
        peak[...] = jnp.zeros_like(peak)

    @pl.when(step < 16)
    def _():
        top = peak[...]
        for k in range(5):
            slot = step * 5 + k
            irrep = irrep_ref[slot]
            left = slab[jnp.maximum(irrep, 0)]
            right = tile_ref[k].reshape(512, 128)
            value = jnp.dot(left, right, preferred_element_type=jnp.float32)
            prod[slot] = value
            high = jnp.max(jnp.abs(value).reshape(16, 8, 128), axis=0)
            top = jnp.maximum(top, jnp.where(irrep >= 0, high, 0.0))
        peak[...] = top

    @pl.when(step == 16)
    def _():
        top = jnp.max(jnp.max(peak[...], axis=1, keepdims=True), axis=0, keepdims=True)
        level = jnp.ceil(jnp.log(jnp.maximum(top, 1e-30)) * (STEPS / LN2))
        code[...] = jnp.broadcast_to(level, (8, 128)).astype(jnp.int32)

    @pl.when(step >= 16)
    def _():
        level = code[...]
        inverse = jnp.exp(level.astype(jnp.float32) * (-LN2 / STEPS)) * TOP
        for k in range(5):
            slot = (step - 16) * 5 + k
            for p in range(8):
                words = []
                for u in row_tiles(p):
                    value = prod[slot, u * 8 : u * 8 + 8, :]
                    words.append(jnp.floor(value * inverse + 0.5).astype(jnp.int32))
                out_ref[0, p, k] = (words[0] << 16) | (words[1] & 0xFFFF)
        for p in range(8):
            out_ref[0, p, 5] = level


def select_body(from_ref, to_ref, in_ref, out_ref):
    def one(j, carry):
        out_ref[to_ref[j]] = in_ref[from_ref[j]]
        return carry

    lax.fori_loop(0, 256, one, 0, unroll=8)


def combine_body(own_ref, own_scale_ref, face_ref, face_scale_ref, sign_ref, here_ref, there_ref, keep_ref, send_ref):
    def scale(index):
        return jnp.exp(here_ref[index].astype(jnp.float32) * (LN2 / STEPS)) * (1.0 / TOP)

    def one(j, carry):
        own = here_ref[own_ref[j]]
        face = there_ref[face_ref[j]]
        own_scale = scale(own_scale_ref[j])
        face_scale = scale(face_scale_ref[j]) * sign_ref[j].astype(jnp.float32)
        own_high = (own >> 16).astype(jnp.float32)
        own_low = ((own << 16) >> 16).astype(jnp.float32)
        face_high = (face >> 16).astype(jnp.float32)
        face_low = ((face << 16) >> 16).astype(jnp.float32)
        columns = pl.ds(pl.multiple_of(j * 128, 128), 128)
        keep_ref[:, columns] = (own_high * own_scale + face_low * face_scale).astype(jnp.bfloat16)
        send_ref[:, columns] = (own_low * own_scale + face_high * face_scale).astype(jnp.bfloat16)
        return carry

    lax.fori_loop(0, 256, one, 0, unroll=4)


def local(amplitudes, integrals, block_irrep, slab_blocks, owner, partner, sign):
    blk = lax.axis_index("blk")
    pair = lax.axis_index("pair")
    me = blk * 8 + pair
    int32 = jnp.int32

    where = jnp.where(slab_blocks // 256 == blk, slab_blocks % 256, -1).astype(int32)
    parts = call(
        extract_body, (1,), 1, [whole((16, 32768))], whole((16, 16, 256)),
        jax.ShapeDtypeStruct((16, 16, 256), jnp.bfloat16), [], 8 * MIB, (0, 1 << 20),
    )(where, amplitudes)
    parts = lax.all_to_all(parts, "blk", split_axis=0, concat_axis=0, tiled=True)
    copies = call(
        merge_body, (1,), 0, [whole((16, 16, 256))], whole((64, 16, 256)),
        jax.ShapeDtypeStruct((64, 16, 256), jnp.bfloat16), [], 8 * MIB, (0, 1 << 20),
    )(parts)
    groups = [[c + 2 * i for i in range(64)] for c in range(2)]
    mine = lax.all_to_all(copies, BOTH, split_axis=0, concat_axis=0, tiled=True, axis_index_groups=groups)
    other = lax.ppermute(mine, "pair", [(i, i ^ 1) for i in range(8)])

    ids = jnp.arange(256, dtype=int32)
    stored = (owner == me).reshape(16, 256)
    earlier = (ids[:, None] < ids[None, :]).astype(jnp.bfloat16)
    slot_rank = jnp.dot(stored.astype(jnp.bfloat16), earlier, preferred_element_type=jnp.float32).astype(int32)
    labels = block_irrep.reshape(16, 256) + 1
    chosen = stored[:, None, :] & (slot_rank[:, None, :] == jnp.arange(5, dtype=int32)[None, :, None])
    slot_irrep = (jnp.sum(jnp.where(chosen, labels[:, None, :], 0), axis=2) - 1).reshape(80)

    my_owner = lax.dynamic_slice_in_dim(owner, blk * 256, 256)
    my_partner = lax.dynamic_slice_in_dim(partner, blk * 256, 256)
    my_sign = lax.dynamic_slice_in_dim(sign, blk * 256, 256)
    before = ids[None, :] < ids[:, None]
    rank = jnp.sum((my_owner[None, :] == my_owner[:, None]) & before, axis=1).astype(int32)
    arrive = my_owner * 6 + rank
    target = my_partner // 256
    leave_key = target * 256 + ids
    leave = jnp.sum(leave_key[None, :] < leave_key[:, None], axis=1).astype(int32)
    back = jnp.sum(my_partner[None, :] < my_partner[:, None], axis=1).astype(int32)
    all_ids = jnp.arange(4096, dtype=int32)
    face_owner = jnp.sum(jnp.where(my_partner[:, None] == all_ids[None, :], owner[None, :], 0), axis=1)

    core = (pair % 2).reshape(1).astype(int32)
    coded = call(
        product_body, (32,), 2,
        [
            whole((64, 16, 256)),
            whole((64, 16, 256)),
            pl.BlockSpec((5, 4, 128, 128), lambda i, *_: (jnp.minimum(i, 15), 0, 0, 0)),
        ],
        pl.BlockSpec((1, 8, 6, 8, 128), lambda i, *_: (jnp.maximum(i - 16, 0), 0, 0, 0, 0)),
        jax.ShapeDtypeStruct((16, 8, 6, 8, 128), int32),
        [
            pltpu.VMEM((8, 128, 512), jnp.bfloat16),
            pltpu.VMEM((80, 128, 128), jnp.float32),
            pltpu.VMEM((8, 128), jnp.float32),
            pltpu.VMEM((8, 128), int32),
        ],
        24 * MIB, (1_342_177_280, 14 << 20),
    )(slot_irrep, core, mine, other, integrals)
    arrived = lax.all_to_all(coded.reshape(128, 48, 128), BOTH, split_axis=0, concat_axis=0, tiled=True)
    arrived = arrived.reshape(768, 8, 128)
    outgoing = call(
        select_body, (1,), 2, [whole((768, 8, 128))], whole((256, 8, 128)),
        jax.ShapeDtypeStruct((256, 8, 128), int32), [], 16 * MIB, (0, 4 << 20),
    )(arrive, leave, arrived)
    incoming = lax.all_to_all(outgoing, "blk", split_axis=0, concat_axis=0, tiled=True)
    half = jax.ShapeDtypeStruct((8, 32768), jnp.bfloat16)
    keep, send = call(
        combine_body, (1,), 5, [whole((768, 8, 128)), whole((256, 8, 128))],
        [whole((8, 32768)), whole((8, 32768))], [half, half], [], 16 * MIB, (0, 5 << 20),
    )(arrive, my_owner * 6 + 5, back, face_owner * 6 + 5, my_sign, arrived, incoming)
    got = lax.ppermute(send, "pair", [(i, i ^ 4) for i in range(8)])
    first = pair < 4
    return jnp.concatenate([jnp.where(first, keep, got), jnp.where(first, got, keep)], axis=0)


def solution(mesh):
    placed = (P("pair", "blk"), P(BOTH, None, None, None), P(), P(), P(), P(), P())
    return jax.shard_map(local, mesh=mesh, in_specs=placed, out_specs=P("pair", "blk"), check_vma=False)
```

time: 401 us -> 146 us (0.36)
  waiting for transfers between devices: 264 us -> 81.2 us
  local copies, waits for them, and re-layouts: 46.6 us -> 9.58 us
  matrix products: 35.5 us -> 0.15 us
  other arithmetic: 22.6 us -> 6.55 us
  blocking collectives: 0 us -> 15.9 us
  Pallas kernels: 0 us -> 15.1 us
  between operations: 13.7 us -> 0.14 us
    psum x1 -> x0, waiting for transfers between devices: 86.4 us -> none  [local(): slab_part = lax.psum(picked.astype(jnp.bfloat16), 'blk')]
    all_to_all x2, waiting for transfers between devices: 100 us -> 51.1 us  [the longest x1 40.4 us: local(): lax.all_to_all(coded.reshape(128, 48, 128), BOTH, split_axis=0, concat_ax...]
    dot_general x17 -> x1, matrix products: 35.5 us -> 0.15 us  [local(): jnp.dot(stored.astype(jnp.bfloat16), earlier, preferred_element_type=jnp....]
    ppermute x1 -> x2, waiting for transfers between devices: 45.5 us -> 14.3 us  [the longest x1 12.9 us: local(): got = lax.ppermute(send, 'pair', [(i, i ^ 4) for i in range(8)])]
    gather x20 -> x0, local copies, waits for them, and re-layouts: 22.2 us -> none  [the longest x16 9.4 us: one_group(): chosen = jnp.take(slab_grouped, group_irreps, axis=1)]
    scatter x2 -> x0, local copies, waits for them, and re-layouts: 17.1 us -> none  [the longest x1 15.7 us: local(): jnp.zeros((blk_count * pair_count * slot_count,), jnp.int32).at[slot_ids]]
    all_to_all x0 -> x1, blocking collectives: none -> 15.9 us  [local(): lax.all_to_all(parts, 'blk', split_axis=0, concat_axis=0, tiled=True)]
    pallas_call x0 -> x5, Pallas kernels: none -> 15.1 us  [the longest x1 7.82 us: local(): call(product_body, (32,), 2, [whole((64, 16, 256)), whole((64, 16, 256)),...]
  transfers between devices with their start and end apart: 6 -> 5, of which waited for: 6 -> 5; matrix products, arithmetic and copies ran while one was open for 7% -> 3% of each run, Pallas kernels for 0% -> 0%
where the time goes in v1:
time: 146 us; the launch traced here: 145 us
  waiting for transfers between devices  81.2 us (56%)
  starting transfers between devices  16.1 us (11%)
  blocking collectives  15.9 us (11%)
  Pallas kernels  15.1 us (10%)
  local copies, waits for them, and re-layouts  9.58 us (7%)
  other arithmetic  6.55 us (4%)
    all_to_all x1, waiting for transfers between devices, local(): lax.all_to_all(coded.reshape(128, 48, 128), BOTH, split_axis=0, concat_ax...  40.4 us
    all_to_all x1, blocking collectives, local(): lax.all_to_all(parts, 'blk', split_axis=0, concat_axis=0, tiled=True)  15.9 us
    all_to_all x1, waiting for transfers between devices, local(): lax.all_to_all(outgoing, 'blk', split_axis=0, concat_axis=0, tiled=True)  15.8 us
    ppermute x1, waiting for transfers between devices, local(): got = lax.ppermute(send, 'pair', [(i, i ^ 4) for i in range(8)])  12.9 us
    all_to_all x1, waiting for transfers between devices, local(): lax.all_to_all(copies, BOTH, split_axis=0, concat_axis=0, tiled=True, axi...  10.7 us
    unnamed x12, local copies, waits for them, and re-layouts  8.62 us
    pallas_call x1, Pallas kernels, local(): call(product_body, (32,), 2, [whole((64, 16, 256)), whole((64, 16, 256)),...  7.82 us
    all_to_all x1, starting transfers between devices, local(): lax.all_to_all(copies, BOTH, split_axis=0, concat_axis=0, tiled=True, axi...  6.64 us
  transfers between devices with their start and end apart: 5, of which 5 were waited for; matrix products, arithmetic and copies ran while one was open for 3% of the time, Pallas kernels for 0%

profile of v1, /device:TPU:0, one launch (start us, length us, event | category | flops | bytes accessed | tf_op | source)
XLA Modules:
  0.0 144.8 jit_solution(17295034380102836820)
XLA Ops:
  0.0 0.7 compare_select_fusion.where_ref
  0.7 1.2 copy-done.3
  1.9 0.6 shard_map.73
  2.5 15.9 %all_to_all.20.in_ref = bf16[16,16,256]{2,1,0:T(8,128)(2,1)S(1)} all-to-all(bf16[16,16,256]{2,1,0:T(8,128)(2,1)S(1)} %shard_map.73), channel_id=1, replica_groups=mesh['blk'=16,'pair'=8] {'blk'}, dimensions={0} | all-to-all | bytes 262144 | tf_op jit(solution)/shard_map/all_to_all | solution.py:143
  18.4 0.8 shard_map.74
  19.3 6.6 %all-to-all-start.1 = ((bf16[64,16,256]{2,1,0:T(8,128)(2,1)}), bf16[64,16,256]{2,1,0:T(8,128)(2,1)S(1)}, u32[]{:S(2)}, u32[]{:S(2)}) async-start(bf16[64,16,256]{2,1,0:T(8,128)(2,1)} %shard_map.74), calls=%async_computation.1 | async-start | bytes 1048576 | tf_op jit(solution)/shard_map/all_to_all | solution.py:149
  26.0 0.7 broadcast_compare_fusion
  26.7 0.7 broadcast_add_fusion
  27.4 10.7 %all-to-all-done.1.mine_ref = bf16[64,16,256]{2,1,0:T(8,128)(2,1)S(1)} async-done(((bf16[64,16,256]{2,1,0:T(8,128)(2,1)}), bf16[64,16,256]{2,1,0:T(8,128)(2,1)S(1)}, u32[]{:S(2)}, u32[]{:S(2)}) %all-to-all-start.1) | async-done | bytes 524320 | tf_op jit(solution)/shard_map/all_to_all | solution.py:149
  38.3 0.2 select_reduce_fusion.1
  38.7 1.4 collective-permute-done.other_ref
  40.1 4.0 %copy-done.1 = bf16[80,4,128,128]{3,2,1,0:T(8,128)(2,1)S(1)} copy-done((bf16[80,4,128,128]{3,2,1,0:T(8,128)(2,1)S(1)}, bf16[80,4,128,128]{3,2,1,0:T(8,128)(2,1)}, u32[]{:S(2)}) %copy-start.1) | copy-done | bytes 10485784
  44.1 7.8 %shard_map.75 = s32[16,8,6,8,128]{4,3,2,1,0:T(8,128)S(1)} custom-call(s32[80]{0:T(128)S(1)} %sub.19.irrep_ref, s32[1]{0:T(128)} %bitcast.core_ref, bf16[64,16,256]{2,1,0:T(8,128)(2,1)S(1)} %all-to-all-done.1.mine_ref, bf16[64,16,256]{2,1,0:T(8,128)(2,1)S(1)} %collective-permute-done.other_ref, bf16[80,4,128,128]{3,2,1,0:T(8,128)(2,1)S(1)} %copy-done.1), custom_call_target="tpu_custom_call" | custom-call | flops 1342177280 | bytes 14680064 | tf_op jit(solution)/shard_map/pallas_call | solution.py:174
  51.9 1.6 %copy-done = s32[16,8,6,8,128]{4,3,2,1,0:T(8,128)} copy-done((s32[16,8,6,8,128]{4,3,2,1,0:T(8,128)}, s32[16,8,6,8,128]{4,3,2,1,0:T(8,128)S(1)}, u32[]{:S(2)}) %copy-start) | copy-done | bytes 3145752
  53.6 4.8 %all-to-all-start.2 = ((s32[128,48,128]{2,1,0:T(8,128)}), s32[128,48,128]{2,1,0:T(8,128)S(1)}, u32[]{:S(2)}, u32[]{:S(2)}) async-start(s32[128,48,128]{2,1,0:T(8,128)} %bitcast.6), calls=%async_computation.2 | async-start | bytes 6291456 | tf_op jit(solution)/shard_map/all_to_all | solution.py:191
  58.5 0.8 iota_add_fusion
  59.2 0.2 convert_reduce_fusion.to_ref
  59.4 0.2 convert_reduce_fusion.2
  59.6 40.4 %all-to-all-done.2 = s32[128,48,128]{2,1,0:T(8,128)S(1)} async-done(((s32[128,48,128]{2,1,0:T(8,128)}), s32[128,48,128]{2,1,0:T(8,128)S(1)}, u32[]{:S(2)}, u32[]{:S(2)}) %all-to-all-start.2) | async-done | bytes 3145760 | tf_op jit(solution)/shard_map/all_to_all | solution.py:191
  100.0 1.2 shard_map.76
  101.2 1.0 copy-done.2
  102.2 4.3 %all-to-all-start.3 = ((s32[256,8,128]{2,1,0:T(8,128)}), s32[256,8,128]{2,1,0:T(8,128)}, u32[]{:S(2)}, u32[]{:S(2)}) async-start(s32[256,8,128]{2,1,0:T(8,128)} %copy-done.2), calls=%async_computation.3 | async-start | bytes 2097152 | tf_op jit(solution)/shard_map/all_to_all | solution.py:197
  106.5 0.8 dynamic_slice.11.sign_ref
  107.3 0.2 convert_reduce_fusion.1.face_ref
  107.4 0.7 select_reduce_fusion
  108.1 15.8 %all-to-all-done.3.there_ref = s32[256,8,128]{2,1,0:T(8,128)} async-done(((s32[256,8,128]{2,1,0:T(8,128)}), s32[256,8,128]{2,1,0:T(8,128)}, u32[]{:S(2)}, u32[]{:S(2)}) %all-to-all-start.3) | async-done | bytes 1048608 | tf_op jit(solution)/shard_map/all_to_all | solution.py:197
  123.9 4.7 %shard_map.77 = (bf16[8,32768]{1,0:T(8,128)(2,1)S(1)}, bf16[8,32768]{1,0:T(8,128)(2,1)}) custom-call(s32[256]{0:T(256)S(1)} %multiply_add_fusion.2.from_ref.own_ref, s32[256]{0:T(256)S(1)} %get-tuple-element.11.own_scale_ref, s32[256]{0:T(256)S(1)} %convert_reduce_fusion.1.face_ref, s32[256]{0:T(256)S(1)} %multiply_add_fusion.face_scale_ref, ...), custom_call_target="tpu_custom_call" | custom-call | bytes 5242880 | tf_op jit(solution)/shard_map/pallas_call | solution.py:199
  128.6 0.8 copy-done.4
  129.4 0.3 collective-permute-start.1
  129.7 12.9 %collective-permute-done.1 = bf16[8,32768]{1,0:T(8,128)(2,1)S(1)} collective-permute-done((bf16[8,32768]{1,0:T(8,128)(2,1)}, bf16[8,32768]{1,0:T(8,128)(2,1)S(1)}, u32[]{:S(2)}, u32[]{:S(2)}) %collective-permute-start.1) | collective-permute-done | bytes 524320 | tf_op jit(solution)/shard_map/ppermute | solution.py:203
  142.6 1.1 broadcast_select_fusion.1
  143.7 1.0 pad_maximum_fusion
  (17 shorter events, 0.5 us)
Async XLA Ops:
  0.7 1.2 copy-start.3
  19.3 18.9 %all-to-all-start.1 = ((bf16[64,16,256]{2,1,0:T(8,128)(2,1)}), bf16[64,16,256]{2,1,0:T(8,128)(2,1)S(1)}, u32[]{:S(2)}, u32[]{:S(2)}) async-start(bf16[64,16,256]{2,1,0:T(8,128)(2,1)} %shard_map.74), calls=%async_computation.1 | async-start | bytes 1048576 | tf_op jit(solution)/shard_map/all_to_all | solution.py:149
  38.2 1.9 %collective-permute-start = (bf16[64,16,256]{2,1,0:T(8,128)(2,1)S(1)}, bf16[64,16,256]{2,1,0:T(8,128)(2,1)S(1)}, u32[]{:S(2)}, u32[]{:S(2)}) collective-permute-start(bf16[64,16,256]{2,1,0:T(8,128)(2,1)S(1)} %all-to-all-done.1.mine_ref), channel_id=1, source_target_pairs={{0,1},{1,0},{2,3},{3,2},{4,5},{5,4},{6,7},{7,6},{8,9},{9,8},{10,11... | collective-permute-start | bytes 1572872 | tf_op jit(solution)/shard_map/ppermute | solution.py:150
  40.1 4.0 %copy-start.1 = (bf16[80,4,128,128]{3,2,1,0:T(8,128)(2,1)S(1)}, bf16[80,4,128,128]{3,2,1,0:T(8,128)(2,1)}, u32[]{:S(2)}) copy-start(bf16[80,4,128,128]{3,2,1,0:T(8,128)(2,1)} %tile_ref.1) | copy-start | bytes 31457284
  51.9 1.6 %copy-start = (s32[16,8,6,8,128]{4,3,2,1,0:T(8,128)}, s32[16,8,6,8,128]{4,3,2,1,0:T(8,128)S(1)}, u32[]{:S(2)}) copy-start(s32[16,8,6,8,128]{4,3,2,1,0:T(8,128)S(1)} %shard_map.75) | copy-start | bytes 9437188
  53.6 4.8 %copy-start.5 = (s32[4096]{0:T(1024)S(1)}, s32[4096]{0:T(1024)}, u32[]{:S(2)}) copy-start(s32[4096]{0:T(1024)} %param.11) | copy-start | bytes 49156
  53.6 46.4 %all-to-all-start.2 = ((s32[128,48,128]{2,1,0:T(8,128)}), s32[128,48,128]{2,1,0:T(8,128)S(1)}, u32[]{:S(2)}, u32[]{:S(2)}) async-start(s32[128,48,128]{2,1,0:T(8,128)} %bitcast.6), calls=%async_computation.2 | async-start | bytes 6291456 | tf_op jit(solution)/shard_map/all_to_all | solution.py:191
  101.2 1.0 copy-start.2
  102.2 21.8 %all-to-all-start.3 = ((s32[256,8,128]{2,1,0:T(8,128)}), s32[256,8,128]{2,1,0:T(8,128)}, u32[]{:S(2)}, u32[]{:S(2)}) async-start(s32[256,8,128]{2,1,0:T(8,128)} %copy-done.2), calls=%async_computation.3 | async-start | bytes 2097152 | tf_op jit(solution)/shard_map/all_to_all | solution.py:197
  128.6 0.8 copy-start.4
  129.4 13.2 %collective-permute-start.1 = (bf16[8,32768]{1,0:T(8,128)(2,1)}, bf16[8,32768]{1,0:T(8,128)(2,1)S(1)}, u32[]{:S(2)}, u32[]{:S(2)}) collective-permute-start(bf16[8,32768]{1,0:T(8,128)(2,1)} %get-tuple-element.8), channel_id=1, source_target_pairs={{0,4},{1,5},{2,6},{3,7},{4,0},{5,1},{6,2},{7,3},{8,12},{9,13},{10,... | collective-permute-start | bytes 1572872 | tf_op jit(solution)/shard_map/ppermute | solution.py:203

commit v2 on v1

v2 whole, which is shorter than its diff:
```python
import jax
import jax.numpy as jnp
from jax import lax
from jax.experimental import pallas as pl
from jax.experimental.pallas import tpu as pltpu
from jax.sharding import PartitionSpec as P

BOTH = ("blk", "pair")
TOP = 32760.0
STEPS = 64.0
LN2 = 0.6931471805599453
MIB = 1 << 20
VMEM = pl.BlockSpec(memory_space=pltpu.VMEM)
HBM = pl.BlockSpec(memory_space=pltpu.HBM)
SMEM = pl.BlockSpec(memory_space=pltpu.SMEM)


def call(body, ins, outs, shapes, scratch, vmem, flops, moved):
    return pl.pallas_call(
        body,
        in_specs=ins,
        out_specs=outs,
        out_shape=shapes,
        scratch_shapes=scratch,
        compiler_params=pltpu.CompilerParams(vmem_limit_bytes=vmem),
        cost_estimate=pl.CostEstimate(flops=flops, bytes_accessed=moved, transcendentals=0),
    )


def extract_body(blocks_ref, amp_ref, out_ref, sems):
    blk = lax.axis_index("blk")

    def move(n):
        start = pl.multiple_of((blocks_ref[n] & 255) * 128, 128)
        return pltpu.make_async_copy(
            amp_ref.at[:, pl.ds(start, 128)],
            out_ref.at[n // 2, :, pl.ds((n % 2) * 128, 128)],
            sems.at[n],
        )

    for n in range(32):
        held = (blocks_ref[n] >> 8) == blk

        @pl.when(held)
        def _():
            move(n).start()

        @pl.when(jnp.logical_not(held))
        def _():
            out_ref[n // 2, :, (n % 2) * 128 : (n % 2) * 128 + 128] = jnp.zeros((16, 128), jnp.bfloat16)

    for n in range(32):

        @pl.when((blocks_ref[n] >> 8) == blk)
        def _():
            move(n).wait()


def merge_body(in_ref, out_ref):
    total = in_ref[0].astype(jnp.float32)
    for s in range(1, 16):
        total += in_ref[s].astype(jnp.float32)
    part = total.astype(jnp.bfloat16)
    for s in range(64):
        out_ref[s] = part


def row_tiles(p):
    return (2 * p, 2 * p + 8) if p < 4 else (2 * (p - 4) + 9, 2 * (p - 4) + 1)


def product_body(irrep_ref, mine_ref, other_ref, tiles_ref, out_ref, level_ref, held, slab, prod, code, in_sems, out_sems):
    def fetch(t):
        span = pl.ds(t * 5, 5)
        return pltpu.make_async_copy(tiles_ref.at[span], held.at[span], in_sems.at[t])

    def store(t):
        return pltpu.make_async_copy(code.at[t], out_ref.at[t], out_sems.at[t])

    for t in range(16):
        fetch(t).start()
    core = lax.axis_index("pair") % 2
    for source, shift in ((mine_ref, core), (other_ref, 1 - core)):
        for c in range(16):
            for x in range(4):
                rows = pl.ds(pl.multiple_of((2 * x + shift) * 16, 16), 16)
                slab[c // 2, rows, (c % 2) * 256 : (c % 2) * 256 + 256] = source[c * 4 + x]

    def multiply(t, top):
        fetch(t).wait()
        for k in range(5):
            slot = t * 5 + k
            irrep = irrep_ref[slot]
            left = slab[jnp.maximum(irrep, 0)]
            right = held[slot].reshape(512, 128)
            value = jnp.dot(left, right, preferred_element_type=jnp.float32)
            prod[slot] = value
            high = jnp.max(jnp.abs(value).reshape(16, 8, 128), axis=0)
            top = jnp.maximum(top, jnp.where(irrep >= 0, high, 0.0))
        return top

    top = lax.fori_loop(0, 16, multiply, jnp.zeros((8, 128), jnp.float32))
    top = jnp.max(jnp.max(top, axis=1, keepdims=True), axis=0, keepdims=True)
    level = jnp.ceil(jnp.log(jnp.maximum(top, 1e-30)) * (STEPS / LN2))
    level = jnp.broadcast_to(level, (8, 128))
    level_ref[...] = level.astype(jnp.int32)
    inverse = jnp.exp(level * (-LN2 / STEPS)) * TOP

    def quantise(t, carry):
        for k in range(5):
            for p in range(8):
                high, low = (
                    jnp.floor(prod[t * 5 + k, u * 8 : u * 8 + 8, :] * inverse + 0.5).astype(jnp.int32) for u in row_tiles(p)
                )
                code[t, p, k] = (high << 16) | (low & 0xFFFF)
        store(t).start()
        return carry

    lax.fori_loop(0, 16, quantise, 0)
    for t in range(16):
        store(t).wait()


def select_body(from_ref, in_ref, level_ref, out_ref):
    def one(t, carry):
        for i in range(16):
            out_ref[t, i] = in_ref[from_ref[t * 16 + i]]
        out_ref[t, 16] = level_ref[...]
        return carry

    lax.fori_loop(0, 16, one, 0)


def combine(index_ref, here_ref, there_ref, table, out_ref, own_part, face_part):
    def one(step, carry):
        for i in range(8):
            j = step * 8 + i
            own = own_part(here_ref[index_ref[0, j]]).astype(jnp.float32)
            face = face_part(there_ref[index_ref[1, j]]).astype(jnp.float32)
            face_scale = table[index_ref[3, j]] * index_ref[4, j].astype(jnp.float32)
            value = own * table[index_ref[2, j]] + face * face_scale
            out_ref[:, pl.ds(pl.multiple_of(j * 128, 128), 128)] = value.astype(jnp.bfloat16)
        return carry

    lax.fori_loop(0, 32, one, 0)


def high_part(word):
    return word >> 16


def low_part(word):
    return (word << 16) >> 16


def send_body(index_ref, here_ref, there_ref, out_ref, table_ref):
    for s in range(16):
        scale = jnp.exp(there_ref[s * 17 + 16].astype(jnp.float32) * (LN2 / STEPS)) * (1.0 / TOP)
        for r in range(8):
            table_ref[s * 8 + r] = jnp.broadcast_to(scale[r : r + 1, :], (8, 128))
    combine(index_ref, here_ref, there_ref, table_ref, out_ref, low_part, high_part)


def keep_body(index_ref, here_ref, there_ref, table_ref, out_ref):
    combine(index_ref, here_ref, there_ref, table_ref, out_ref, high_part, low_part)


def swap(value, mask):
    return lax.ppermute(value, "pair", [(i, i ^ mask) for i in range(8)])


def local(amplitudes, integrals, block_irrep, slab_blocks, owner, partner, sign):
    blk = lax.axis_index("blk")
    pair = lax.axis_index("pair")
    me = blk * 8 + pair
    int32 = jnp.int32
    dma = pltpu.SemaphoreType.DMA

    parts = call(
        extract_body, [SMEM, HBM], VMEM, jax.ShapeDtypeStruct((16, 16, 256), jnp.bfloat16), [dma((32,))], 60 * MIB, 0, 1 << 18
    )(slab_blocks, amplitudes)
    parts = lax.all_to_all(parts, "blk", split_axis=0, concat_axis=0, tiled=True)
    copies = call(
        merge_body, [VMEM], VMEM, jax.ShapeDtypeStruct((64, 16, 256), jnp.bfloat16), [], 4 * MIB, 0, 1 << 20
    )(parts)
    groups = [[c + 2 * i for i in range(64)] for c in range(2)]
    mine = lax.all_to_all(copies, BOTH, split_axis=0, concat_axis=0, tiled=True, axis_index_groups=groups)
    other = swap(mine, 1)

    ids = jnp.arange(256, dtype=int32)
    stored = (owner == me).reshape(16, 256)
    earlier = (ids[:, None] < ids[None, :]).astype(jnp.bfloat16)
    slot_rank = jnp.dot(stored.astype(jnp.bfloat16), earlier, preferred_element_type=jnp.float32).astype(int32)
    labels = block_irrep.reshape(16, 256) + 1
    chosen = stored[:, None, :] & (slot_rank[:, None, :] == jnp.arange(5, dtype=int32)[None, :, None])
    slot_irrep = (jnp.sum(jnp.where(chosen, labels[:, None, :], 0), axis=2) - 1).reshape(80)

    my_owner = lax.dynamic_slice_in_dim(owner, blk * 256, 256)
    my_partner = lax.dynamic_slice_in_dim(partner, blk * 256, 256)
    my_sign = lax.dynamic_slice_in_dim(sign, blk * 256, 256)
    before = ids[None, :] < ids[:, None]
    rank = jnp.sum((my_owner[None, :] == my_owner[:, None]) & before, axis=1).astype(int32)
    arrive = my_owner * 5 + rank
    leave_key = (my_partner // 256) * 256 + ids
    leave = jnp.sum(leave_key[None, :] < leave_key[:, None], axis=1).astype(int32)
    leaving = jnp.sum(jnp.where(leave[None, :] == ids[:, None], arrive[None, :], 0), axis=1).astype(int32)
    back = jnp.sum(my_partner[None, :] < my_partner[:, None], axis=1).astype(int32)
    all_ids = jnp.arange(4096, dtype=int32)
    face_owner = jnp.sum(jnp.where(my_partner[:, None] == all_ids[None, :], owner[None, :], 0), axis=1)
    index = jnp.stack([arrive, back + back // 16, my_owner ^ pair, face_owner ^ pair, my_sign])

    coded, level = call(
        product_body, [SMEM, VMEM, VMEM, HBM], [HBM, VMEM],
        [jax.ShapeDtypeStruct((16, 8, 5, 8, 128), int32), jax.ShapeDtypeStruct((8, 128), int32)],
        [
            pltpu.VMEM((80, 4, 128, 128), jnp.bfloat16),
            pltpu.VMEM((8, 128, 512), jnp.bfloat16),
            pltpu.VMEM((80, 128, 128), jnp.float32),
            pltpu.VMEM((16, 8, 5, 8, 128), int32),
            dma((16,)),
            dma((16,)),
        ],
        52 * MIB, 1_342_177_280, 14 << 20,
    )(slot_irrep, mine, other, integrals)
    arrived = lax.all_to_all(coded.reshape(128, 40, 128), BOTH, split_axis=0, concat_axis=0, tiled=True)
    arrived = arrived.reshape(640, 8, 128)
    levels = level[:1]
    for mask in (1, 2, 4):
        levels = jnp.concatenate([levels, swap(levels, mask)], axis=0)
    outgoing = call(
        select_body, [SMEM, VMEM, VMEM], VMEM, jax.ShapeDtypeStruct((16, 17, 8, 128), int32), [], 16 * MIB, 0, 3 << 20
    )(leaving, arrived, levels)
    incoming = lax.all_to_all(outgoing, "blk", split_axis=0, concat_axis=0, tiled=True).reshape(272, 8, 128)
    half = jax.ShapeDtypeStruct((8, 32768), jnp.bfloat16)
    send, table = call(
        send_body, [SMEM, VMEM, VMEM], [VMEM, VMEM], [half, jax.ShapeDtypeStruct((128, 8, 128), jnp.float32)],
        [], 16 * MIB, 0, 4 << 20,
    )(index, arrived, incoming)
    got = swap(send, 4)
    keep = call(
        keep_body, [SMEM, VMEM, VMEM, VMEM], VMEM, half, [], 16 * MIB, 0, 4 << 20
    )(index, arrived, incoming, table)
    kept = (lax.broadcasted_iota(int32, (2, 1, 1), 0) == pair // 4)
    return jnp.where(kept, keep[None], got[None]).reshape(16, 32768)


def solution(mesh):
    placed = (P("pair", "blk"), P(BOTH, None, None, None), P(), P(), P(), P(), P())
    return jax.shard_map(local, mesh=mesh, in_specs=placed, out_specs=P("pair", "blk"), check_vma=False)
```

time: 146 us -> 135 us (0.925)
  waiting for transfers between devices: 81.2 us -> 64.2 us
  starting transfers between devices: 16.1 us -> 23.6 us
  local copies, waits for them, and re-layouts: 9.58 us -> 2.2 us
  Pallas kernels: 15.1 us -> 21.4 us
    all_to_all x1, waiting for transfers between devices: 40.4 us -> 1.56 us  [local(): lax.all_to_all(coded.reshape(128, 40, 128), BOTH, split_axis=0, concat_ax...]
    ppermute x2 -> x5, waiting for transfers between devices: 14.3 us -> 35.9 us  [swap(): return lax.ppermute(value, 'pair', [(i, i ^ mask) for i in range(8)])]
    unnamed x12 -> x4, local copies, waits for them, and re-layouts: 8.62 us -> 1.05 us
    pallas_call x5 -> x6, Pallas kernels: 15.1 us -> 21.4 us  [the longest x1 8.98 us: local(): call(product_body, [SMEM, VMEM, VMEM, HBM], [HBM, VMEM], [jax.ShapeDtypeS...]
    ppermute x2 -> x5, starting transfers between devices: 0.33 us -> 6.4 us  [swap(): return lax.ppermute(value, 'pair', [(i, i ^ mask) for i in range(8)])]
    all_to_all x1, starting transfers between devices: 4.34 us -> 5.92 us  [local(): lax.all_to_all(outgoing, 'blk', split_axis=0, concat_axis=0, tiled=True)]
  transfers between devices with their start and end apart: 5 -> 8, of which waited for: 5 -> 8; matrix products, arithmetic and copies ran while one was open for 3% -> 4% of each run, Pallas kernels for 0% -> 3%
where the time goes in v2:
time: 135 us; the launch traced here: 134 us
  waiting for transfers between devices  64.2 us (48%)
  starting transfers between devices  23.6 us (17%)
  Pallas kernels  21.4 us (16%)
  blocking collectives  16 us (12%)
  other arithmetic  6.06 us (4%)
  local copies, waits for them, and re-layouts  2.2 us (2%)
    ppermute x5, waiting for transfers between devices, swap(): return lax.ppermute(value, 'pair', [(i, i ^ mask) for i in range(8)])  35.9 us
    all_to_all x1, waiting for transfers between devices, local(): lax.all_to_all(outgoing, 'blk', split_axis=0, concat_axis=0, tiled=True)  16 us
    all_to_all x1, blocking collectives, local(): lax.all_to_all(parts, 'blk', split_axis=0, concat_axis=0, tiled=True)  16 us
    all_to_all x1, waiting for transfers between devices, local(): lax.all_to_all(copies, BOTH, split_axis=0, concat_axis=0, tiled=True, axi...  10.7 us
    pallas_call x1, Pallas kernels, local(): call(product_body, [SMEM, VMEM, VMEM, HBM], [HBM, VMEM], [jax.ShapeDtypeS...  8.98 us
    all_to_all x1, starting transfers between devices, local(): lax.all_to_all(copies, BOTH, split_axis=0, concat_axis=0, tiled=True, axi...  6.64 us
    ppermute x5, starting transfers between devices, swap(): return lax.ppermute(value, 'pair', [(i, i ^ mask) for i in range(8)])  6.4 us
    all_to_all x1, starting transfers between devices, local(): lax.all_to_all(outgoing, 'blk', split_axis=0, concat_axis=0, tiled=True)  5.92 us
  transfers between devices with their start and end apart: 8, of which 8 were waited for; matrix products, arithmetic and copies ran while one was open for 4% of the time, Pallas kernels for 3%

profile of v2, /device:TPU:0, one launch (start us, length us, event | category | flops | bytes accessed | tf_op | source)
XLA Modules:
  0.0 133.8 jit_solution(3897970189454942063)
XLA Ops:
  0.0 2.4 %shard_map.73 = bf16[16,16,256]{2,1,0:T(8,128)(2,1)} custom-call(s32[32]{0:T(128)} %blocks_ref.1, bf16[16,32768]{1,0:T(8,128)(2,1)} %amp_ref.1), custom_call_target="tpu_custom_call" | custom-call | bytes 262144 | tf_op jit(solution)/shard_map/pallas_call | solution.py:179
  2.4 16.0 %all_to_all.20.in_ref = bf16[16,16,256]{2,1,0:T(8,128)(2,1)S(1)} all-to-all(bf16[16,16,256]{2,1,0:T(8,128)(2,1)} %shard_map.73), channel_id=1, replica_groups=mesh['blk'=16,'pair'=8] {'blk'}, dimensions={0} | all-to-all | bytes 262144 | tf_op jit(solution)/shard_map/all_to_all | solution.py:182
  18.4 0.8 shard_map.74
  19.2 6.6 %all-to-all-start.1 = ((bf16[64,16,256]{2,1,0:T(8,128)(2,1)}), bf16[64,16,256]{2,1,0:T(8,128)(2,1)S(1)}, u32[]{:S(2)}, u32[]{:S(2)}) async-start(bf16[64,16,256]{2,1,0:T(8,128)(2,1)} %shard_map.74), calls=%async_computation.1 | async-start | bytes 1048576 | tf_op jit(solution)/shard_map/all_to_all | solution.py:187
  25.9 0.7 broadcast_compare_fusion
  26.6 0.7 broadcast_add_fusion
  27.4 10.7 %all-to-all-done.1.mine_ref = bf16[64,16,256]{2,1,0:T(8,128)(2,1)S(1)} async-done(((bf16[64,16,256]{2,1,0:T(8,128)(2,1)}), bf16[64,16,256]{2,1,0:T(8,128)(2,1)S(1)}, u32[]{:S(2)}, u32[]{:S(2)}) %all-to-all-start.1) | async-done | bytes 524320 | tf_op jit(solution)/shard_map/all_to_all | solution.py:187
  38.3 0.2 select_reduce_fusion.2
  38.6 1.4 %collective-permute-done.other_ref = bf16[64,16,256]{2,1,0:T(8,128)(2,1)S(1)} collective-permute-done((bf16[64,16,256]{2,1,0:T(8,128)(2,1)S(1)}, bf16[64,16,256]{2,1,0:T(8,128)(2,1)S(1)}, u32[]{:S(2)}, u32[]{:S(2)}) %collective-permute-start) | collective-permute-done | bytes 524320 | tf_op jit(solution)/shard_map/ppermute | solution.py:169
  40.0 9.0 %shard_map.75 = (s32[16,8,5,8,128]{4,3,2,1,0:T(8,128)}, s32[8,128]{1,0:T(8,128)S(1)}) custom-call(s32[80]{0:T(128)S(1)} %sub.23.irrep_ref, bf16[64,16,256]{2,1,0:T(8,128)(2,1)S(1)} %all-to-all-done.1.mine_ref, bf16[64,16,256]{2,1,0:T(8,128)(2,1)S(1)} %collective-permute-done.other_ref, bf16[80,4,128,128]{3,2,1,0:T(8,128)(2,1)} %tiles_ref.1), custom_call_target="tpu_custom_call" | custom-call | flops 1342177280 | bytes 14680064 | tf_op jit(solution)/shard_map/pallas_call | solution.py:212
  49.0 4.7 %all-to-all-start.2 = ((s32[128,40,128]{2,1,0:T(8,128)}), s32[128,40,128]{2,1,0:T(8,128)S(1)}, u32[]{:S(2)}, u32[]{:S(2)}) async-start(s32[128,40,128]{2,1,0:T(8,128)} %bitcast.16), calls=%async_computation.2 | async-start | bytes 5242880 | tf_op jit(solution)/shard_map/all_to_all | solution.py:225
  53.7 0.8 iota_add_fusion
  54.5 0.7 select_reduce_fusion
  55.3 0.2 convert_reduce_fusion.2
  55.6 1.1 collective-permute-done.1
  56.7 0.8 collective-permute-start.2
  57.5 0.2 convert_reduce_fusion
  57.7 25.3 %collective-permute-done.2 = s32[2,128]{1,0:T(2,128)S(1)} collective-permute-done((s32[2,128]{1,0:T(2,128)S(1)}, s32[2,128]{1,0:T(2,128)S(1)}, u32[]{:S(2)}, u32[]{:S(2)}) %collective-permute-start.2) | collective-permute-done | bytes 1056 | tf_op jit(solution)/shard_map/ppermute | solution.py:169
  83.0 2.8 %collective-permute-start.3 = (s32[4,128]{1,0:T(4,128)S(1)}, s32[4,128]{1,0:T(4,128)S(1)}, u32[]{:S(2)}, u32[]{:S(2)}) collective-permute-start(s32[4,128]{1,0:T(4,128)S(1)} %pad_add_fusion.1), channel_id=1, source_target_pairs={{0,4},{1,5},{2,6},{3,7},{4,0},{5,1},{6,2},{7,3},{8,12},{9,13},{10,... | collective-permute-start | bytes 6152 | tf_op jit(solution)/shard_map/ppermute | solution.py:169
  85.9 2.3 %collective-permute-done.3 = s32[4,128]{1,0:T(4,128)S(1)} collective-permute-done((s32[4,128]{1,0:T(4,128)S(1)}, s32[4,128]{1,0:T(4,128)S(1)}, u32[]{:S(2)}, u32[]{:S(2)}) %collective-permute-start.3) | collective-permute-done | bytes 2080 | tf_op jit(solution)/shard_map/ppermute | solution.py:169
  88.2 1.6 %all-to-all-done.2 = s32[128,40,128]{2,1,0:T(8,128)S(1)} async-done(((s32[128,40,128]{2,1,0:T(8,128)}), s32[128,40,128]{2,1,0:T(8,128)S(1)}, u32[]{:S(2)}, u32[]{:S(2)}) %all-to-all-start.2) | async-done | bytes 2621472 | tf_op jit(solution)/shard_map/all_to_all | solution.py:225
  89.7 0.9 shard_map.76
  90.6 1.0 copy-done
  91.7 5.9 %all-to-all-start.3 = ((s32[16,17,8,128]{3,2,1,0:T(8,128)}), s32[16,17,8,128]{3,2,1,0:T(8,128)}, u32[]{:S(2)}, u32[]{:S(2)}) async-start(s32[16,17,8,128]{3,2,1,0:T(8,128)} %copy-done), calls=%async_computation.3 | async-start | bytes 2228224 | tf_op jit(solution)/shard_map/all_to_all | solution.py:233
  97.6 0.8 dynamic_slice.11
  98.4 0.2 convert_reduce_fusion.1
  98.6 16.0 %all-to-all-done.3 = s32[16,17,8,128]{3,2,1,0:T(8,128)} async-done(((s32[16,17,8,128]{3,2,1,0:T(8,128)}), s32[16,17,8,128]{3,2,1,0:T(8,128)}, u32[]{:S(2)}, u32[]{:S(2)}) %all-to-all-start.3) | async-done | bytes 1114144 | tf_op jit(solution)/shard_map/all_to_all | solution.py:233
  114.6 4.6 %shard_map.77 = (bf16[8,32768]{1,0:T(8,128)(2,1)}, f32[128,8,128]{2,1,0:T(8,128)S(1)}) custom-call(s32[5,256]{1,0:T(8,128)S(1)} %stack.17.index_ref, s32[640,8,128]{2,1,0:T(8,128)S(1)} %bitcast.14, s32[272,8,128]{2,1,0:T(8,128)} %bitcast.7.there_ref), custom_call_target="tpu_custom_call" | custom-call | bytes 4194304 | tf_op jit(solution)/shard_map/pallas_call | solution.py:235
  119.2 2.7 %collective-permute-start.4 = (bf16[8,32768]{1,0:T(8,128)(2,1)}, bf16[8,32768]{1,0:T(8,128)(2,1)}, u32[]{:S(2)}, u32[]{:S(2)}) collective-permute-start(bf16[8,32768]{1,0:T(8,128)(2,1)} %get-tuple-element.12), channel_id=1, source_target_pairs={{0,4},{1,5},{2,6},{3,7},{4,0},{5,1},{6,2},{7,3},{8,12},{9,13},{10,... | collective-permute-start | bytes 1572872 | tf_op jit(solution)/shard_map/ppermute | solution.py:169
  122.1 3.7 %shard_map.78 = bf16[8,32768]{1,0:T(8,128)(2,1)S(1)} custom-call(s32[5,256]{1,0:T(8,128)S(1)} %stack.17.index_ref, s32[640,8,128]{2,1,0:T(8,128)S(1)} %bitcast.15, s32[272,8,128]{2,1,0:T(8,128)} %bitcast.7.there_ref, f32[128,8,128]{2,1,0:T(8,128)S(1)} %get-tuple-element.11.table_ref), custom_call_target="tpu_custom_call" | custom-call | bytes 4194304 | tf_op jit(solution)/shard_map/pallas_call | solution.py:240
  125.8 5.8 %collective-permute-done.4 = bf16[8,32768]{1,0:T(8,128)(2,1)} collective-permute-done((bf16[8,32768]{1,0:T(8,128)(2,1)}, bf16[8,32768]{1,0:T(8,128)(2,1)}, u32[]{:S(2)}, u32[]{:S(2)}) %collective-permute-start.4) | collective-permute-done | bytes 524320 | tf_op jit(solution)/shard_map/ppermute | solution.py:169
  131.6 2.2 %bitcast_select_fusion = bf16[16,32768]{1,0:T(8,128)(2,1)} fusion(pred[16]{0:T(512)(128)(4,1)S(1)} %broadcast_in_dim.90, bf16[8,32768]{1,0:T(8,128)(2,1)} %collective-permute-done.4, bf16[8,32768]{1,0:T(8,128)(2,1)S(1)} %shard_map.78), kind=kLoop, calls=%fused_computation.3 | loop fusion | flops 524288 | bytes 2097168 | tf_op jit(solution)/shard_map/jit(_where)/select_n | solution.py:244
  (23 shorter events, 0.9 us)
Async XLA Ops:
  19.2 18.9 %all-to-all-start.1 = ((bf16[64,16,256]{2,1,0:T(8,128)(2,1)}), bf16[64,16,256]{2,1,0:T(8,128)(2,1)S(1)}, u32[]{:S(2)}, u32[]{:S(2)}) async-start(bf16[64,16,256]{2,1,0:T(8,128)(2,1)} %shard_map.74), calls=%async_computation.1 | async-start | bytes 1048576 | tf_op jit(solution)/shard_map/all_to_all | solution.py:187
  38.1 1.9 %collective-permute-start = (bf16[64,16,256]{2,1,0:T(8,128)(2,1)S(1)}, bf16[64,16,256]{2,1,0:T(8,128)(2,1)S(1)}, u32[]{:S(2)}, u32[]{:S(2)}) collective-permute-start(bf16[64,16,256]{2,1,0:T(8,128)(2,1)S(1)} %all-to-all-done.1.mine_ref), channel_id=1, source_target_pairs={{0,1},{1,0},{2,3},{3,2},{4,5},{5,4},{6,7},{7,6},{8,9},{9,8},{10,11... | collective-permute-start | bytes 1572872 | tf_op jit(solution)/shard_map/ppermute | solution.py:169
  49.0 5.5 %copy-start.1 = (s32[4096]{0:T(1024)S(1)}, s32[4096]{0:T(1024)}, u32[]{:S(2)}) copy-start(s32[4096]{0:T(1024)} %param.11) | copy-start | bytes 49156
  49.0 40.7 %all-to-all-start.2 = ((s32[128,40,128]{2,1,0:T(8,128)}), s32[128,40,128]{2,1,0:T(8,128)S(1)}, u32[]{:S(2)}, u32[]{:S(2)}) async-start(s32[128,40,128]{2,1,0:T(8,128)} %bitcast.16), calls=%async_computation.2 | async-start | bytes 5242880 | tf_op jit(solution)/shard_map/all_to_all | solution.py:225
  55.4 1.2 collective-permute-start.1
  56.7 26.3 %collective-permute-start.2 = (s32[2,128]{1,0:T(2,128)S(1)}, s32[2,128]{1,0:T(2,128)S(1)}, u32[]{:S(2)}, u32[]{:S(2)}) collective-permute-start(s32[2,128]{1,0:T(2,128)S(1)} %pad_add_fusion.2), channel_id=1, source_target_pairs={{0,2},{1,3},{2,0},{3,1},{4,6},{5,7},{6,4},{7,5},{8,10},{9,11},{10,... | collective-permute-start | bytes 3080 | tf_op jit(solution)/shard_map/ppermute | solution.py:169
  83.0 5.2 %collective-permute-start.3 = (s32[4,128]{1,0:T(4,128)S(1)}, s32[4,128]{1,0:T(4,128)S(1)}, u32[]{:S(2)}, u32[]{:S(2)}) collective-permute-start(s32[4,128]{1,0:T(4,128)S(1)} %pad_add_fusion.1), channel_id=1, source_target_pairs={{0,4},{1,5},{2,6},{3,7},{4,0},{5,1},{6,2},{7,3},{8,12},{9,13},{10,... | collective-permute-start | bytes 6152 | tf_op jit(solution)/shard_map/ppermute | solution.py:169
  90.6 1.1 copy-start
  91.7 22.9 %all-to-all-start.3 = ((s32[16,17,8,128]{3,2,1,0:T(8,128)}), s32[16,17,8,128]{3,2,1,0:T(8,128)}, u32[]{:S(2)}, u32[]{:S(2)}) async-start(s32[16,17,8,128]{3,2,1,0:T(8,128)} %copy-done), calls=%async_computation.3 | async-start | bytes 2228224 | tf_op jit(solution)/shard_map/all_to_all | solution.py:233
  119.2 12.4 %collective-permute-start.4 = (bf16[8,32768]{1,0:T(8,128)(2,1)}, bf16[8,32768]{1,0:T(8,128)(2,1)}, u32[]{:S(2)}, u32[]{:S(2)}) collective-permute-start(bf16[8,32768]{1,0:T(8,128)(2,1)} %get-tuple-element.12), channel_id=1, source_target_pairs={{0,4},{1,5},{2,6},{3,7},{4,0},{5,1},{6,2},{7,3},{8,12},{9,13},{10,... | collective-permute-start | bytes 1572872 | tf_op jit(solution)/shard_map/ppermute | solution.py:169

commit v3 on v2

--- a/solution.py
+++ b/solution.py
@@ -10,6 +10,7 @@
 STEPS = 64.0
 LN2 = 0.6931471805599453
 MIB = 1 << 20
+GROUP = 4
 VMEM = pl.BlockSpec(memory_space=pltpu.VMEM)
 HBM = pl.BlockSpec(memory_space=pltpu.HBM)
 SMEM = pl.BlockSpec(memory_space=pltpu.SMEM)
@@ -86,20 +87,26 @@
                 rows = pl.ds(pl.multiple_of((2 * x + shift) * 16, 16), 16)
                 slab[c // 2, rows, (c % 2) * 256 : (c % 2) * 256 + 256] = source[c * 4 + x]
 
-    def multiply(t, top):
-        fetch(t).wait()
-        for k in range(5):
-            slot = t * 5 + k
-            irrep = irrep_ref[slot]
-            left = slab[jnp.maximum(irrep, 0)]
-            right = held[slot].reshape(512, 128)
-            value = jnp.dot(left, right, preferred_element_type=jnp.float32)
-            prod[slot] = value
-            high = jnp.max(jnp.abs(value).reshape(16, 8, 128), axis=0)
-            top = jnp.maximum(top, jnp.where(irrep >= 0, high, 0.0))
+    def multiply(step, top):
+        for t in range(GROUP):
+            fetch(step * GROUP + t).wait()
+        count = GROUP * 5
+        values = []
+        for k in range(count + 1):
+            if k < count:
+                slot = step * count + k
+                left = slab[jnp.maximum(irrep_ref[slot], 0)]
+                right = held[slot].reshape(512, 128)
+                values.append(jnp.dot(left, right, preferred_element_type=jnp.float32))
+            if k > 0:
+                slot = step * count + k - 1
+                value = values[k - 1]
+                prod[slot] = value
+                high = jnp.max(jnp.abs(value).reshape(16, 8, 128), axis=0)
+                top = jnp.maximum(top, jnp.where(irrep_ref[slot] >= 0, high, 0.0))
         return top
 
-    top = lax.fori_loop(0, 16, multiply, jnp.zeros((8, 128), jnp.float32))
+    top = lax.fori_loop(0, 16 // GROUP, multiply, jnp.zeros((8, 128), jnp.float32))
     top = jnp.max(jnp.max(top, axis=1, keepdims=True), axis=0, keepdims=True)
     level = jnp.ceil(jnp.log(jnp.maximum(top, 1e-30)) * (STEPS / LN2))
     level = jnp.broadcast_to(level, (8, 128))
@@ -108,11 +115,15 @@
 
     def quantise(t, carry):
         for k in range(5):
+            value = prod[t * 5 + k]
+            words = []
             for p in range(8):
                 high, low = (
-                    jnp.floor(prod[t * 5 + k, u * 8 : u * 8 + 8, :] * inverse + 0.5).astype(jnp.int32) for u in row_tiles(p)
+                    jnp.floor(value[u * 8 : u * 8 + 8, :] * inverse + 0.5).astype(jnp.int32) for u in row_tiles(p)
                 )
-                code[t, p, k] = (high << 16) | (low & 0xFFFF)
+                words.append((high << 16) | (low & 0xFFFF))
+            for p in range(8):
+                code[t, p, k] = words[p]
         store(t).start()
         return carry
 
@@ -121,25 +132,48 @@
         store(t).wait()
 
 
-def select_body(from_ref, in_ref, level_ref, out_ref):
+def select_body(from_ref, in_ref, level_ref, out_ref, picked, sems):
+    def store(c):
+        span = pl.ds(c * 4, 4)
+        return pltpu.make_async_copy(picked.at[span], out_ref.at[span], sems.at[c])
+
     def one(t, carry):
         for i in range(16):
-            out_ref[t, i] = in_ref[from_ref[t * 16 + i]]
-        out_ref[t, 16] = level_ref[...]
+            picked[t, i] = in_ref[from_ref[t * 16 + i]]
+        picked[t, 16] = level_ref[...]
         return carry
 
+    for c in range(4):
+        lax.fori_loop(c * 4, c * 4 + 4, one, 0)
+        store(c).start()
+    for c in range(4):
+        store(c).wait()
+
+
+def gather_body(from_ref, in_ref, out_ref, picked, sems):
+    def one(step, carry):
+        for i in range(16):
+            picked[step * 16 + i] = in_ref[from_ref[step * 16 + i]]
+        return carry
+
     lax.fori_loop(0, 16, one, 0)
-
-
-def combine(index_ref, here_ref, there_ref, table, out_ref, own_part, face_part):
+    store = pltpu.make_async_copy(picked, out_ref, sems.at[0])
+    store.start()
+    store.wait()
+
+
+def combine(back_ref, own_ref, there_ref, scale_ref, out_ref, own_part, face_part):
     def one(step, carry):
+        rows = pl.multiple_of(step * 8, 8)
+        own_scale = scale_ref[pl.ds(rows, 8), :]
+        face_scale = scale_ref[pl.ds(256 + rows, 8), :]
+        values = []
         for i in range(8):
-            j = step * 8 + i
-            own = own_part(here_ref[index_ref[0, j]]).astype(jnp.float32)
-            face = face_part(there_ref[index_ref[1, j]]).astype(jnp.float32)
-            face_scale = table[index_ref[3, j]] * index_ref[4, j].astype(jnp.float32)
-            value = own * table[index_ref[2, j]] + face * face_scale
-            out_ref[:, pl.ds(pl.multiple_of(j * 128, 128), 128)] = value.astype(jnp.bfloat16)
+            own = own_part(own_ref[step * 8 + i]).astype(jnp.float32)
+            face = face_part(there_ref[back_ref[step * 8 + i]]).astype(jnp.float32)
+            values.append((own * own_scale[i : i + 1, :] + face * face_scale[i : i + 1, :]).astype(jnp.bfloat16))
+        for i in range(8):
+            out_ref[:, pl.ds(pl.multiple_of((step * 8 + i) * 128, 128), 128)] = values[i]
         return carry
 
     lax.fori_loop(0, 32, one, 0)
@@ -153,16 +187,70 @@
     return (word << 16) >> 16
 
 
-def send_body(index_ref, here_ref, there_ref, out_ref, table_ref):
-    for s in range(16):
-        scale = jnp.exp(there_ref[s * 17 + 16].astype(jnp.float32) * (LN2 / STEPS)) * (1.0 / TOP)
-        for r in range(8):
-            table_ref[s * 8 + r] = jnp.broadcast_to(scale[r : r + 1, :], (8, 128))
-    combine(index_ref, here_ref, there_ref, table_ref, out_ref, low_part, high_part)
-
-
-def keep_body(index_ref, here_ref, there_ref, table_ref, out_ref):
-    combine(index_ref, here_ref, there_ref, table_ref, out_ref, high_part, low_part)
+def send_body(back_ref, own_ref, there_ref, pick_ref, sign_ref, out_ref, scale_ref):
+    levels = jnp.concatenate([there_ref[s * 17 + 16] for s in range(16)], axis=0)
+    pick = pick_ref[...]
+    upper = jnp.dot(pick, (levels >> 5).astype(jnp.bfloat16), preferred_element_type=jnp.float32)
+    lower = jnp.dot(pick, (levels & 31).astype(jnp.bfloat16), preferred_element_type=jnp.float32)
+    scale_ref[...] = jnp.exp((upper * 32.0 + lower) * (LN2 / STEPS)) * (1.0 / TOP) * sign_ref[...]
+    combine(back_ref, own_ref, there_ref, scale_ref, out_ref, low_part, high_part)
+
+
+def keep_body(back_ref, own_ref, there_ref, scale_ref, out_ref):
+    combine(back_ref, own_ref, there_ref, scale_ref, out_ref, high_part, low_part)
+
+
+def finish_body(keep_ref, got_ref, out_ref):
+    first = lax.axis_index("pair") < 4
+    keep = keep_ref[...]
+    got = got_ref[...]
+    out_ref[0:8, :] = jnp.where(first, keep, got)
+    out_ref[8:16, :] = jnp.where(first, got, keep)
+
+
+def call_product(irreps, mine, other, tiles):
+    dma = pltpu.SemaphoreType.DMA
+    int32 = jnp.int32
+    return call(
+        product_body, [SMEM, VMEM, VMEM, HBM], [HBM, VMEM],
+        [pltpu.HBM((16, 8, 5, 8, 128), int32), jax.ShapeDtypeStruct((8, 128), int32)],
+        [
+            pltpu.VMEM((80, 4, 128, 128), jnp.bfloat16),
+            pltpu.VMEM((8, 128, 512), jnp.bfloat16),
+            pltpu.VMEM((80, 128, 128), jnp.float32),
+            pltpu.VMEM((16, 8, 5, 8, 128), int32),
+            dma((16,)),
+            dma((16,)),
+        ],
+        52 * MIB, 1_342_177_280, 14 << 20,
+    )(irreps, mine, other, tiles)
+
+
+HALF = jax.ShapeDtypeStruct((8, 32768), jnp.bfloat16)
+
+
+def call_send(back, own, there, pick, signs):
+    scale = jax.ShapeDtypeStruct((512, 128), jnp.float32)
+    return call(send_body, [SMEM] + [VMEM] * 4, [VMEM, VMEM], [HALF, scale], [], 16 * MIB, 0, 4 << 20)(
+        back, own, there, pick, signs
+    )
+
+
+def call_keep(back, own, there, scale):
+    return call(keep_body, [SMEM] + [VMEM] * 3, VMEM, HALF, [], 16 * MIB, 0, 4 << 20)(back, own, there, scale)
+
+
+def call_finish(keep, got):
+    half = pl.BlockSpec((8, 16384), lambda i: (0, i))
+    return pl.pallas_call(
+        finish_body,
+        grid=(2,),
+        in_specs=[half, half],
+        out_specs=pl.BlockSpec((16, 16384), lambda i: (0, i)),
+        out_shape=jax.ShapeDtypeStruct((16, 32768), jnp.bfloat16),
+        compiler_params=pltpu.CompilerParams(vmem_limit_bytes=16 * MIB),
+        cost_estimate=pl.CostEstimate(flops=0, bytes_accessed=2 << 20, transcendentals=0),
+    )(keep, got)
 
 
 def swap(value, mask):
@@ -207,41 +295,30 @@
     back = jnp.sum(my_partner[None, :] < my_partner[:, None], axis=1).astype(int32)
     all_ids = jnp.arange(4096, dtype=int32)
     face_owner = jnp.sum(jnp.where(my_partner[:, None] == all_ids[None, :], owner[None, :], 0), axis=1)
-    index = jnp.stack([arrive, back + back // 16, my_owner ^ pair, face_owner ^ pair, my_sign])
-
-    coded, level = call(
-        product_body, [SMEM, VMEM, VMEM, HBM], [HBM, VMEM],
-        [jax.ShapeDtypeStruct((16, 8, 5, 8, 128), int32), jax.ShapeDtypeStruct((8, 128), int32)],
-        [
-            pltpu.VMEM((80, 4, 128, 128), jnp.bfloat16),
-            pltpu.VMEM((8, 128, 512), jnp.bfloat16),
-            pltpu.VMEM((80, 128, 128), jnp.float32),
-            pltpu.VMEM((16, 8, 5, 8, 128), int32),
-            dma((16,)),
-            dma((16,)),
-        ],
-        52 * MIB, 1_342_177_280, 14 << 20,
-    )(slot_irrep, mine, other, integrals)
+    back = back + back // 16
+    rows = jnp.concatenate([my_owner ^ pair, face_owner ^ pair])
+    pick = (rows[:, None] == jnp.arange(128, dtype=int32)[None, :]).astype(jnp.bfloat16)
+    signs = jnp.concatenate([jnp.ones_like(my_sign), my_sign]).astype(jnp.float32)
+    signs = jnp.broadcast_to(signs[:, None], (512, 128))
+
+    coded, level = call_product(slot_irrep, mine, other, integrals)
     arrived = lax.all_to_all(coded.reshape(128, 40, 128), BOTH, split_axis=0, concat_axis=0, tiled=True)
     arrived = arrived.reshape(640, 8, 128)
     levels = level[:1]
     for mask in (1, 2, 4):
         levels = jnp.concatenate([levels, swap(levels, mask)], axis=0)
     outgoing = call(
-        select_body, [SMEM, VMEM, VMEM], VMEM, jax.ShapeDtypeStruct((16, 17, 8, 128), int32), [], 16 * MIB, 0, 3 << 20
+        select_body, [SMEM, VMEM, VMEM], HBM, pltpu.HBM((16, 17, 8, 128), int32),
+        [pltpu.VMEM((16, 17, 8, 128), int32), dma((4,))], 16 * MIB, 0, 3 << 20,
     )(leaving, arrived, levels)
     incoming = lax.all_to_all(outgoing, "blk", split_axis=0, concat_axis=0, tiled=True).reshape(272, 8, 128)
-    half = jax.ShapeDtypeStruct((8, 32768), jnp.bfloat16)
-    send, table = call(
-        send_body, [SMEM, VMEM, VMEM], [VMEM, VMEM], [half, jax.ShapeDtypeStruct((128, 8, 128), jnp.float32)],
-        [], 16 * MIB, 0, 4 << 20,
-    )(index, arrived, incoming)
+    own = call(
+        gather_body, [SMEM, VMEM], HBM, pltpu.HBM((256, 8, 128), int32), [pltpu.VMEM((256, 8, 128), int32), dma((1,))], 16 * MIB, 0, 2 << 20
+    )(arrive, arrived)
+    send, scale = call_send(back, own, incoming, pick, signs)
     got = swap(send, 4)
-    keep = call(
-        keep_body, [SMEM, VMEM, VMEM, VMEM], VMEM, half, [], 16 * MIB, 0, 4 << 20
-    )(index, arrived, incoming, table)
-    kept = (lax.broadcasted_iota(int32, (2, 1, 1), 0) == pair // 4)
-    return jnp.where(kept, keep[None], got[None]).reshape(16, 32768)
+    keep = call_keep(back, own, incoming, scale)
+    return call_finish(keep, got)
 
 
 def solution(mesh):

time: 135 us -> 131 us (0.970)
  other arithmetic: 6.06 us -> 3.95 us
  Pallas kernels: 21.4 us -> 19.9 us
    all_to_all x1, waiting for transfers between devices: 16 us -> 13.3 us  [local(): lax.all_to_all(outgoing, 'blk', split_axis=0, concat_axis=0, tiled=True)]
    ppermute x5, waiting for transfers between devices: 35.9 us -> 38.2 us  [swap(): return lax.ppermute(value, 'pair', [(i, i ^ mask) for i in range(8)])]
    select_n x1 -> x0, other arithmetic: 2.18 us -> none  [local(): return jnp.where(kept, keep[None], got[None]).reshape(16, 32768)]
    pallas_call x4 -> x6, Pallas kernels: 18.1 us -> 16.6 us  [the longest x1 7.73 us: call_product(): call(product_body, [SMEM, VMEM, VMEM, HBM], [HBM, VMEM], [pltpu.HBM((16,...]
where the time goes in v3:
time: 131 us; the launch traced here: 130 us
  waiting for transfers between devices  63.8 us (49%)
  starting transfers between devices  23.7 us (18%)
  Pallas kernels  19.9 us (15%)
  blocking collectives  16.1 us (12%)
  other arithmetic  3.95 us (3%)
  local copies, waits for them, and re-layouts  2.31 us (2%)
    ppermute x5, waiting for transfers between devices, swap(): return lax.ppermute(value, 'pair', [(i, i ^ mask) for i in range(8)])  38.2 us
    all_to_all x1, blocking collectives, local(): lax.all_to_all(parts, 'blk', split_axis=0, concat_axis=0, tiled=True)  16.1 us
    all_to_all x1, waiting for transfers between devices, local(): lax.all_to_all(outgoing, 'blk', split_axis=0, concat_axis=0, tiled=True)  13.3 us
    all_to_all x1, waiting for transfers between devices, local(): lax.all_to_all(copies, BOTH, split_axis=0, concat_axis=0, tiled=True, axi...  10.7 us
    pallas_call x1, Pallas kernels, call_product(): call(product_body, [SMEM, VMEM, VMEM, HBM], [HBM, VMEM], [pltpu.HBM((16,...  7.73 us
    all_to_all x1, starting transfers between devices, local(): lax.all_to_all(copies, BOTH, split_axis=0, concat_axis=0, tiled=True, axi...  6.64 us
    ppermute x5, starting transfers between devices, swap(): return lax.ppermute(value, 'pair', [(i, i ^ mask) for i in range(8)])  6.48 us
    all_to_all x1, starting transfers between devices, local(): lax.all_to_all(outgoing, 'blk', split_axis=0, concat_axis=0, tiled=True)  5.93 us
  transfers between devices with their start and end apart: 8, of which 8 were waited for; matrix products, arithmetic and copies ran while one was open for 4% of the time, Pallas kernels for 3%

profile of v3, /device:TPU:0, one launch (start us, length us, event | category | flops | bytes accessed | tf_op | source)
XLA Modules:
  0.0 130.1 jit_solution(5151667581573945999)
XLA Ops:
  0.0 2.5 %shard_map.73 = bf16[16,16,256]{2,1,0:T(8,128)(2,1)} custom-call(s32[32]{0:T(128)} %blocks_ref.1, bf16[16,32768]{1,0:T(8,128)(2,1)} %amp_ref.1), custom_call_target="tpu_custom_call" | custom-call | bytes 262144 | tf_op jit(solution)/shard_map/pallas_call | solution.py:267
  2.5 16.1 %all_to_all.20.in_ref = bf16[16,16,256]{2,1,0:T(8,128)(2,1)S(1)} all-to-all(bf16[16,16,256]{2,1,0:T(8,128)(2,1)} %shard_map.73), channel_id=1, replica_groups=mesh['blk'=16,'pair'=8] {'blk'}, dimensions={0} | all-to-all | bytes 262144 | tf_op jit(solution)/shard_map/all_to_all | solution.py:270
  18.6 0.8 shard_map.74
  19.5 6.6 %all-to-all-start.1 = ((bf16[64,16,256]{2,1,0:T(8,128)(2,1)}), bf16[64,16,256]{2,1,0:T(8,128)(2,1)S(1)}, u32[]{:S(2)}, u32[]{:S(2)}) async-start(bf16[64,16,256]{2,1,0:T(8,128)(2,1)} %shard_map.74), calls=%async_computation.1 | async-start | bytes 1048576 | tf_op jit(solution)/shard_map/all_to_all | solution.py:275
  26.2 0.7 broadcast_compare_fusion
  26.9 0.7 broadcast_add_fusion
  27.6 10.7 %all-to-all-done.1.mine_ref = bf16[64,16,256]{2,1,0:T(8,128)(2,1)S(1)} async-done(((bf16[64,16,256]{2,1,0:T(8,128)(2,1)}), bf16[64,16,256]{2,1,0:T(8,128)(2,1)S(1)}, u32[]{:S(2)}, u32[]{:S(2)}) %all-to-all-start.1) | async-done | bytes 524320 | tf_op jit(solution)/shard_map/all_to_all | solution.py:275
  38.5 0.2 select_reduce_fusion.2
  38.9 1.4 %collective-permute-done.other_ref = bf16[64,16,256]{2,1,0:T(8,128)(2,1)S(1)} collective-permute-done((bf16[64,16,256]{2,1,0:T(8,128)(2,1)S(1)}, bf16[64,16,256]{2,1,0:T(8,128)(2,1)S(1)}, u32[]{:S(2)}, u32[]{:S(2)}) %collective-permute-start) | collective-permute-done | bytes 524320 | tf_op jit(solution)/shard_map/ppermute | solution.py:257
  40.3 7.7 %shard_map.75 = (s32[16,8,5,8,128]{4,3,2,1,0:T(8,128)}, s32[8,128]{1,0:T(8,128)S(1)}) custom-call(s32[80]{0:T(128)S(1)} %sub.18.irrep_ref, bf16[64,16,256]{2,1,0:T(8,128)(2,1)S(1)} %all-to-all-done.1.mine_ref, bf16[64,16,256]{2,1,0:T(8,128)(2,1)S(1)} %collective-permute-done.other_ref, bf16[80,4,128,128]{3,2,1,0:T(8,128)(2,1)} %tiles_ref.1), custom_call_target="tpu_custom_call" | custom-call | flops 1342177280 | bytes 14680064 | tf_op jit(solution)/shard_map/pallas_call | solution.py:214
  48.0 4.7 %all-to-all-start.2 = ((s32[128,40,128]{2,1,0:T(8,128)}), s32[128,40,128]{2,1,0:T(8,128)S(1)}, u32[]{:S(2)}, u32[]{:S(2)}) async-start(s32[128,40,128]{2,1,0:T(8,128)} %bitcast.6), calls=%async_computation.2 | async-start | bytes 5242880 | tf_op jit(solution)/shard_map/all_to_all | solution.py:305
  52.7 0.8 iota_add_fusion
  53.8 1.1 collective-permute-done.1
  54.9 0.8 collective-permute-start.2
  55.7 0.2 convert_reduce_fusion
  55.9 26.1 %collective-permute-done.2 = s32[2,128]{1,0:T(2,128)S(1)} collective-permute-done((s32[2,128]{1,0:T(2,128)S(1)}, s32[2,128]{1,0:T(2,128)S(1)}, u32[]{:S(2)}, u32[]{:S(2)}) %collective-permute-start.2) | collective-permute-done | bytes 1056 | tf_op jit(solution)/shard_map/ppermute | solution.py:257
  82.0 2.8 %collective-permute-start.3 = (s32[4,128]{1,0:T(4,128)S(1)}, s32[4,128]{1,0:T(4,128)S(1)}, u32[]{:S(2)}, u32[]{:S(2)}) collective-permute-start(s32[4,128]{1,0:T(4,128)S(1)} %pad_add_fusion.1), channel_id=1, source_target_pairs={{0,4},{1,5},{2,6},{3,7},{4,0},{5,1},{6,2},{7,3},{8,12},{9,13},{10,... | collective-permute-start | bytes 6152 | tf_op jit(solution)/shard_map/ppermute | solution.py:257
  84.9 2.3 %collective-permute-done.3 = s32[4,128]{1,0:T(4,128)S(1)} collective-permute-done((s32[4,128]{1,0:T(4,128)S(1)}, s32[4,128]{1,0:T(4,128)S(1)}, u32[]{:S(2)}, u32[]{:S(2)}) %collective-permute-start.3) | collective-permute-done | bytes 2080 | tf_op jit(solution)/shard_map/ppermute | solution.py:257
  87.2 1.6 %all-to-all-done.2 = s32[128,40,128]{2,1,0:T(8,128)S(1)} async-done(((s32[128,40,128]{2,1,0:T(8,128)}), s32[128,40,128]{2,1,0:T(8,128)S(1)}, u32[]{:S(2)}, u32[]{:S(2)}) %all-to-all-start.2) | async-done | bytes 2621472 | tf_op jit(solution)/shard_map/all_to_all | solution.py:305
  88.7 1.7 %shard_map.77 = s32[16,17,8,128]{3,2,1,0:T(8,128)} custom-call(s32[256]{0:T(256)S(1)} %select_reduce_fusion.1.from_ref, s32[640,8,128]{2,1,0:T(8,128)S(1)} %bitcast.4, s32[8,128]{1,0:T(8,128)S(1)} %pad_add_fusion.level_ref), custom_call_target="tpu_custom_call" | custom-call | bytes 3145728 | tf_op jit(solution)/shard_map/pallas_call | solution.py:310
  90.5 5.9 %all-to-all-start.3 = ((s32[16,17,8,128]{3,2,1,0:T(8,128)}), s32[16,17,8,128]{3,2,1,0:T(8,128)}, u32[]{:S(2)}, u32[]{:S(2)}) async-start(s32[16,17,8,128]{3,2,1,0:T(8,128)} %shard_map.77), calls=%async_computation.3 | async-start | bytes 2228224 | tf_op jit(solution)/shard_map/all_to_all | solution.py:314
  96.4 0.7 select_reduce_fusion
  97.1 0.8 dynamic_slice.11
  97.9 0.2 convert_reduce_fusion.2
  98.2 1.9 %shard_map.76.own_ref = s32[256,8,128]{2,1,0:T(8,128)} custom-call(s32[256]{0:T(256)S(1)} %multiply_add_fusion.from_ref, s32[640,8,128]{2,1,0:T(8,128)S(1)} %bitcast.5), custom_call_target="tpu_custom_call" | custom-call | bytes 2097152 | tf_op jit(solution)/shard_map/pallas_call | solution.py:315
  100.1 13.3 %all-to-all-done.3 = s32[16,17,8,128]{3,2,1,0:T(8,128)} async-done(((s32[16,17,8,128]{3,2,1,0:T(8,128)}), s32[16,17,8,128]{3,2,1,0:T(8,128)}, u32[]{:S(2)}, u32[]{:S(2)}) %all-to-all-start.3) | async-done | bytes 1114144 | tf_op jit(solution)/shard_map/all_to_all | solution.py:314
  113.6 1.2 copy-done
  114.8 2.2 %shard_map.78 = (bf16[8,32768]{1,0:T(8,128)(2,1)S(1)}, f32[512,128]{1,0:T(8,128)S(1)}) custom-call(s32[256]{0:T(256)S(1)} %fusion.3.back_ref, s32[256,8,128]{2,1,0:T(8,128)S(1)} %copy-done, s32[272,8,128]{2,1,0:T(8,128)} %bitcast.2.there_ref, bf16[512,128]{1,0:T(8,128)(2,1)S(1)} %fusion.1.pick_ref, f32[512,128]{1,0:T(8,128)S(1)} %broadcast_in_dim.44.sign_ref), custom_call_target="tpu_custom_call" | custom-call | bytes 4194304 | tf_op jit(solution)/shard_map/pallas_call | solution.py:234
  117.0 2.8 %collective-permute-start.4 = (bf16[8,32768]{1,0:T(8,128)(2,1)S(1)}, bf16[8,32768]{1,0:T(8,128)(2,1)S(1)}, u32[]{:S(2)}, u32[]{:S(2)}) collective-permute-start(bf16[8,32768]{1,0:T(8,128)(2,1)S(1)} %get-tuple-element.12), channel_id=1, source_target_pairs={{0,4},{1,5},{2,6},{3,7},{4,0},{5,1},{6,2},{7,3},{8,12},{9,13},{10,... | collective-permute-start | bytes 1572872 | tf_op jit(solution)/shard_map/ppermute | solution.py:257
  119.8 2.0 %shard_map.79.keep_ref = bf16[8,32768]{1,0:T(8,128)(2,1)S(1)} custom-call(s32[256]{0:T(256)S(1)} %fusion.3.back_ref, s32[256,8,128]{2,1,0:T(8,128)S(1)} %copy-done, s32[272,8,128]{2,1,0:T(8,128)} %bitcast.2.there_ref, f32[512,128]{1,0:T(8,128)S(1)} %get-tuple-element.11.scale_ref), custom_call_target="tpu_custom_call" | custom-call | bytes 4194304 | tf_op jit(solution)/shard_map/pallas_call | solution.py:240
  121.8 7.4 %collective-permute-done.4.got_ref = bf16[8,32768]{1,0:T(8,128)(2,1)S(1)} collective-permute-done((bf16[8,32768]{1,0:T(8,128)(2,1)S(1)}, bf16[8,32768]{1,0:T(8,128)(2,1)S(1)}, u32[]{:S(2)}, u32[]{:S(2)}) %collective-permute-start.4) | collective-permute-done | bytes 524320 | tf_op jit(solution)/shard_map/ppermute | solution.py:257
  129.1 1.0 shard_map.80
  (24 shorter events, 1.1 us)
Async XLA Ops:
  19.5 18.9 %all-to-all-start.1 = ((bf16[64,16,256]{2,1,0:T(8,128)(2,1)}), bf16[64,16,256]{2,1,0:T(8,128)(2,1)S(1)}, u32[]{:S(2)}, u32[]{:S(2)}) async-start(bf16[64,16,256]{2,1,0:T(8,128)(2,1)} %shard_map.74), calls=%async_computation.1 | async-start | bytes 1048576 | tf_op jit(solution)/shard_map/all_to_all | solution.py:275
  38.4 1.9 %collective-permute-start = (bf16[64,16,256]{2,1,0:T(8,128)(2,1)S(1)}, bf16[64,16,256]{2,1,0:T(8,128)(2,1)S(1)}, u32[]{:S(2)}, u32[]{:S(2)}) collective-permute-start(bf16[64,16,256]{2,1,0:T(8,128)(2,1)S(1)} %all-to-all-done.1.mine_ref), channel_id=1, source_target_pairs={{0,1},{1,0},{2,3},{3,2},{4,5},{5,4},{6,7},{7,6},{8,9},{9,8},{10,11... | collective-permute-start | bytes 1572872 | tf_op jit(solution)/shard_map/ppermute | solution.py:257
  48.0 4.7 %copy-start.1 = (s32[4096]{0:T(1024)S(1)}, s32[4096]{0:T(1024)}, u32[]{:S(2)}) copy-start(s32[4096]{0:T(1024)} %param.11) | copy-start | bytes 49156
  48.0 40.7 %all-to-all-start.2 = ((s32[128,40,128]{2,1,0:T(8,128)}), s32[128,40,128]{2,1,0:T(8,128)S(1)}, u32[]{:S(2)}, u32[]{:S(2)}) async-start(s32[128,40,128]{2,1,0:T(8,128)} %bitcast.6), calls=%async_computation.2 | async-start | bytes 5242880 | tf_op jit(solution)/shard_map/all_to_all | solution.py:305
  53.7 1.2 collective-permute-start.1
  54.9 27.1 %collective-permute-start.2 = (s32[2,128]{1,0:T(2,128)S(1)}, s32[2,128]{1,0:T(2,128)S(1)}, u32[]{:S(2)}, u32[]{:S(2)}) collective-permute-start(s32[2,128]{1,0:T(2,128)S(1)} %pad_add_fusion.3), channel_id=1, source_target_pairs={{0,2},{1,3},{2,0},{3,1},{4,6},{5,7},{6,4},{7,5},{8,10},{9,11},{10,... | collective-permute-start | bytes 3080 | tf_op jit(solution)/shard_map/ppermute | solution.py:257
  82.0 5.2 %collective-permute-start.3 = (s32[4,128]{1,0:T(4,128)S(1)}, s32[4,128]{1,0:T(4,128)S(1)}, u32[]{:S(2)}, u32[]{:S(2)}) collective-permute-start(s32[4,128]{1,0:T(4,128)S(1)} %pad_add_fusion.1), channel_id=1, source_target_pairs={{0,4},{1,5},{2,6},{3,7},{4,0},{5,1},{6,2},{7,3},{8,12},{9,13},{10,... | collective-permute-start | bytes 6152 | tf_op jit(solution)/shard_map/ppermute | solution.py:257
  90.5 23.0 %all-to-all-start.3 = ((s32[16,17,8,128]{3,2,1,0:T(8,128)}), s32[16,17,8,128]{3,2,1,0:T(8,128)}, u32[]{:S(2)}, u32[]{:S(2)}) async-start(s32[16,17,8,128]{3,2,1,0:T(8,128)} %shard_map.77), calls=%async_computation.3 | async-start | bytes 2228224 | tf_op jit(solution)/shard_map/all_to_all | solution.py:314
  113.5 1.2 copy-start
  117.0 12.1 %collective-permute-start.4 = (bf16[8,32768]{1,0:T(8,128)(2,1)S(1)}, bf16[8,32768]{1,0:T(8,128)(2,1)S(1)}, u32[]{:S(2)}, u32[]{:S(2)}) collective-permute-start(bf16[8,32768]{1,0:T(8,128)(2,1)S(1)} %get-tuple-element.12), channel_id=1, source_target_pairs={{0,4},{1,5},{2,6},{3,7},{4,0},{5,1},{6,2},{7,3},{8,12},{9,13},{10,... | collective-permute-start | bytes 1572872 | tf_op jit(solution)/shard_map/ppermute | solution.py:257

commit v4 on v3

--- a/solution.py
+++ b/solution.py
@@ -67,7 +67,7 @@
 
 
 def row_tiles(p):
-    return (2 * p, 2 * p + 8) if p < 4 else (2 * (p - 4) + 9, 2 * (p - 4) + 1)
+    return 2 * (p ^ 4), 2 * (p ^ 4) + 1
 
 
 def product_body(irrep_ref, mine_ref, other_ref, tiles_ref, out_ref, level_ref, held, slab, prod, code, in_sems, out_sems):
@@ -150,62 +150,39 @@
         store(c).wait()
 
 
-def gather_body(from_ref, in_ref, out_ref, picked, sems):
-    def one(step, carry):
-        for i in range(16):
-            picked[step * 16 + i] = in_ref[from_ref[step * 16 + i]]
-        return carry
-
-    lax.fori_loop(0, 16, one, 0)
-    store = pltpu.make_async_copy(picked, out_ref, sems.at[0])
-    store.start()
-    store.wait()
-
-
-def combine(back_ref, own_ref, there_ref, scale_ref, out_ref, own_part, face_part):
-    def one(step, carry):
-        rows = pl.multiple_of(step * 8, 8)
-        own_scale = scale_ref[pl.ds(rows, 8), :]
-        face_scale = scale_ref[pl.ds(256 + rows, 8), :]
-        values = []
-        for i in range(8):
-            own = own_part(own_ref[step * 8 + i]).astype(jnp.float32)
-            face = face_part(there_ref[back_ref[step * 8 + i]]).astype(jnp.float32)
-            values.append((own * own_scale[i : i + 1, :] + face * face_scale[i : i + 1, :]).astype(jnp.bfloat16))
-        for i in range(8):
-            out_ref[:, pl.ds(pl.multiple_of((step * 8 + i) * 128, 128), 128)] = values[i]
-        return carry
-
-    lax.fori_loop(0, 32, one, 0)
-
-
-def high_part(word):
-    return word >> 16
-
-
-def low_part(word):
-    return (word << 16) >> 16
-
-
-def send_body(back_ref, own_ref, there_ref, pick_ref, sign_ref, out_ref, scale_ref):
+def combine_body(own_ref, face_ref, here_ref, there_ref, pick_ref, sign_ref, out_ref, scale, result, sems):
     levels = jnp.concatenate([there_ref[s * 17 + 16] for s in range(16)], axis=0)
     pick = pick_ref[...]
     upper = jnp.dot(pick, (levels >> 5).astype(jnp.bfloat16), preferred_element_type=jnp.float32)
     lower = jnp.dot(pick, (levels & 31).astype(jnp.bfloat16), preferred_element_type=jnp.float32)
-    scale_ref[...] = jnp.exp((upper * 32.0 + lower) * (LN2 / STEPS)) * (1.0 / TOP) * sign_ref[...]
-    combine(back_ref, own_ref, there_ref, scale_ref, out_ref, low_part, high_part)
-
-
-def keep_body(back_ref, own_ref, there_ref, scale_ref, out_ref):
-    combine(back_ref, own_ref, there_ref, scale_ref, out_ref, high_part, low_part)
-
-
-def finish_body(keep_ref, got_ref, out_ref):
-    first = lax.axis_index("pair") < 4
-    keep = keep_ref[...]
-    got = got_ref[...]
-    out_ref[0:8, :] = jnp.where(first, keep, got)
-    out_ref[8:16, :] = jnp.where(first, got, keep)
+    scale[...] = jnp.exp((upper * 32.0 + lower) * (LN2 / STEPS)) * (1.0 / TOP) * sign_ref[...]
+
+    def store(c):
+        span = pl.ds(c * 8192, 8192)
+        return pltpu.make_async_copy(result.at[:, span], out_ref.at[:, span], sems.at[c])
+
+    def parts(word):
+        return (word >> 16).astype(jnp.float32), ((word << 16) >> 16).astype(jnp.float32)
+
+    def one(step, carry):
+        rows = pl.multiple_of(step * 8, 8)
+        own_scale = scale[pl.ds(rows, 8), :]
+        face_scale = scale[pl.ds(256 + rows, 8), :]
+        values = []
+        for i in range(8):
+            own = parts(here_ref[own_ref[step * 8 + i]])
+            face = parts(there_ref[face_ref[step * 8 + i]])
+            halves = [o * own_scale[i : i + 1, :] + f * face_scale[i : i + 1, :] for o, f in zip(own, face)]
+            values.append(jnp.concatenate(halves, axis=0).astype(jnp.bfloat16))
+        for i in range(8):
+            result[:, pl.ds(pl.multiple_of((step * 8 + i) * 128, 128), 128)] = values[i]
+        return carry
+
+    for c in range(4):
+        lax.fori_loop(c * 8, c * 8 + 8, one, 0)
+        store(c).start()
+    for c in range(4):
+        store(c).wait()
 
 
 def call_product(irreps, mine, other, tiles):
@@ -226,31 +203,16 @@
     )(irreps, mine, other, tiles)
 
 
-HALF = jax.ShapeDtypeStruct((8, 32768), jnp.bfloat16)
-
-
-def call_send(back, own, there, pick, signs):
-    scale = jax.ShapeDtypeStruct((512, 128), jnp.float32)
-    return call(send_body, [SMEM] + [VMEM] * 4, [VMEM, VMEM], [HALF, scale], [], 16 * MIB, 0, 4 << 20)(
-        back, own, there, pick, signs
+def call_combine(own, face, here, there, pick, signs):
+    scratch = [
+        pltpu.VMEM((512, 128), jnp.float32),
+        pltpu.VMEM((16, 32768), jnp.bfloat16),
+        pltpu.SemaphoreType.DMA((4,)),
+    ]
+    out = jax.ShapeDtypeStruct((16, 32768), jnp.bfloat16)
+    return call(combine_body, [SMEM] * 2 + [VMEM] * 4, HBM, out, scratch, 16 * MIB, 0, 4 << 20)(
+        own, face, here, there, pick, signs
     )
-
-
-def call_keep(back, own, there, scale):
-    return call(keep_body, [SMEM] + [VMEM] * 3, VMEM, HALF, [], 16 * MIB, 0, 4 << 20)(back, own, there, scale)
-
-
-def call_finish(keep, got):
-    half = pl.BlockSpec((8, 16384), lambda i: (0, i))
-    return pl.pallas_call(
-        finish_body,
-        grid=(2,),
-        in_specs=[half, half],
-        out_specs=pl.BlockSpec((16, 16384), lambda i: (0, i)),
-        out_shape=jax.ShapeDtypeStruct((16, 32768), jnp.bfloat16),
-        compiler_params=pltpu.CompilerParams(vmem_limit_bytes=16 * MIB),
-        cost_estimate=pl.CostEstimate(flops=0, bytes_accessed=2 << 20, transcendentals=0),
-    )(keep, got)
 
 
 def swap(value, mask):
@@ -311,14 +273,9 @@
         select_body, [SMEM, VMEM, VMEM], HBM, pltpu.HBM((16, 17, 8, 128), int32),
         [pltpu.VMEM((16, 17, 8, 128), int32), dma((4,))], 16 * MIB, 0, 3 << 20,
     )(leaving, arrived, levels)
+    own = swap(outgoing, 4).reshape(272, 8, 128)
     incoming = lax.all_to_all(outgoing, "blk", split_axis=0, concat_axis=0, tiled=True).reshape(272, 8, 128)
-    own = call(
-        gather_body, [SMEM, VMEM], HBM, pltpu.HBM((256, 8, 128), int32), [pltpu.VMEM((256, 8, 128), int32), dma((1,))], 16 * MIB, 0, 2 << 20
-    )(arrive, arrived)
-    send, scale = call_send(back, own, incoming, pick, signs)
-    got = swap(send, 4)
-    keep = call_keep(back, own, incoming, scale)
-    return call_finish(keep, got)
+    return call_combine(leave + leave // 16, back, own, incoming, pick, signs)
 
 
 def solution(mesh):

time: 131 us -> 121 us (0.924)
  Pallas kernels: 19.9 us -> 14.7 us
  waiting for transfers between devices: 63.8 us -> 60.3 us
    ppermute x5, waiting for transfers between devices: 38.2 us -> 32.4 us  [swap(): return lax.ppermute(value, 'pair', [(i, i ^ mask) for i in range(8)])]
    pallas_call x4 -> x1, Pallas kernels: 7.1 us -> 2.48 us  [call_combine(): call(combine_body, [SMEM] * 2 + [VMEM] * 4, HBM, out, scratch, 16 * MIB,...]
    all_to_all x1, waiting for transfers between devices: 13.3 us -> 15.6 us  [local(): lax.all_to_all(outgoing, 'blk', split_axis=0, concat_axis=0, tiled=True)]
    ppermute x5, starting transfers between devices: 6.48 us -> 4.93 us  [swap(): return lax.ppermute(value, 'pair', [(i, i ^ mask) for i in range(8)])]
    all_to_all x1, starting transfers between devices: 5.93 us -> 7.43 us  [local(): lax.all_to_all(outgoing, 'blk', split_axis=0, concat_axis=0, tiled=True)]
  transfers between devices with their start and end apart: 8 -> 8, of which waited for: 8 -> 8; matrix products, arithmetic and copies ran while one was open for 4% -> 4% of each run, Pallas kernels for 3% -> 0%
where the time goes in v4:
time: 121 us
  waiting for transfers between devices  60.3 us (50%)
  starting transfers between devices  23.7 us (20%)
  blocking collectives  16.5 us (14%)
  Pallas kernels  14.7 us (12%)
  other arithmetic  3.95 us (3%)
    ppermute x5, waiting for transfers between devices, swap(): return lax.ppermute(value, 'pair', [(i, i ^ mask) for i in range(8)])  32.4 us
    all_to_all x1, blocking collectives, local(): lax.all_to_all(parts, 'blk', split_axis=0, concat_axis=0, tiled=True)  16.5 us
    all_to_all x1, waiting for transfers between devices, local(): lax.all_to_all(outgoing, 'blk', split_axis=0, concat_axis=0, tiled=True)  15.6 us
    all_to_all x1, waiting for transfers between devices, local(): lax.all_to_all(copies, BOTH, split_axis=0, concat_axis=0, tiled=True, axi...  10.7 us
    pallas_call x1, Pallas kernels, call_product(): call(product_body, [SMEM, VMEM, VMEM, HBM], [HBM, VMEM], [pltpu.HBM((16,...  7.73 us
    all_to_all x1, starting transfers between devices, local(): lax.all_to_all(outgoing, 'blk', split_axis=0, concat_axis=0, tiled=True)  7.43 us
    all_to_all x1, starting transfers between devices, local(): lax.all_to_all(copies, BOTH, split_axis=0, concat_axis=0, tiled=True, axi...  6.64 us
    ppermute x5, starting transfers between devices, swap(): return lax.ppermute(value, 'pair', [(i, i ^ mask) for i in range(8)])  4.93 us
  transfers between devices with their start and end apart: 8, of which 8 were waited for; matrix products, arithmetic and copies ran while one was open for 4% of the time, Pallas kernels for 0%

profile of v4, /device:TPU:0, one launch (start us, length us, event | category | flops | bytes accessed | tf_op | source)
XLA Modules:
  0.0 120.6 jit_solution(8179691041412948544)
XLA Ops:
  0.0 2.0 %shard_map.73 = bf16[16,16,256]{2,1,0:T(8,128)(2,1)} custom-call(s32[32]{0:T(128)} %blocks_ref.1, bf16[16,32768]{1,0:T(8,128)(2,1)} %amp_ref.1), custom_call_target="tpu_custom_call" | custom-call | bytes 262144 | tf_op jit(solution)/shard_map/pallas_call | solution.py:229
  2.0 16.5 %all_to_all.20.in_ref = bf16[16,16,256]{2,1,0:T(8,128)(2,1)S(1)} all-to-all(bf16[16,16,256]{2,1,0:T(8,128)(2,1)} %shard_map.73), channel_id=1, replica_groups=mesh['blk'=16,'pair'=8] {'blk'}, dimensions={0} | all-to-all | bytes 262144 | tf_op jit(solution)/shard_map/all_to_all | solution.py:232
  18.5 0.8 shard_map.74
  19.4 6.6 %all-to-all-start.1 = ((bf16[64,16,256]{2,1,0:T(8,128)(2,1)}), bf16[64,16,256]{2,1,0:T(8,128)(2,1)S(1)}, u32[]{:S(2)}, u32[]{:S(2)}) async-start(bf16[64,16,256]{2,1,0:T(8,128)(2,1)} %shard_map.74), calls=%async_computation.1 | async-start | bytes 1048576 | tf_op jit(solution)/shard_map/all_to_all | solution.py:237
  26.0 0.7 broadcast_compare_fusion
  26.8 0.7 broadcast_add_fusion
  27.5 10.7 %all-to-all-done.1.mine_ref = bf16[64,16,256]{2,1,0:T(8,128)(2,1)S(1)} async-done(((bf16[64,16,256]{2,1,0:T(8,128)(2,1)}), bf16[64,16,256]{2,1,0:T(8,128)(2,1)S(1)}, u32[]{:S(2)}, u32[]{:S(2)}) %all-to-all-start.1) | async-done | bytes 524320 | tf_op jit(solution)/shard_map/all_to_all | solution.py:237
  38.3 0.1 convolution_convert_fusion
  38.4 0.2 select_reduce_fusion.2
  38.8 1.4 %collective-permute-done.other_ref = bf16[64,16,256]{2,1,0:T(8,128)(2,1)S(1)} collective-permute-done((bf16[64,16,256]{2,1,0:T(8,128)(2,1)S(1)}, bf16[64,16,256]{2,1,0:T(8,128)(2,1)S(1)}, u32[]{:S(2)}, u32[]{:S(2)}) %collective-permute-start) | collective-permute-done | bytes 524320 | tf_op jit(solution)/shard_map/ppermute | solution.py:219
  40.2 7.7 %shard_map.75 = (s32[16,8,5,8,128]{4,3,2,1,0:T(8,128)}, s32[8,128]{1,0:T(8,128)S(1)}) custom-call(s32[80]{0:T(128)S(1)} %sub.24.irrep_ref, bf16[64,16,256]{2,1,0:T(8,128)(2,1)S(1)} %all-to-all-done.1.mine_ref, bf16[64,16,256]{2,1,0:T(8,128)(2,1)S(1)} %collective-permute-done.other_ref, bf16[80,4,128,128]{3,2,1,0:T(8,128)(2,1)} %tiles_ref.1), custom_call_target="tpu_custom_call" | custom-call | flops 1342177280 | bytes 14680064 | tf_op jit(solution)/shard_map/pallas_call | solution.py:191
  47.9 4.7 %all-to-all-start.2 = ((s32[128,40,128]{2,1,0:T(8,128)}), s32[128,40,128]{2,1,0:T(8,128)S(1)}, u32[]{:S(2)}, u32[]{:S(2)}) async-start(s32[128,40,128]{2,1,0:T(8,128)} %bitcast.8), calls=%async_computation.2 | async-start | bytes 5242880 | tf_op jit(solution)/shard_map/all_to_all | solution.py:267
  52.6 0.8 iota_add_fusion
  53.4 0.2 convert_reduce_fusion
  53.7 0.7 select_reduce_fusion
  54.4 0.4 collective-permute-done.1
  54.8 0.8 collective-permute-start.2
  55.6 0.2 convert_reduce_fusion.2
  55.8 26.1 %collective-permute-done.2 = s32[2,128]{1,0:T(2,128)S(1)} collective-permute-done((s32[2,128]{1,0:T(2,128)S(1)}, s32[2,128]{1,0:T(2,128)S(1)}, u32[]{:S(2)}, u32[]{:S(2)}) %collective-permute-start.2) | collective-permute-done | bytes 1056 | tf_op jit(solution)/shard_map/ppermute | solution.py:219
  81.9 2.8 %collective-permute-start.3 = (s32[4,128]{1,0:T(4,128)S(1)}, s32[4,128]{1,0:T(4,128)S(1)}, u32[]{:S(2)}, u32[]{:S(2)}) collective-permute-start(s32[4,128]{1,0:T(4,128)S(1)} %pad_add_fusion.1), channel_id=1, source_target_pairs={{0,4},{1,5},{2,6},{3,7},{4,0},{5,1},{6,2},{7,3},{8,12},{9,13},{10,... | collective-permute-start | bytes 6152 | tf_op jit(solution)/shard_map/ppermute | solution.py:219
  84.8 2.3 %collective-permute-done.3 = s32[4,128]{1,0:T(4,128)S(1)} collective-permute-done((s32[4,128]{1,0:T(4,128)S(1)}, s32[4,128]{1,0:T(4,128)S(1)}, u32[]{:S(2)}, u32[]{:S(2)}) %collective-permute-start.3) | collective-permute-done | bytes 2080 | tf_op jit(solution)/shard_map/ppermute | solution.py:219
  87.1 1.6 %all-to-all-done.2 = s32[128,40,128]{2,1,0:T(8,128)S(1)} async-done(((s32[128,40,128]{2,1,0:T(8,128)}), s32[128,40,128]{2,1,0:T(8,128)S(1)}, u32[]{:S(2)}, u32[]{:S(2)}) %all-to-all-start.2) | async-done | bytes 2621472 | tf_op jit(solution)/shard_map/all_to_all | solution.py:267
  88.6 1.7 %shard_map.76 = s32[16,17,8,128]{3,2,1,0:T(8,128)} custom-call(s32[256]{0:T(256)S(1)} %select_reduce_fusion.1.from_ref, s32[640,8,128]{2,1,0:T(8,128)S(1)} %bitcast.5, s32[8,128]{1,0:T(8,128)S(1)} %pad_add_fusion.level_ref), custom_call_target="tpu_custom_call" | custom-call | bytes 3145728 | tf_op jit(solution)/shard_map/pallas_call | solution.py:272
  90.3 1.2 %collective-permute-start.4 = (s32[16,17,8,128]{3,2,1,0:T(8,128)}, s32[16,17,8,128]{3,2,1,0:T(8,128)S(1)}, u32[]{:S(2)}, u32[]{:S(2)}) collective-permute-start(s32[16,17,8,128]{3,2,1,0:T(8,128)} %shard_map.76), channel_id=1, source_target_pairs={{0,4},{1,5},{2,6},{3,7},{4,0},{5,1},{6,2},{7,3},{8,12},{9,13},{10,... | collective-permute-start | bytes 3342344 | tf_op jit(solution)/shard_map/ppermute | solution.py:219
  91.5 7.4 %all-to-all-start.3 = ((s32[16,17,8,128]{3,2,1,0:T(8,128)}), s32[16,17,8,128]{3,2,1,0:T(8,128)S(1)}, u32[]{:S(2)}, u32[]{:S(2)}) async-start(s32[16,17,8,128]{3,2,1,0:T(8,128)} %shard_map.76), calls=%async_computation.3 | async-start | bytes 2228224 | tf_op jit(solution)/shard_map/all_to_all | solution.py:277
  99.0 0.8 dynamic_slice.11
  99.7 0.2 convert_reduce_fusion.1
  100.0 0.1 fusion.1.pick_ref
  100.1 15.6 %all-to-all-done.3 = s32[16,17,8,128]{3,2,1,0:T(8,128)S(1)} async-done(((s32[16,17,8,128]{3,2,1,0:T(8,128)}), s32[16,17,8,128]{3,2,1,0:T(8,128)S(1)}, u32[]{:S(2)}, u32[]{:S(2)}) %all-to-all-start.3) | async-done | bytes 1114144 | tf_op jit(solution)/shard_map/all_to_all | solution.py:277
  115.7 2.3 %collective-permute-done.4 = s32[16,17,8,128]{3,2,1,0:T(8,128)S(1)} collective-permute-done((s32[16,17,8,128]{3,2,1,0:T(8,128)}, s32[16,17,8,128]{3,2,1,0:T(8,128)S(1)}, u32[]{:S(2)}, u32[]{:S(2)}) %collective-permute-start.4) | collective-permute-done | bytes 1114144 | tf_op jit(solution)/shard_map/ppermute | solution.py:219
  118.0 0.1 broadcast_in_dim.44.sign_ref
  118.1 2.5 %shard_map.77 = bf16[16,32768]{1,0:T(8,128)(2,1)} custom-call(s32[256]{0:T(256)S(1)} %fusion.3.own_ref, s32[256]{0:T(256)S(1)} %fusion.4.face_ref, s32[272,8,128]{2,1,0:T(8,128)S(1)} %bitcast.7, s32[272,8,128]{2,1,0:T(8,128)S(1)} %bitcast.6, bf16[512,128]{1,0:T(8,128)(2,1)S(1)} %fusion.1.pick_ref, f32[512,128]{1,0:T(8,128)S(1)} %broadcast_in_dim.44.sign_ref), custom_call_target="tpu_custom_call" | custom-call | bytes 4194304 | tf_op jit(solution)/shard_map/pallas_call | solution.py:213
  (20 shorter events, 0.5 us)
Async XLA Ops:
  19.4 18.9 %all-to-all-start.1 = ((bf16[64,16,256]{2,1,0:T(8,128)(2,1)}), bf16[64,16,256]{2,1,0:T(8,128)(2,1)S(1)}, u32[]{:S(2)}, u32[]{:S(2)}) async-start(bf16[64,16,256]{2,1,0:T(8,128)(2,1)} %shard_map.74), calls=%async_computation.1 | async-start | bytes 1048576 | tf_op jit(solution)/shard_map/all_to_all | solution.py:237
  38.3 1.9 %collective-permute-start = (bf16[64,16,256]{2,1,0:T(8,128)(2,1)S(1)}, bf16[64,16,256]{2,1,0:T(8,128)(2,1)S(1)}, u32[]{:S(2)}, u32[]{:S(2)}) collective-permute-start(bf16[64,16,256]{2,1,0:T(8,128)(2,1)S(1)} %all-to-all-done.1.mine_ref), channel_id=1, source_target_pairs={{0,1},{1,0},{2,3},{3,2},{4,5},{5,4},{6,7},{7,6},{8,9},{9,8},{10,11... | collective-permute-start | bytes 1572872 | tf_op jit(solution)/shard_map/ppermute | solution.py:219
  47.9 4.7 %copy-start = (s32[4096]{0:T(1024)S(1)}, s32[4096]{0:T(1024)}, u32[]{:S(2)}) copy-start(s32[4096]{0:T(1024)} %param.11) | copy-start | bytes 49156
  47.9 40.7 %all-to-all-start.2 = ((s32[128,40,128]{2,1,0:T(8,128)}), s32[128,40,128]{2,1,0:T(8,128)S(1)}, u32[]{:S(2)}, u32[]{:S(2)}) async-start(s32[128,40,128]{2,1,0:T(8,128)} %bitcast.8), calls=%async_computation.2 | async-start | bytes 5242880 | tf_op jit(solution)/shard_map/all_to_all | solution.py:267
  53.6 1.2 collective-permute-start.1
  54.8 27.1 %collective-permute-start.2 = (s32[2,128]{1,0:T(2,128)S(1)}, s32[2,128]{1,0:T(2,128)S(1)}, u32[]{:S(2)}, u32[]{:S(2)}) collective-permute-start(s32[2,128]{1,0:T(2,128)S(1)} %pad_add_fusion.3), channel_id=1, source_target_pairs={{0,2},{1,3},{2,0},{3,1},{4,6},{5,7},{6,4},{7,5},{8,10},{9,11},{10,... | collective-permute-start | bytes 3080 | tf_op jit(solution)/shard_map/ppermute | solution.py:219
  81.9 5.2 %collective-permute-start.3 = (s32[4,128]{1,0:T(4,128)S(1)}, s32[4,128]{1,0:T(4,128)S(1)}, u32[]{:S(2)}, u32[]{:S(2)}) collective-permute-start(s32[4,128]{1,0:T(4,128)S(1)} %pad_add_fusion.1), channel_id=1, source_target_pairs={{0,4},{1,5},{2,6},{3,7},{4,0},{5,1},{6,2},{7,3},{8,12},{9,13},{10,... | collective-permute-start | bytes 6152 | tf_op jit(solution)/shard_map/ppermute | solution.py:219
  90.3 27.7 %collective-permute-start.4 = (s32[16,17,8,128]{3,2,1,0:T(8,128)}, s32[16,17,8,128]{3,2,1,0:T(8,128)S(1)}, u32[]{:S(2)}, u32[]{:S(2)}) collective-permute-start(s32[16,17,8,128]{3,2,1,0:T(8,128)} %shard_map.76), channel_id=1, source_target_pairs={{0,4},{1,5},{2,6},{3,7},{4,0},{5,1},{6,2},{7,3},{8,12},{9,13},{10,... | collective-permute-start | bytes 3342344 | tf_op jit(solution)/shard_map/ppermute | solution.py:219
  91.5 24.1 %all-to-all-start.3 = ((s32[16,17,8,128]{3,2,1,0:T(8,128)}), s32[16,17,8,128]{3,2,1,0:T(8,128)S(1)}, u32[]{:S(2)}, u32[]{:S(2)}) async-start(s32[16,17,8,128]{3,2,1,0:T(8,128)} %shard_map.76), calls=%async_computation.3 | async-start | bytes 2228224 | tf_op jit(solution)/shard_map/all_to_all | solution.py:277

commit v5 on v4

--- a/solution.py
+++ b/solution.py
@@ -132,10 +132,14 @@
         store(t).wait()
 
 
-def select_body(from_ref, in_ref, level_ref, out_ref, picked, sems):
+def select_body(from_ref, in_ref, level_ref, out_ref, words_ref, picked, sems, word_sems):
     def store(c):
         span = pl.ds(c * 4, 4)
         return pltpu.make_async_copy(picked.at[span], out_ref.at[span], sems.at[c])
+
+    def store_words(c):
+        span = pl.ds(c * 4, 4)
+        return pltpu.make_async_copy(picked.at[span, pl.ds(0, 16)], words_ref.at[span], word_sems.at[c])
 
     def one(t, carry):
         for i in range(16):
@@ -145,8 +149,10 @@
 
     for c in range(4):
         lax.fori_loop(c * 4, c * 4 + 4, one, 0)
+        store_words(c).start()
         store(c).start()
     for c in range(4):
+        store_words(c).wait()
         store(c).wait()
 
 
@@ -269,13 +275,14 @@
     levels = level[:1]
     for mask in (1, 2, 4):
         levels = jnp.concatenate([levels, swap(levels, mask)], axis=0)
-    outgoing = call(
-        select_body, [SMEM, VMEM, VMEM], HBM, pltpu.HBM((16, 17, 8, 128), int32),
-        [pltpu.VMEM((16, 17, 8, 128), int32), dma((4,))], 16 * MIB, 0, 3 << 20,
+    outgoing, words = call(
+        select_body, [SMEM, VMEM, VMEM], [HBM, HBM],
+        [pltpu.HBM((16, 17, 8, 128), int32), pltpu.HBM((16, 16, 8, 128), int32)],
+        [pltpu.VMEM((16, 17, 8, 128), int32), dma((4,)), dma((4,))], 16 * MIB, 0, 4 << 20,
     )(leaving, arrived, levels)
-    own = swap(outgoing, 4).reshape(272, 8, 128)
+    own = swap(words, 4).reshape(256, 8, 128)
     incoming = lax.all_to_all(outgoing, "blk", split_axis=0, concat_axis=0, tiled=True).reshape(272, 8, 128)
-    return call_combine(leave + leave // 16, back, own, incoming, pick, signs)
+    return call_combine(leave, back, own, incoming, pick, signs)
 
 
 def solution(mesh):

time: 121 us -> 120 us (level)
  waiting for transfers between devices: 60.3 us -> 58.9 us
where the time goes in v5:
time: 120 us
  waiting for transfers between devices  58.9 us (49%)
  starting transfers between devices  23.7 us (20%)
  blocking collectives  16.1 us (13%)
  Pallas kernels  15.6 us (13%)
  other arithmetic  3.95 us (3%)
    ppermute x5, waiting for transfers between devices, swap(): return lax.ppermute(value, 'pair', [(i, i ^ mask) for i in range(8)])  31.7 us
    all_to_all x1, blocking collectives, local(): lax.all_to_all(parts, 'blk', split_axis=0, concat_axis=0, tiled=True)  16.1 us
    all_to_all x1, waiting for transfers between devices, local(): lax.all_to_all(outgoing, 'blk', split_axis=0, concat_axis=0, tiled=True)  14.9 us
    all_to_all x1, waiting for transfers between devices, local(): lax.all_to_all(copies, BOTH, split_axis=0, concat_axis=0, tiled=True, axi...  10.7 us
    pallas_call x1, Pallas kernels, call_product(): call(product_body, [SMEM, VMEM, VMEM, HBM], [HBM, VMEM], [pltpu.HBM((16,...  7.73 us
    all_to_all x1, starting transfers between devices, local(): lax.all_to_all(outgoing, 'blk', split_axis=0, concat_axis=0, tiled=True)  7.43 us
    all_to_all x1, starting transfers between devices, local(): lax.all_to_all(copies, BOTH, split_axis=0, concat_axis=0, tiled=True, axi...  6.64 us
    ppermute x5, starting transfers between devices, swap(): return lax.ppermute(value, 'pair', [(i, i ^ mask) for i in range(8)])  4.93 us
  transfers between devices with their start and end apart: 8, of which 8 were waited for; matrix products, arithmetic and copies ran while one was open for 4% of the time, Pallas kernels for 0%

profile of v5, /device:TPU:0, one launch (start us, length us, event | category | flops | bytes accessed | tf_op | source)
XLA Modules:
  0.0 119.6 jit_solution(11623701556973728334)
XLA Ops:
  0.0 2.5 %shard_map.73 = bf16[16,16,256]{2,1,0:T(8,128)(2,1)} custom-call(s32[32]{0:T(128)} %blocks_ref.1, bf16[16,32768]{1,0:T(8,128)(2,1)} %amp_ref.1), custom_call_target="tpu_custom_call" | custom-call | bytes 262144 | tf_op jit(solution)/shard_map/pallas_call | solution.py:235
  2.5 16.1 %all_to_all.20.in_ref = bf16[16,16,256]{2,1,0:T(8,128)(2,1)S(1)} all-to-all(bf16[16,16,256]{2,1,0:T(8,128)(2,1)} %shard_map.73), channel_id=1, replica_groups=mesh['blk'=16,'pair'=8] {'blk'}, dimensions={0} | all-to-all | bytes 262144 | tf_op jit(solution)/shard_map/all_to_all | solution.py:238
  18.6 0.8 shard_map.74
  19.4 6.6 %all-to-all-start.1 = ((bf16[64,16,256]{2,1,0:T(8,128)(2,1)}), bf16[64,16,256]{2,1,0:T(8,128)(2,1)S(1)}, u32[]{:S(2)}, u32[]{:S(2)}) async-start(bf16[64,16,256]{2,1,0:T(8,128)(2,1)} %shard_map.74), calls=%async_computation.1 | async-start | bytes 1048576 | tf_op jit(solution)/shard_map/all_to_all | solution.py:243
  26.1 0.7 broadcast_compare_fusion
  26.8 0.7 broadcast_add_fusion
  27.6 10.7 %all-to-all-done.1.mine_ref = bf16[64,16,256]{2,1,0:T(8,128)(2,1)S(1)} async-done(((bf16[64,16,256]{2,1,0:T(8,128)(2,1)}), bf16[64,16,256]{2,1,0:T(8,128)(2,1)S(1)}, u32[]{:S(2)}, u32[]{:S(2)}) %all-to-all-start.1) | async-done | bytes 524320 | tf_op jit(solution)/shard_map/all_to_all | solution.py:243
  38.3 0.1 convolution_convert_fusion
  38.5 0.2 select_reduce_fusion.2
  38.8 1.4 %collective-permute-done.other_ref = bf16[64,16,256]{2,1,0:T(8,128)(2,1)S(1)} collective-permute-done((bf16[64,16,256]{2,1,0:T(8,128)(2,1)S(1)}, bf16[64,16,256]{2,1,0:T(8,128)(2,1)S(1)}, u32[]{:S(2)}, u32[]{:S(2)}) %collective-permute-start) | collective-permute-done | bytes 524320 | tf_op jit(solution)/shard_map/ppermute | solution.py:225
  40.2 7.7 %shard_map.75 = (s32[16,8,5,8,128]{4,3,2,1,0:T(8,128)}, s32[8,128]{1,0:T(8,128)S(1)}) custom-call(s32[80]{0:T(128)S(1)} %sub.19.irrep_ref, bf16[64,16,256]{2,1,0:T(8,128)(2,1)S(1)} %all-to-all-done.1.mine_ref, bf16[64,16,256]{2,1,0:T(8,128)(2,1)S(1)} %collective-permute-done.other_ref, bf16[80,4,128,128]{3,2,1,0:T(8,128)(2,1)} %tiles_ref.1), custom_call_target="tpu_custom_call" | custom-call | flops 1342177280 | bytes 14680064 | tf_op jit(solution)/shard_map/pallas_call | solution.py:197
  48.0 4.7 %all-to-all-start.2 = ((s32[128,40,128]{2,1,0:T(8,128)}), s32[128,40,128]{2,1,0:T(8,128)S(1)}, u32[]{:S(2)}, u32[]{:S(2)}) async-start(s32[128,40,128]{2,1,0:T(8,128)} %bitcast.8), calls=%async_computation.2 | async-start | bytes 5242880 | tf_op jit(solution)/shard_map/all_to_all | solution.py:273
  52.7 0.8 iota_add_fusion
  53.5 0.2 convert_reduce_fusion
  53.7 1.1 collective-permute-done.1
  54.8 0.8 collective-permute-start.2
  55.7 0.2 convert_reduce_fusion.2.own_ref
  55.9 26.1 %collective-permute-done.2 = s32[2,128]{1,0:T(2,128)S(1)} collective-permute-done((s32[2,128]{1,0:T(2,128)S(1)}, s32[2,128]{1,0:T(2,128)S(1)}, u32[]{:S(2)}, u32[]{:S(2)}) %collective-permute-start.2) | collective-permute-done | bytes 1056 | tf_op jit(solution)/shard_map/ppermute | solution.py:225
  81.9 2.8 %collective-permute-start.3 = (s32[4,128]{1,0:T(4,128)S(1)}, s32[4,128]{1,0:T(4,128)S(1)}, u32[]{:S(2)}, u32[]{:S(2)}) collective-permute-start(s32[4,128]{1,0:T(4,128)S(1)} %pad_add_fusion.1), channel_id=1, source_target_pairs={{0,4},{1,5},{2,6},{3,7},{4,0},{5,1},{6,2},{7,3},{8,12},{9,13},{10,... | collective-permute-start | bytes 6152 | tf_op jit(solution)/shard_map/ppermute | solution.py:225
  84.8 2.3 %collective-permute-done.3 = s32[4,128]{1,0:T(4,128)S(1)} collective-permute-done((s32[4,128]{1,0:T(4,128)S(1)}, s32[4,128]{1,0:T(4,128)S(1)}, u32[]{:S(2)}, u32[]{:S(2)}) %collective-permute-start.3) | collective-permute-done | bytes 2080 | tf_op jit(solution)/shard_map/ppermute | solution.py:225
  87.1 1.6 %all-to-all-done.2 = s32[128,40,128]{2,1,0:T(8,128)S(1)} async-done(((s32[128,40,128]{2,1,0:T(8,128)}), s32[128,40,128]{2,1,0:T(8,128)S(1)}, u32[]{:S(2)}, u32[]{:S(2)}) %all-to-all-start.2) | async-done | bytes 2621472 | tf_op jit(solution)/shard_map/all_to_all | solution.py:273
  88.7 2.0 %shard_map.76 = (s32[16,17,8,128]{3,2,1,0:T(8,128)}, s32[16,16,8,128]{3,2,1,0:T(8,128)}) custom-call(s32[256]{0:T(256)S(1)} %select_reduce_fusion.1.from_ref, s32[640,8,128]{2,1,0:T(8,128)S(1)} %bitcast.5, s32[8,128]{1,0:T(8,128)S(1)} %pad_add_fusion.level_ref), custom_call_target="tpu_custom_call" | custom-call | bytes 4194304 | tf_op jit(solution)/shard_map/pallas_call | solution.py:278
  90.7 1.2 %collective-permute-start.4 = (s32[16,16,8,128]{3,2,1,0:T(8,128)}, s32[16,16,8,128]{3,2,1,0:T(8,128)S(1)}, u32[]{:S(2)}, u32[]{:S(2)}) collective-permute-start(s32[16,16,8,128]{3,2,1,0:T(8,128)} %get-tuple-element.11), channel_id=1, source_target_pairs={{0,4},{1,5},{2,6},{3,7},{4,0},{5,1},{6,2},{7,3},{8,12},{9,13},{10,... | collective-permute-start | bytes 3145736 | tf_op jit(solution)/shard_map/ppermute | solution.py:225
  91.9 7.4 %all-to-all-start.3 = ((s32[16,17,8,128]{3,2,1,0:T(8,128)}), s32[16,17,8,128]{3,2,1,0:T(8,128)S(1)}, u32[]{:S(2)}, u32[]{:S(2)}) async-start(s32[16,17,8,128]{3,2,1,0:T(8,128)} %get-tuple-element.12), calls=%async_computation.3 | async-start | bytes 2228224 | tf_op jit(solution)/shard_map/all_to_all | solution.py:284
  99.4 0.7 select_reduce_fusion
  100.1 0.8 dynamic_slice.11
  100.9 0.2 convert_reduce_fusion.1
  101.1 0.1 fusion.1.pick_ref
  101.2 14.9 %all-to-all-done.3 = s32[16,17,8,128]{3,2,1,0:T(8,128)S(1)} async-done(((s32[16,17,8,128]{3,2,1,0:T(8,128)}), s32[16,17,8,128]{3,2,1,0:T(8,128)S(1)}, u32[]{:S(2)}, u32[]{:S(2)}) %all-to-all-start.3) | async-done | bytes 1114144 | tf_op jit(solution)/shard_map/all_to_all | solution.py:284
  116.1 0.9 collective-permute-done.4
  117.0 0.1 broadcast_in_dim.44.sign_ref
  117.1 2.5 %shard_map.77 = bf16[16,32768]{1,0:T(8,128)(2,1)} custom-call(s32[256]{0:T(256)S(1)} %convert_reduce_fusion.2.own_ref, s32[256]{0:T(256)S(1)} %fusion.3.face_ref, s32[256,8,128]{2,1,0:T(8,128)S(1)} %bitcast.7, s32[272,8,128]{2,1,0:T(8,128)S(1)} %bitcast.6, bf16[512,128]{1,0:T(8,128)(2,1)S(1)} %fusion.1.pick_ref, f32[512,128]{1,0:T(8,128)S(1)} %broadcast_in_dim.44.sign_ref), custom_call_target="tpu_custom_call" | custom-call | bytes 4194304 | tf_op jit(solution)/shard_map/pallas_call | solution.py:219
  (19 shorter events, 0.5 us)
Async XLA Ops:
  19.4 18.9 %all-to-all-start.1 = ((bf16[64,16,256]{2,1,0:T(8,128)(2,1)}), bf16[64,16,256]{2,1,0:T(8,128)(2,1)S(1)}, u32[]{:S(2)}, u32[]{:S(2)}) async-start(bf16[64,16,256]{2,1,0:T(8,128)(2,1)} %shard_map.74), calls=%async_computation.1 | async-start | bytes 1048576 | tf_op jit(solution)/shard_map/all_to_all | solution.py:243
  38.3 1.9 %collective-permute-start = (bf16[64,16,256]{2,1,0:T(8,128)(2,1)S(1)}, bf16[64,16,256]{2,1,0:T(8,128)(2,1)S(1)}, u32[]{:S(2)}, u32[]{:S(2)}) collective-permute-start(bf16[64,16,256]{2,1,0:T(8,128)(2,1)S(1)} %all-to-all-done.1.mine_ref), channel_id=1, source_target_pairs={{0,1},{1,0},{2,3},{3,2},{4,5},{5,4},{6,7},{7,6},{8,9},{9,8},{10,11... | collective-permute-start | bytes 1572872 | tf_op jit(solution)/shard_map/ppermute | solution.py:225
  48.0 4.7 %copy-start = (s32[4096]{0:T(1024)S(1)}, s32[4096]{0:T(1024)}, u32[]{:S(2)}) copy-start(s32[4096]{0:T(1024)} %param.11) | copy-start | bytes 49156
  48.0 40.7 %all-to-all-start.2 = ((s32[128,40,128]{2,1,0:T(8,128)}), s32[128,40,128]{2,1,0:T(8,128)S(1)}, u32[]{:S(2)}, u32[]{:S(2)}) async-start(s32[128,40,128]{2,1,0:T(8,128)} %bitcast.8), calls=%async_computation.2 | async-start | bytes 5242880 | tf_op jit(solution)/shard_map/all_to_all | solution.py:273
  53.6 1.2 %collective-permute-start.1 = (s32[1,128]{1,0:T(1,128)S(1)}, s32[1,128]{1,0:T(1,128)S(1)}, u32[]{:S(2)}, u32[]{:S(2)}) collective-permute-start(s32[1,128]{1,0:T(1,128)S(1)} %slice.3), channel_id=1, source_target_pairs={{0,1},{1,0},{2,3},{3,2},{4,5},{5,4},{6,7},{7,6},{8,9},{9,8},{10,11... | collective-permute-start | bytes 1544 | tf_op jit(solution)/shard_map/ppermute | solution.py:225
  54.8 27.1 %collective-permute-start.2 = (s32[2,128]{1,0:T(2,128)S(1)}, s32[2,128]{1,0:T(2,128)S(1)}, u32[]{:S(2)}, u32[]{:S(2)}) collective-permute-start(s32[2,128]{1,0:T(2,128)S(1)} %pad_add_fusion.3), channel_id=1, source_target_pairs={{0,2},{1,3},{2,0},{3,1},{4,6},{5,7},{6,4},{7,5},{8,10},{9,11},{10,... | collective-permute-start | bytes 3080 | tf_op jit(solution)/shard_map/ppermute | solution.py:225
  81.9 5.2 %collective-permute-start.3 = (s32[4,128]{1,0:T(4,128)S(1)}, s32[4,128]{1,0:T(4,128)S(1)}, u32[]{:S(2)}, u32[]{:S(2)}) collective-permute-start(s32[4,128]{1,0:T(4,128)S(1)} %pad_add_fusion.1), channel_id=1, source_target_pairs={{0,4},{1,5},{2,6},{3,7},{4,0},{5,1},{6,2},{7,3},{8,12},{9,13},{10,... | collective-permute-start | bytes 6152 | tf_op jit(solution)/shard_map/ppermute | solution.py:225
  90.7 26.3 %collective-permute-start.4 = (s32[16,16,8,128]{3,2,1,0:T(8,128)}, s32[16,16,8,128]{3,2,1,0:T(8,128)S(1)}, u32[]{:S(2)}, u32[]{:S(2)}) collective-permute-start(s32[16,16,8,128]{3,2,1,0:T(8,128)} %get-tuple-element.11), channel_id=1, source_target_pairs={{0,4},{1,5},{2,6},{3,7},{4,0},{5,1},{6,2},{7,3},{8,12},{9,13},{10,... | collective-permute-start | bytes 3145736 | tf_op jit(solution)/shard_map/ppermute | solution.py:225
  91.9 24.1 %all-to-all-start.3 = ((s32[16,17,8,128]{3,2,1,0:T(8,128)}), s32[16,17,8,128]{3,2,1,0:T(8,128)S(1)}, u32[]{:S(2)}, u32[]{:S(2)}) async-start(s32[16,17,8,128]{3,2,1,0:T(8,128)} %get-tuple-element.12), calls=%async_computation.3 | async-start | bytes 2228224 | tf_op jit(solution)/shard_map/all_to_all | solution.py:284

commit v6 on v5

--- a/solution.py
+++ b/solution.py
@@ -28,33 +28,15 @@
     )
 
 
-def extract_body(blocks_ref, amp_ref, out_ref, sems):
+def extract_body(blocks_ref, amp_ref, out_ref):
     blk = lax.axis_index("blk")
-
-    def move(n):
-        start = pl.multiple_of((blocks_ref[n] & 255) * 128, 128)
-        return pltpu.make_async_copy(
-            amp_ref.at[:, pl.ds(start, 128)],
-            out_ref.at[n // 2, :, pl.ds((n % 2) * 128, 128)],
-            sems.at[n],
-        )
-
-    for n in range(32):
-        held = (blocks_ref[n] >> 8) == blk
-
-        @pl.when(held)
-        def _():
-            move(n).start()
-
-        @pl.when(jnp.logical_not(held))
-        def _():
-            out_ref[n // 2, :, (n % 2) * 128 : (n % 2) * 128 + 128] = jnp.zeros((16, 128), jnp.bfloat16)
-
-    for n in range(32):
-
-        @pl.when((blocks_ref[n] >> 8) == blk)
-        def _():
-            move(n).wait()
+    for c in range(16):
+        tiles = []
+        for n in (2 * c, 2 * c + 1):
+            block = blocks_ref[n]
+            tile = amp_ref[:, pl.ds(pl.multiple_of((block & 255) * 128, 128), 128)]
+            tiles.append(jnp.where((block >> 8) == blk, tile, jnp.zeros_like(tile)))
+        out_ref[c] = jnp.concatenate(tiles, axis=1)
 
 
 def merge_body(in_ref, out_ref):
@@ -134,11 +116,11 @@
 
 def select_body(from_ref, in_ref, level_ref, out_ref, words_ref, picked, sems, word_sems):
     def store(c):
-        span = pl.ds(c * 4, 4)
+        span = pl.ds(c * 2, 2)
         return pltpu.make_async_copy(picked.at[span], out_ref.at[span], sems.at[c])
 
     def store_words(c):
-        span = pl.ds(c * 4, 4)
+        span = pl.ds(c * 2, 2)
         return pltpu.make_async_copy(picked.at[span, pl.ds(0, 16)], words_ref.at[span], word_sems.at[c])
 
     def one(t, carry):
@@ -147,11 +129,11 @@
         picked[t, 16] = level_ref[...]
         return carry
 
-    for c in range(4):
-        lax.fori_loop(c * 4, c * 4 + 4, one, 0)
+    for c in range(8):
+        lax.fori_loop(c * 2, c * 2 + 2, one, 0)
         store_words(c).start()
         store(c).start()
-    for c in range(4):
+    for c in range(8):
         store_words(c).wait()
         store(c).wait()
 
@@ -161,10 +143,12 @@
     pick = pick_ref[...]
     upper = jnp.dot(pick, (levels >> 5).astype(jnp.bfloat16), preferred_element_type=jnp.float32)
     lower = jnp.dot(pick, (levels & 31).astype(jnp.bfloat16), preferred_element_type=jnp.float32)
-    scale[...] = jnp.exp((upper * 32.0 + lower) * (LN2 / STEPS)) * (1.0 / TOP) * sign_ref[...]
+    value = jnp.exp((upper * 32.0 + lower) * (LN2 / STEPS)) * (1.0 / TOP)
+    scale[:256] = value[:256]
+    scale[256:] = value[256:] * sign_ref[...]
 
     def store(c):
-        span = pl.ds(c * 8192, 8192)
+        span = pl.ds(c * 4096, 4096)
         return pltpu.make_async_copy(result.at[:, span], out_ref.at[:, span], sems.at[c])
 
     def parts(word):
@@ -184,10 +168,10 @@
             result[:, pl.ds(pl.multiple_of((step * 8 + i) * 128, 128), 128)] = values[i]
         return carry
 
-    for c in range(4):
-        lax.fori_loop(c * 8, c * 8 + 8, one, 0)
+    for c in range(8):
+        lax.fori_loop(c * 4, c * 4 + 4, one, 0)
         store(c).start()
-    for c in range(4):
+    for c in range(8):
         store(c).wait()
 
 
@@ -213,7 +197,7 @@
     scratch = [
         pltpu.VMEM((512, 128), jnp.float32),
         pltpu.VMEM((16, 32768), jnp.bfloat16),
-        pltpu.SemaphoreType.DMA((4,)),
+        pltpu.SemaphoreType.DMA((8,)),
     ]
     out = jax.ShapeDtypeStruct((16, 32768), jnp.bfloat16)
     return call(combine_body, [SMEM] * 2 + [VMEM] * 4, HBM, out, scratch, 16 * MIB, 0, 4 << 20)(
@@ -233,7 +217,7 @@
     dma = pltpu.SemaphoreType.DMA
 
     parts = call(
-        extract_body, [SMEM, HBM], VMEM, jax.ShapeDtypeStruct((16, 16, 256), jnp.bfloat16), [dma((32,))], 60 * MIB, 0, 1 << 18
+        extract_body, [SMEM, VMEM], VMEM, jax.ShapeDtypeStruct((16, 16, 256), jnp.bfloat16), [], 4 * MIB, 0, 1 << 20
     )(slab_blocks, amplitudes)
     parts = lax.all_to_all(parts, "blk", split_axis=0, concat_axis=0, tiled=True)
     copies = call(
@@ -266,8 +250,7 @@
     back = back + back // 16
     rows = jnp.concatenate([my_owner ^ pair, face_owner ^ pair])
     pick = (rows[:, None] == jnp.arange(128, dtype=int32)[None, :]).astype(jnp.bfloat16)
-    signs = jnp.concatenate([jnp.ones_like(my_sign), my_sign]).astype(jnp.float32)
-    signs = jnp.broadcast_to(signs[:, None], (512, 128))
+    signs = jnp.broadcast_to(my_sign.astype(jnp.float32)[:, None], (256, 128))
 
     coded, level = call_product(slot_irrep, mine, other, integrals)
     arrived = lax.all_to_all(coded.reshape(128, 40, 128), BOTH, split_axis=0, concat_axis=0, tiled=True)
@@ -278,7 +261,7 @@
     outgoing, words = call(
         select_body, [SMEM, VMEM, VMEM], [HBM, HBM],
         [pltpu.HBM((16, 17, 8, 128), int32), pltpu.HBM((16, 16, 8, 128), int32)],
-        [pltpu.VMEM((16, 17, 8, 128), int32), dma((4,)), dma((4,))], 16 * MIB, 0, 4 << 20,
+        [pltpu.VMEM((16, 17, 8, 128), int32), dma((8,)), dma((8,))], 16 * MIB, 0, 4 << 20,
     )(leaving, arrived, levels)
     own = swap(words, 4).reshape(256, 8, 128)
     incoming = lax.all_to_all(outgoing, "blk", split_axis=0, concat_axis=0, tiled=True).reshape(272, 8, 128)

time: 120 us -> 120 us (level)
  Pallas kernels: 15.6 us -> 13.7 us
    unnamed x2 -> x6, local copies, waits for them, and re-layouts: 0.01 us -> 1.89 us
    pallas_call x1, Pallas kernels: 2.48 us -> 0.63 us  [local(): call(extract_body, [SMEM, VMEM], VMEM, jax.ShapeDtypeStruct((16, 16, 256)...]
where the time goes in v6:
time: 120 us; the launch traced here: 119 us
  waiting for transfers between devices  58.9 us (49%)
  starting transfers between devices  23.7 us (20%)
  blocking collectives  15.9 us (13%)
  Pallas kernels  13.7 us (11%)
  other arithmetic  4.71 us (4%)
  local copies, waits for them, and re-layouts  2.17 us (2%)
    ppermute x5, waiting for transfers between devices, swap(): return lax.ppermute(value, 'pair', [(i, i ^ mask) for i in range(8)])  31.7 us
    all_to_all x1, blocking collectives, local(): lax.all_to_all(parts, 'blk', split_axis=0, concat_axis=0, tiled=True)  15.9 us
    all_to_all x1, waiting for transfers between devices, local(): lax.all_to_all(outgoing, 'blk', split_axis=0, concat_axis=0, tiled=True)  14.9 us
    all_to_all x1, waiting for transfers between devices, local(): lax.all_to_all(copies, BOTH, split_axis=0, concat_axis=0, tiled=True, axi...  10.7 us
    pallas_call x1, Pallas kernels, call_product(): call(product_body, [SMEM, VMEM, VMEM, HBM], [HBM, VMEM], [pltpu.HBM((16,...  7.73 us
    all_to_all x1, starting transfers between devices, local(): lax.all_to_all(outgoing, 'blk', split_axis=0, concat_axis=0, tiled=True)  7.43 us
    all_to_all x1, starting transfers between devices, local(): lax.all_to_all(copies, BOTH, split_axis=0, concat_axis=0, tiled=True, axi...  6.64 us
    ppermute x5, starting transfers between devices, swap(): return lax.ppermute(value, 'pair', [(i, i ^ mask) for i in range(8)])  4.93 us
  transfers between devices with their start and end apart: 8, of which 8 were waited for; matrix products, arithmetic and copies ran while one was open for 4% of the time, Pallas kernels for 0%

profile of v6, /device:TPU:0, one launch (start us, length us, event | category | flops | bytes accessed | tf_op | source)
XLA Modules:
  0.0 119.4 jit_solution(4714692208605651756)
XLA Ops:
  0.0 1.2 %copy-done = bf16[16,32768]{1,0:T(8,128)(2,1)S(1)} copy-done((bf16[16,32768]{1,0:T(8,128)(2,1)S(1)}, bf16[16,32768]{1,0:T(8,128)(2,1)}, u32[]{:S(2)}) %copy-start) | copy-done | bytes 1048600
  1.2 0.7 copy-done.1
  1.9 0.6 shard_map.73
  2.5 15.9 %all_to_all.20.in_ref = bf16[16,16,256]{2,1,0:T(8,128)(2,1)S(1)} all-to-all(bf16[16,16,256]{2,1,0:T(8,128)(2,1)S(1)} %shard_map.73), channel_id=1, replica_groups=mesh['blk'=16,'pair'=8] {'blk'}, dimensions={0} | all-to-all | bytes 262144 | tf_op jit(solution)/shard_map/all_to_all | solution.py:222
  18.4 0.8 shard_map.74
  19.3 6.6 %all-to-all-start.1 = ((bf16[64,16,256]{2,1,0:T(8,128)(2,1)}), bf16[64,16,256]{2,1,0:T(8,128)(2,1)S(1)}, u32[]{:S(2)}, u32[]{:S(2)}) async-start(bf16[64,16,256]{2,1,0:T(8,128)(2,1)} %shard_map.74), calls=%async_computation.1 | async-start | bytes 1048576 | tf_op jit(solution)/shard_map/all_to_all | solution.py:227
  25.9 0.7 broadcast_compare_fusion
  26.7 0.7 broadcast_add_fusion
  27.4 10.7 %all-to-all-done.1.mine_ref = bf16[64,16,256]{2,1,0:T(8,128)(2,1)S(1)} async-done(((bf16[64,16,256]{2,1,0:T(8,128)(2,1)}), bf16[64,16,256]{2,1,0:T(8,128)(2,1)S(1)}, u32[]{:S(2)}, u32[]{:S(2)}) %all-to-all-start.1) | async-done | bytes 524320 | tf_op jit(solution)/shard_map/all_to_all | solution.py:227
  38.2 0.1 convolution_convert_fusion
  38.3 0.2 select_reduce_fusion.2
  38.7 1.4 %collective-permute-done.other_ref = bf16[64,16,256]{2,1,0:T(8,128)(2,1)S(1)} collective-permute-done((bf16[64,16,256]{2,1,0:T(8,128)(2,1)S(1)}, bf16[64,16,256]{2,1,0:T(8,128)(2,1)S(1)}, u32[]{:S(2)}, u32[]{:S(2)}) %collective-permute-start) | collective-permute-done | bytes 524320 | tf_op jit(solution)/shard_map/ppermute | solution.py:209
  40.1 7.7 %shard_map.75 = (s32[16,8,5,8,128]{4,3,2,1,0:T(8,128)}, s32[8,128]{1,0:T(8,128)S(1)}) custom-call(s32[80]{0:T(128)S(1)} %sub.19.irrep_ref, bf16[64,16,256]{2,1,0:T(8,128)(2,1)S(1)} %all-to-all-done.1.mine_ref, bf16[64,16,256]{2,1,0:T(8,128)(2,1)S(1)} %collective-permute-done.other_ref, bf16[80,4,128,128]{3,2,1,0:T(8,128)(2,1)} %tiles_ref.1), custom_call_target="tpu_custom_call" | custom-call | flops 1342177280 | bytes 14680064 | tf_op jit(solution)/shard_map/pallas_call | solution.py:181
  47.8 4.7 %all-to-all-start.2 = ((s32[128,40,128]{2,1,0:T(8,128)}), s32[128,40,128]{2,1,0:T(8,128)S(1)}, u32[]{:S(2)}, u32[]{:S(2)}) async-start(s32[128,40,128]{2,1,0:T(8,128)} %bitcast.8), calls=%async_computation.2 | async-start | bytes 5242880 | tf_op jit(solution)/shard_map/all_to_all | solution.py:256
  52.5 0.8 iota_add_fusion
  53.3 0.2 convert_reduce_fusion
  53.6 1.1 collective-permute-done.1
  54.7 0.8 collective-permute-start.2
  55.5 0.2 convert_reduce_fusion.2.own_ref
  55.7 26.1 %collective-permute-done.2 = s32[2,128]{1,0:T(2,128)S(1)} collective-permute-done((s32[2,128]{1,0:T(2,128)S(1)}, s32[2,128]{1,0:T(2,128)S(1)}, u32[]{:S(2)}, u32[]{:S(2)}) %collective-permute-start.2) | collective-permute-done | bytes 1056 | tf_op jit(solution)/shard_map/ppermute | solution.py:209
  81.8 2.8 %collective-permute-start.3 = (s32[4,128]{1,0:T(4,128)S(1)}, s32[4,128]{1,0:T(4,128)S(1)}, u32[]{:S(2)}, u32[]{:S(2)}) collective-permute-start(s32[4,128]{1,0:T(4,128)S(1)} %pad_add_fusion.1), channel_id=1, source_target_pairs={{0,4},{1,5},{2,6},{3,7},{4,0},{5,1},{6,2},{7,3},{8,12},{9,13},{10,... | collective-permute-start | bytes 6152 | tf_op jit(solution)/shard_map/ppermute | solution.py:209
  84.7 2.3 %collective-permute-done.3 = s32[4,128]{1,0:T(4,128)S(1)} collective-permute-done((s32[4,128]{1,0:T(4,128)S(1)}, s32[4,128]{1,0:T(4,128)S(1)}, u32[]{:S(2)}, u32[]{:S(2)}) %collective-permute-start.3) | collective-permute-done | bytes 2080 | tf_op jit(solution)/shard_map/ppermute | solution.py:209
  87.0 1.6 %all-to-all-done.2 = s32[128,40,128]{2,1,0:T(8,128)S(1)} async-done(((s32[128,40,128]{2,1,0:T(8,128)}), s32[128,40,128]{2,1,0:T(8,128)S(1)}, u32[]{:S(2)}, u32[]{:S(2)}) %all-to-all-start.2) | async-done | bytes 2621472 | tf_op jit(solution)/shard_map/all_to_all | solution.py:256
  88.5 2.1 %shard_map.76 = (s32[16,17,8,128]{3,2,1,0:T(8,128)}, s32[16,16,8,128]{3,2,1,0:T(8,128)}) custom-call(s32[256]{0:T(256)S(1)} %select_reduce_fusion.1.from_ref, s32[640,8,128]{2,1,0:T(8,128)S(1)} %bitcast.5, s32[8,128]{1,0:T(8,128)S(1)} %pad_add_fusion.level_ref), custom_call_target="tpu_custom_call" | custom-call | bytes 4194304 | tf_op jit(solution)/shard_map/pallas_call | solution.py:261
  90.6 1.2 %collective-permute-start.4 = (s32[16,16,8,128]{3,2,1,0:T(8,128)}, s32[16,16,8,128]{3,2,1,0:T(8,128)S(1)}, u32[]{:S(2)}, u32[]{:S(2)}) collective-permute-start(s32[16,16,8,128]{3,2,1,0:T(8,128)} %get-tuple-element.11), channel_id=1, source_target_pairs={{0,4},{1,5},{2,6},{3,7},{4,0},{5,1},{6,2},{7,3},{8,12},{9,13},{10,... | collective-permute-start | bytes 3145736 | tf_op jit(solution)/shard_map/ppermute | solution.py:209
  91.8 7.4 %all-to-all-start.3 = ((s32[16,17,8,128]{3,2,1,0:T(8,128)}), s32[16,17,8,128]{3,2,1,0:T(8,128)S(1)}, u32[]{:S(2)}, u32[]{:S(2)}) async-start(s32[16,17,8,128]{3,2,1,0:T(8,128)} %get-tuple-element.12), calls=%async_computation.3 | async-start | bytes 2228224 | tf_op jit(solution)/shard_map/all_to_all | solution.py:267
  99.3 0.7 select_reduce_fusion
  99.9 0.8 dynamic-slice_convert_fusion
  100.7 0.2 convert_reduce_fusion.1
  101.1 14.9 %all-to-all-done.3 = s32[16,17,8,128]{3,2,1,0:T(8,128)S(1)} async-done(((s32[16,17,8,128]{3,2,1,0:T(8,128)}), s32[16,17,8,128]{3,2,1,0:T(8,128)S(1)}, u32[]{:S(2)}, u32[]{:S(2)}) %all-to-all-start.3) | async-done | bytes 1114144 | tf_op jit(solution)/shard_map/all_to_all | solution.py:267
  116.0 0.9 collective-permute-done.4
  117.0 2.5 %shard_map.77 = bf16[16,32768]{1,0:T(8,128)(2,1)} custom-call(s32[256]{0:T(256)S(1)} %convert_reduce_fusion.2.own_ref, s32[256]{0:T(256)S(1)} %fusion.3.face_ref, s32[256,8,128]{2,1,0:T(8,128)S(1)} %bitcast.7, s32[272,8,128]{2,1,0:T(8,128)S(1)} %bitcast.6, bf16[512,128]{1,0:T(8,128)(2,1)S(1)} %fusion.1.pick_ref, f32[256,128]{1,0:T(8,128)S(1)} %broadcast_in_dim.44.sign_ref), custom_call_target="tpu_custom_call" | custom-call | bytes 4194304 | tf_op jit(solution)/shard_map/pallas_call | solution.py:203
  (22 shorter events, 0.7 us)
Async XLA Ops:
  0.0 1.2 %copy-start = (bf16[16,32768]{1,0:T(8,128)(2,1)S(1)}, bf16[16,32768]{1,0:T(8,128)(2,1)}, u32[]{:S(2)}) copy-start(bf16[16,32768]{1,0:T(8,128)(2,1)} %amp_ref.1) | copy-start | bytes 3145732
  1.2 0.7 copy-start.1
  19.3 18.9 %all-to-all-start.1 = ((bf16[64,16,256]{2,1,0:T(8,128)(2,1)}), bf16[64,16,256]{2,1,0:T(8,128)(2,1)S(1)}, u32[]{:S(2)}, u32[]{:S(2)}) async-start(bf16[64,16,256]{2,1,0:T(8,128)(2,1)} %shard_map.74), calls=%async_computation.1 | async-start | bytes 1048576 | tf_op jit(solution)/shard_map/all_to_all | solution.py:227
  38.2 1.9 %collective-permute-start = (bf16[64,16,256]{2,1,0:T(8,128)(2,1)S(1)}, bf16[64,16,256]{2,1,0:T(8,128)(2,1)S(1)}, u32[]{:S(2)}, u32[]{:S(2)}) collective-permute-start(bf16[64,16,256]{2,1,0:T(8,128)(2,1)S(1)} %all-to-all-done.1.mine_ref), channel_id=1, source_target_pairs={{0,1},{1,0},{2,3},{3,2},{4,5},{5,4},{6,7},{7,6},{8,9},{9,8},{10,11... | collective-permute-start | bytes 1572872 | tf_op jit(solution)/shard_map/ppermute | solution.py:209
  47.8 4.7 %copy-start.2 = (s32[4096]{0:T(1024)S(1)}, s32[4096]{0:T(1024)}, u32[]{:S(2)}) copy-start(s32[4096]{0:T(1024)} %param.11) | copy-start | bytes 49156
  47.8 40.7 %all-to-all-start.2 = ((s32[128,40,128]{2,1,0:T(8,128)}), s32[128,40,128]{2,1,0:T(8,128)S(1)}, u32[]{:S(2)}, u32[]{:S(2)}) async-start(s32[128,40,128]{2,1,0:T(8,128)} %bitcast.8), calls=%async_computation.2 | async-start | bytes 5242880 | tf_op jit(solution)/shard_map/all_to_all | solution.py:256
  53.5 1.2 %collective-permute-start.1 = (s32[1,128]{1,0:T(1,128)S(1)}, s32[1,128]{1,0:T(1,128)S(1)}, u32[]{:S(2)}, u32[]{:S(2)}) collective-permute-start(s32[1,128]{1,0:T(1,128)S(1)} %slice.3), channel_id=1, source_target_pairs={{0,1},{1,0},{2,3},{3,2},{4,5},{5,4},{6,7},{7,6},{8,9},{9,8},{10,11... | collective-permute-start | bytes 1544 | tf_op jit(solution)/shard_map/ppermute | solution.py:209
  54.7 27.1 %collective-permute-start.2 = (s32[2,128]{1,0:T(2,128)S(1)}, s32[2,128]{1,0:T(2,128)S(1)}, u32[]{:S(2)}, u32[]{:S(2)}) collective-permute-start(s32[2,128]{1,0:T(2,128)S(1)} %pad_add_fusion.3), channel_id=1, source_target_pairs={{0,2},{1,3},{2,0},{3,1},{4,6},{5,7},{6,4},{7,5},{8,10},{9,11},{10,... | collective-permute-start | bytes 3080 | tf_op jit(solution)/shard_map/ppermute | solution.py:209
  81.8 5.2 %collective-permute-start.3 = (s32[4,128]{1,0:T(4,128)S(1)}, s32[4,128]{1,0:T(4,128)S(1)}, u32[]{:S(2)}, u32[]{:S(2)}) collective-permute-start(s32[4,128]{1,0:T(4,128)S(1)} %pad_add_fusion.1), channel_id=1, source_target_pairs={{0,4},{1,5},{2,6},{3,7},{4,0},{5,1},{6,2},{7,3},{8,12},{9,13},{10,... | collective-permute-start | bytes 6152 | tf_op jit(solution)/shard_map/ppermute | solution.py:209
  90.6 26.3 %collective-permute-start.4 = (s32[16,16,8,128]{3,2,1,0:T(8,128)}, s32[16,16,8,128]{3,2,1,0:T(8,128)S(1)}, u32[]{:S(2)}, u32[]{:S(2)}) collective-permute-start(s32[16,16,8,128]{3,2,1,0:T(8,128)} %get-tuple-element.11), channel_id=1, source_target_pairs={{0,4},{1,5},{2,6},{3,7},{4,0},{5,1},{6,2},{7,3},{8,12},{9,13},{10,... | collective-permute-start | bytes 3145736 | tf_op jit(solution)/shard_map/ppermute | solution.py:209
  91.8 24.1 %all-to-all-start.3 = ((s32[16,17,8,128]{3,2,1,0:T(8,128)}), s32[16,17,8,128]{3,2,1,0:T(8,128)S(1)}, u32[]{:S(2)}, u32[]{:S(2)}) async-start(s32[16,17,8,128]{3,2,1,0:T(8,128)} %get-tuple-element.12), calls=%async_computation.3 | async-start | bytes 2228224 | tf_op jit(solution)/shard_map/all_to_all | solution.py:267

commit v7 on v6

--- a/solution.py
+++ b/solution.py
@@ -217,7 +217,7 @@
     dma = pltpu.SemaphoreType.DMA
 
     parts = call(
-        extract_body, [SMEM, VMEM], VMEM, jax.ShapeDtypeStruct((16, 16, 256), jnp.bfloat16), [], 4 * MIB, 0, 1 << 20
+        extract_body, [SMEM, VMEM], VMEM, jax.ShapeDtypeStruct((16, 16, 256), jnp.bfloat16), [], 53 * MIB, 0, 1 << 20
     )(slab_blocks, amplitudes)
     parts = lax.all_to_all(parts, "blk", split_axis=0, concat_axis=0, tiled=True)
     copies = call(

time: 120 us -> 120 us (level)
  local copies, waits for them, and re-layouts: 2.17 us -> 0.95 us
    unnamed x6 -> x4, local copies, waits for them, and re-layouts: 1.89 us -> 0.66 us
where the time goes in v7:
time: 120 us; the launch traced here: 119 us
  waiting for transfers between devices  58.9 us (49%)
  starting transfers between devices  23.7 us (20%)
  blocking collectives  15.9 us (13%)
  Pallas kernels  14.4 us (12%)
  other arithmetic  4.71 us (4%)
    ppermute x5, waiting for transfers between devices, swap(): return lax.ppermute(value, 'pair', [(i, i ^ mask) for i in range(8)])  31.7 us
    all_to_all x1, blocking collectives, local(): lax.all_to_all(parts, 'blk', split_axis=0, concat_axis=0, tiled=True)  15.9 us
    all_to_all x1, waiting for transfers between devices, local(): lax.all_to_all(outgoing, 'blk', split_axis=0, concat_axis=0, tiled=True)  14.9 us
    all_to_all x1, waiting for transfers between devices, local(): lax.all_to_all(copies, BOTH, split_axis=0, concat_axis=0, tiled=True, axi...  10.7 us
    pallas_call x1, Pallas kernels, call_product(): call(product_body, [SMEM, VMEM, VMEM, HBM], [HBM, VMEM], [pltpu.HBM((16,...  7.73 us
    all_to_all x1, starting transfers between devices, local(): lax.all_to_all(outgoing, 'blk', split_axis=0, concat_axis=0, tiled=True)  7.43 us
    all_to_all x1, starting transfers between devices, local(): lax.all_to_all(copies, BOTH, split_axis=0, concat_axis=0, tiled=True, axi...  6.64 us
    ppermute x5, starting transfers between devices, swap(): return lax.ppermute(value, 'pair', [(i, i ^ mask) for i in range(8)])  4.93 us
  transfers between devices with their start and end apart: 8, of which 8 were waited for; matrix products, arithmetic and copies ran while one was open for 4% of the time, Pallas kernels for 0%

profile of v7, /device:TPU:0, one launch (start us, length us, event | category | flops | bytes accessed | tf_op | source)
XLA Modules:
  0.0 118.9 jit_solution(3903286224251895383)
XLA Ops:
  0.0 0.7 copy-done
  0.7 1.3 %shard_map.73 = bf16[16,16,256]{2,1,0:T(8,128)(2,1)S(1)} custom-call(s32[32]{0:T(128)S(1)} %copy-done, bf16[16,32768]{1,0:T(8,128)(2,1)} %amp_ref.1), custom_call_target="tpu_custom_call" | custom-call | bytes 1048576 | tf_op jit(solution)/shard_map/pallas_call | solution.py:219
  2.0 15.9 %all_to_all.20.in_ref = bf16[16,16,256]{2,1,0:T(8,128)(2,1)S(1)} all-to-all(bf16[16,16,256]{2,1,0:T(8,128)(2,1)S(1)} %shard_map.73), channel_id=1, replica_groups=mesh['blk'=16,'pair'=8] {'blk'}, dimensions={0} | all-to-all | bytes 262144 | tf_op jit(solution)/shard_map/all_to_all | solution.py:222
  17.9 0.8 shard_map.74
  18.8 6.6 %all-to-all-start.1 = ((bf16[64,16,256]{2,1,0:T(8,128)(2,1)}), bf16[64,16,256]{2,1,0:T(8,128)(2,1)S(1)}, u32[]{:S(2)}, u32[]{:S(2)}) async-start(bf16[64,16,256]{2,1,0:T(8,128)(2,1)} %shard_map.74), calls=%async_computation.1 | async-start | bytes 1048576 | tf_op jit(solution)/shard_map/all_to_all | solution.py:227
  25.4 0.7 broadcast_compare_fusion
  26.2 0.7 broadcast_add_fusion
  26.9 10.7 %all-to-all-done.1.mine_ref = bf16[64,16,256]{2,1,0:T(8,128)(2,1)S(1)} async-done(((bf16[64,16,256]{2,1,0:T(8,128)(2,1)}), bf16[64,16,256]{2,1,0:T(8,128)(2,1)S(1)}, u32[]{:S(2)}, u32[]{:S(2)}) %all-to-all-start.1) | async-done | bytes 524320 | tf_op jit(solution)/shard_map/all_to_all | solution.py:227
  37.6 0.1 convolution_convert_fusion
  37.8 0.2 select_reduce_fusion.2
  38.2 1.4 %collective-permute-done.other_ref = bf16[64,16,256]{2,1,0:T(8,128)(2,1)S(1)} collective-permute-done((bf16[64,16,256]{2,1,0:T(8,128)(2,1)S(1)}, bf16[64,16,256]{2,1,0:T(8,128)(2,1)S(1)}, u32[]{:S(2)}, u32[]{:S(2)}) %collective-permute-start) | collective-permute-done | bytes 524320 | tf_op jit(solution)/shard_map/ppermute | solution.py:209
  39.5 7.7 %shard_map.75 = (s32[16,8,5,8,128]{4,3,2,1,0:T(8,128)}, s32[8,128]{1,0:T(8,128)S(1)}) custom-call(s32[80]{0:T(128)S(1)} %sub.19.irrep_ref, bf16[64,16,256]{2,1,0:T(8,128)(2,1)S(1)} %all-to-all-done.1.mine_ref, bf16[64,16,256]{2,1,0:T(8,128)(2,1)S(1)} %collective-permute-done.other_ref, bf16[80,4,128,128]{3,2,1,0:T(8,128)(2,1)} %tiles_ref.1), custom_call_target="tpu_custom_call" | custom-call | flops 1342177280 | bytes 14680064 | tf_op jit(solution)/shard_map/pallas_call | solution.py:181
  47.3 4.7 %all-to-all-start.2 = ((s32[128,40,128]{2,1,0:T(8,128)}), s32[128,40,128]{2,1,0:T(8,128)S(1)}, u32[]{:S(2)}, u32[]{:S(2)}) async-start(s32[128,40,128]{2,1,0:T(8,128)} %bitcast.8), calls=%async_computation.2 | async-start | bytes 5242880 | tf_op jit(solution)/shard_map/all_to_all | solution.py:256
  52.0 0.8 iota_add_fusion
  52.8 0.2 convert_reduce_fusion
  53.1 1.1 collective-permute-done.1
  54.2 0.8 collective-permute-start.2
  55.0 0.2 convert_reduce_fusion.2.own_ref
  55.2 26.1 %collective-permute-done.2 = s32[2,128]{1,0:T(2,128)S(1)} collective-permute-done((s32[2,128]{1,0:T(2,128)S(1)}, s32[2,128]{1,0:T(2,128)S(1)}, u32[]{:S(2)}, u32[]{:S(2)}) %collective-permute-start.2) | collective-permute-done | bytes 1056 | tf_op jit(solution)/shard_map/ppermute | solution.py:209
  81.3 2.8 %collective-permute-start.3 = (s32[4,128]{1,0:T(4,128)S(1)}, s32[4,128]{1,0:T(4,128)S(1)}, u32[]{:S(2)}, u32[]{:S(2)}) collective-permute-start(s32[4,128]{1,0:T(4,128)S(1)} %pad_add_fusion.1), channel_id=1, source_target_pairs={{0,4},{1,5},{2,6},{3,7},{4,0},{5,1},{6,2},{7,3},{8,12},{9,13},{10,... | collective-permute-start | bytes 6152 | tf_op jit(solution)/shard_map/ppermute | solution.py:209
  84.2 2.3 %collective-permute-done.3 = s32[4,128]{1,0:T(4,128)S(1)} collective-permute-done((s32[4,128]{1,0:T(4,128)S(1)}, s32[4,128]{1,0:T(4,128)S(1)}, u32[]{:S(2)}, u32[]{:S(2)}) %collective-permute-start.3) | collective-permute-done | bytes 2080 | tf_op jit(solution)/shard_map/ppermute | solution.py:209
  86.4 1.6 %all-to-all-done.2 = s32[128,40,128]{2,1,0:T(8,128)S(1)} async-done(((s32[128,40,128]{2,1,0:T(8,128)}), s32[128,40,128]{2,1,0:T(8,128)S(1)}, u32[]{:S(2)}, u32[]{:S(2)}) %all-to-all-start.2) | async-done | bytes 2621472 | tf_op jit(solution)/shard_map/all_to_all | solution.py:256
  88.0 2.1 %shard_map.76 = (s32[16,17,8,128]{3,2,1,0:T(8,128)}, s32[16,16,8,128]{3,2,1,0:T(8,128)}) custom-call(s32[256]{0:T(256)S(1)} %select_reduce_fusion.1.from_ref, s32[640,8,128]{2,1,0:T(8,128)S(1)} %bitcast.5, s32[8,128]{1,0:T(8,128)S(1)} %pad_add_fusion.level_ref), custom_call_target="tpu_custom_call" | custom-call | bytes 4194304 | tf_op jit(solution)/shard_map/pallas_call | solution.py:261
  90.1 1.2 %collective-permute-start.4 = (s32[16,16,8,128]{3,2,1,0:T(8,128)}, s32[16,16,8,128]{3,2,1,0:T(8,128)S(1)}, u32[]{:S(2)}, u32[]{:S(2)}) collective-permute-start(s32[16,16,8,128]{3,2,1,0:T(8,128)} %get-tuple-element.11), channel_id=1, source_target_pairs={{0,4},{1,5},{2,6},{3,7},{4,0},{5,1},{6,2},{7,3},{8,12},{9,13},{10,... | collective-permute-start | bytes 3145736 | tf_op jit(solution)/shard_map/ppermute | solution.py:209
  91.3 7.4 %all-to-all-start.3 = ((s32[16,17,8,128]{3,2,1,0:T(8,128)}), s32[16,17,8,128]{3,2,1,0:T(8,128)S(1)}, u32[]{:S(2)}, u32[]{:S(2)}) async-start(s32[16,17,8,128]{3,2,1,0:T(8,128)} %get-tuple-element.12), calls=%async_computation.3 | async-start | bytes 2228224 | tf_op jit(solution)/shard_map/all_to_all | solution.py:267
  98.7 0.7 select_reduce_fusion
  99.4 0.8 dynamic-slice_convert_fusion
  100.2 0.2 convert_reduce_fusion.1
  100.4 0.1 fusion.1.pick_ref
  100.5 14.9 %all-to-all-done.3 = s32[16,17,8,128]{3,2,1,0:T(8,128)S(1)} async-done(((s32[16,17,8,128]{3,2,1,0:T(8,128)}), s32[16,17,8,128]{3,2,1,0:T(8,128)S(1)}, u32[]{:S(2)}, u32[]{:S(2)}) %all-to-all-start.3) | async-done | bytes 1114144 | tf_op jit(solution)/shard_map/all_to_all | solution.py:267
  115.4 0.9 collective-permute-done.4
  116.4 2.5 %shard_map.77 = bf16[16,32768]{1,0:T(8,128)(2,1)} custom-call(s32[256]{0:T(256)S(1)} %convert_reduce_fusion.2.own_ref, s32[256]{0:T(256)S(1)} %fusion.3.face_ref, s32[256,8,128]{2,1,0:T(8,128)S(1)} %bitcast.7, s32[272,8,128]{2,1,0:T(8,128)S(1)} %bitcast.6, bf16[512,128]{1,0:T(8,128)(2,1)S(1)} %fusion.1.pick_ref, f32[256,128]{1,0:T(8,128)S(1)} %broadcast_in_dim.44.sign_ref), custom_call_target="tpu_custom_call" | custom-call | bytes 4194304 | tf_op jit(solution)/shard_map/pallas_call | solution.py:203
  (20 shorter events, 0.6 us)
Async XLA Ops:
  0.0 0.7 copy-start
  18.8 18.9 %all-to-all-start.1 = ((bf16[64,16,256]{2,1,0:T(8,128)(2,1)}), bf16[64,16,256]{2,1,0:T(8,128)(2,1)S(1)}, u32[]{:S(2)}, u32[]{:S(2)}) async-start(bf16[64,16,256]{2,1,0:T(8,128)(2,1)} %shard_map.74), calls=%async_computation.1 | async-start | bytes 1048576 | tf_op jit(solution)/shard_map/all_to_all | solution.py:227
  37.6 1.9 %collective-permute-start = (bf16[64,16,256]{2,1,0:T(8,128)(2,1)S(1)}, bf16[64,16,256]{2,1,0:T(8,128)(2,1)S(1)}, u32[]{:S(2)}, u32[]{:S(2)}) collective-permute-start(bf16[64,16,256]{2,1,0:T(8,128)(2,1)S(1)} %all-to-all-done.1.mine_ref), channel_id=1, source_target_pairs={{0,1},{1,0},{2,3},{3,2},{4,5},{5,4},{6,7},{7,6},{8,9},{9,8},{10,11... | collective-permute-start | bytes 1572872 | tf_op jit(solution)/shard_map/ppermute | solution.py:209
  47.3 4.7 %copy-start.1 = (s32[4096]{0:T(1024)S(1)}, s32[4096]{0:T(1024)}, u32[]{:S(2)}) copy-start(s32[4096]{0:T(1024)} %param.11) | copy-start | bytes 49156
  47.3 40.7 %all-to-all-start.2 = ((s32[128,40,128]{2,1,0:T(8,128)}), s32[128,40,128]{2,1,0:T(8,128)S(1)}, u32[]{:S(2)}, u32[]{:S(2)}) async-start(s32[128,40,128]{2,1,0:T(8,128)} %bitcast.8), calls=%async_computation.2 | async-start | bytes 5242880 | tf_op jit(solution)/shard_map/all_to_all | solution.py:256
  53.0 1.2 %collective-permute-start.1 = (s32[1,128]{1,0:T(1,128)S(1)}, s32[1,128]{1,0:T(1,128)S(1)}, u32[]{:S(2)}, u32[]{:S(2)}) collective-permute-start(s32[1,128]{1,0:T(1,128)S(1)} %slice.3), channel_id=1, source_target_pairs={{0,1},{1,0},{2,3},{3,2},{4,5},{5,4},{6,7},{7,6},{8,9},{9,8},{10,11... | collective-permute-start | bytes 1544 | tf_op jit(solution)/shard_map/ppermute | solution.py:209
  54.2 27.1 %collective-permute-start.2 = (s32[2,128]{1,0:T(2,128)S(1)}, s32[2,128]{1,0:T(2,128)S(1)}, u32[]{:S(2)}, u32[]{:S(2)}) collective-permute-start(s32[2,128]{1,0:T(2,128)S(1)} %pad_add_fusion.3), channel_id=1, source_target_pairs={{0,2},{1,3},{2,0},{3,1},{4,6},{5,7},{6,4},{7,5},{8,10},{9,11},{10,... | collective-permute-start | bytes 3080 | tf_op jit(solution)/shard_map/ppermute | solution.py:209
  81.3 5.2 %collective-permute-start.3 = (s32[4,128]{1,0:T(4,128)S(1)}, s32[4,128]{1,0:T(4,128)S(1)}, u32[]{:S(2)}, u32[]{:S(2)}) collective-permute-start(s32[4,128]{1,0:T(4,128)S(1)} %pad_add_fusion.1), channel_id=1, source_target_pairs={{0,4},{1,5},{2,6},{3,7},{4,0},{5,1},{6,2},{7,3},{8,12},{9,13},{10,... | collective-permute-start | bytes 6152 | tf_op jit(solution)/shard_map/ppermute | solution.py:209
  90.1 26.3 %collective-permute-start.4 = (s32[16,16,8,128]{3,2,1,0:T(8,128)}, s32[16,16,8,128]{3,2,1,0:T(8,128)S(1)}, u32[]{:S(2)}, u32[]{:S(2)}) collective-permute-start(s32[16,16,8,128]{3,2,1,0:T(8,128)} %get-tuple-element.11), channel_id=1, source_target_pairs={{0,4},{1,5},{2,6},{3,7},{4,0},{5,1},{6,2},{7,3},{8,12},{9,13},{10,... | collective-permute-start | bytes 3145736 | tf_op jit(solution)/shard_map/ppermute | solution.py:209
  91.3 24.1 %all-to-all-start.3 = ((s32[16,17,8,128]{3,2,1,0:T(8,128)}), s32[16,17,8,128]{3,2,1,0:T(8,128)S(1)}, u32[]{:S(2)}, u32[]{:S(2)}) async-start(s32[16,17,8,128]{3,2,1,0:T(8,128)} %get-tuple-element.12), calls=%async_computation.3 | async-start | bytes 2228224 | tf_op jit(solution)/shard_map/all_to_all | solution.py:267

commit v8 on v7

--- a/solution.py
+++ b/solution.py
@@ -52,15 +52,29 @@
     return 2 * (p ^ 4), 2 * (p ^ 4) + 1
 
 
-def product_body(irrep_ref, mine_ref, other_ref, tiles_ref, out_ref, level_ref, held, slab, prod, code, in_sems, out_sems):
+def first_body(tiles_ref, after_ref, held_ref, sems):
     def fetch(t):
         span = pl.ds(t * 5, 5)
-        return pltpu.make_async_copy(tiles_ref.at[span], held.at[span], in_sems.at[t])
+        return pltpu.make_async_copy(tiles_ref.at[span], held_ref.at[span], sems.at[t])
+
+    for t in range(GROUP):
+        fetch(t).start()
+    for t in range(GROUP):
+        fetch(t).wait()
+
+
+def product_body(
+    irrep_ref, mine_ref, other_ref, first_ref, tiles_ref, out_ref, level_ref, held, slab, prod, code, in_sems, out_sems
+):
+    def fetch(t):
+        return pltpu.make_async_copy(
+            tiles_ref.at[pl.ds(t * 5, 5)], held.at[pl.ds((t - GROUP) * 5, 5)], in_sems.at[t - GROUP]
+        )
 
     def store(t):
         return pltpu.make_async_copy(code.at[t], out_ref.at[t], out_sems.at[t])
 
-    for t in range(16):
+    for t in range(GROUP, 16):
         fetch(t).start()
     core = lax.axis_index("pair") % 2
     for source, shift in ((mine_ref, core), (other_ref, 1 - core)):
@@ -69,16 +83,14 @@
                 rows = pl.ds(pl.multiple_of((2 * x + shift) * 16, 16), 16)
                 slab[c // 2, rows, (c % 2) * 256 : (c % 2) * 256 + 256] = source[c * 4 + x]
 
-    def multiply(step, top):
-        for t in range(GROUP):
-            fetch(step * GROUP + t).wait()
-        count = GROUP * 5
+    count = GROUP * 5
+
+    def multiply(step, source, offset, top):
         values = []
         for k in range(count + 1):
             if k < count:
-                slot = step * count + k
-                left = slab[jnp.maximum(irrep_ref[slot], 0)]
-                right = held[slot].reshape(512, 128)
+                left = slab[jnp.maximum(irrep_ref[step * count + k], 0)]
+                right = source[offset + k].reshape(512, 128)
                 values.append(jnp.dot(left, right, preferred_element_type=jnp.float32))
             if k > 0:
                 slot = step * count + k - 1
@@ -88,7 +100,13 @@
                 top = jnp.maximum(top, jnp.where(irrep_ref[slot] >= 0, high, 0.0))
         return top
 
-    top = lax.fori_loop(0, 16 // GROUP, multiply, jnp.zeros((8, 128), jnp.float32))
+    def later(step, top):
+        for t in range(GROUP):
+            fetch(step * GROUP + t).wait()
+        return multiply(step, held, (step - 1) * count, top)
+
+    top = multiply(0, first_ref, 0, jnp.zeros((8, 128), jnp.float32))
+    top = lax.fori_loop(1, 16 // GROUP, later, top)
     top = jnp.max(jnp.max(top, axis=1, keepdims=True), axis=0, keepdims=True)
     level = jnp.ceil(jnp.log(jnp.maximum(top, 1e-30)) * (STEPS / LN2))
     level = jnp.broadcast_to(level, (8, 128))
@@ -175,22 +193,27 @@
         store(c).wait()
 
 
-def call_product(irreps, mine, other, tiles):
+def call_product(irreps, mine, other, first, tiles):
     dma = pltpu.SemaphoreType.DMA
     int32 = jnp.int32
     return call(
-        product_body, [SMEM, VMEM, VMEM, HBM], [HBM, VMEM],
+        product_body, [SMEM, VMEM, VMEM, VMEM, HBM], [HBM, VMEM],
         [pltpu.HBM((16, 8, 5, 8, 128), int32), jax.ShapeDtypeStruct((8, 128), int32)],
         [
-            pltpu.VMEM((80, 4, 128, 128), jnp.bfloat16),
+            pltpu.VMEM((80 - GROUP * 5, 4, 128, 128), jnp.bfloat16),
             pltpu.VMEM((8, 128, 512), jnp.bfloat16),
             pltpu.VMEM((80, 128, 128), jnp.float32),
             pltpu.VMEM((16, 8, 5, 8, 128), int32),
-            dma((16,)),
+            dma((16 - GROUP,)),
             dma((16,)),
         ],
-        52 * MIB, 1_342_177_280, 14 << 20,
-    )(irreps, mine, other, tiles)
+        48 * MIB, 1_342_177_280, 14 << 20,
+    )(irreps, mine, other, first, tiles)
+
+
+def call_first(tiles, after):
+    shape = pltpu.VMEM((GROUP * 5, 4, 128, 128), jnp.bfloat16)
+    return call(first_body, [HBM, pl.BlockSpec(memory_space=pl.ANY)], VMEM, shape, [pltpu.SemaphoreType.DMA((GROUP,))], 47 * MIB, 0, 5 << 20)(tiles, after)
 
 
 def call_combine(own, face, here, there, pick, signs):
@@ -252,7 +275,8 @@
     pick = (rows[:, None] == jnp.arange(128, dtype=int32)[None, :]).astype(jnp.bfloat16)
     signs = jnp.broadcast_to(my_sign.astype(jnp.float32)[:, None], (256, 128))
 
-    coded, level = call_product(slot_irrep, mine, other, integrals)
+    first = call_first(integrals, mine)
+    coded, level = call_product(slot_irrep, mine, other, first, integrals)
     arrived = lax.all_to_all(coded.reshape(128, 40, 128), BOTH, split_axis=0, concat_axis=0, tiled=True)
     arrived = arrived.reshape(640, 8, 128)
     levels = level[:1]

time: 120 us -> 120 us (level)
  Pallas kernels: 14.4 us -> 16 us
  waiting for transfers between devices: 58.9 us -> 57.6 us
    pallas_call x1 -> x2, Pallas kernels: 7.73 us -> 9.32 us  [the longest x1 7.6 us: call_product(): call(product_body, [SMEM, VMEM, VMEM, VMEM, HBM], [HBM, VMEM], [pltpu.HBM...]
    ppermute x5, waiting for transfers between devices: 31.7 us -> 30.3 us  [swap(): return lax.ppermute(value, 'pair', [(i, i ^ mask) for i in range(8)])]
  transfers between devices with their start and end apart: 8 -> 8, of which waited for: 8 -> 7; matrix products, arithmetic and copies ran while one was open for 4% -> 4% of each run, Pallas kernels for 0% -> 1%
where the time goes in v8:
time: 120 us; the launch traced here: 119 us
  waiting for transfers between devices  57.6 us (48%)
  starting transfers between devices  23.7 us (20%)
  Pallas kernels  16 us (13%)
  blocking collectives  15.9 us (13%)
  other arithmetic  4.71 us (4%)
    ppermute x5, waiting for transfers between devices, swap(): return lax.ppermute(value, 'pair', [(i, i ^ mask) for i in range(8)])  30.3 us
    all_to_all x1, blocking collectives, local(): lax.all_to_all(parts, 'blk', split_axis=0, concat_axis=0, tiled=True)  15.9 us
    all_to_all x1, waiting for transfers between devices, local(): lax.all_to_all(outgoing, 'blk', split_axis=0, concat_axis=0, tiled=True)  14.9 us
    all_to_all x1, waiting for transfers between devices, local(): lax.all_to_all(copies, BOTH, split_axis=0, concat_axis=0, tiled=True, axi...  10.7 us
    pallas_call x1, Pallas kernels, call_product(): call(product_body, [SMEM, VMEM, VMEM, VMEM, HBM], [HBM, VMEM], [pltpu.HBM...  7.6 us
    all_to_all x1, starting transfers between devices, local(): lax.all_to_all(outgoing, 'blk', split_axis=0, concat_axis=0, tiled=True)  7.43 us
    all_to_all x1, starting transfers between devices, local(): lax.all_to_all(copies, BOTH, split_axis=0, concat_axis=0, tiled=True, axi...  6.64 us
    ppermute x5, starting transfers between devices, swap(): return lax.ppermute(value, 'pair', [(i, i ^ mask) for i in range(8)])  4.93 us
  transfers between devices with their start and end apart: 8, of which 7 were waited for; matrix products, arithmetic and copies ran while one was open for 4% of the time, Pallas kernels for 1%

profile of v8, /device:TPU:0, one launch (start us, length us, event | category | flops | bytes accessed | tf_op | source)
XLA Modules:
  0.0 119.1 jit_solution(17422491944976525469)
XLA Ops:
  0.0 0.7 copy-done
  0.7 1.3 %shard_map.73 = bf16[16,16,256]{2,1,0:T(8,128)(2,1)S(1)} custom-call(s32[32]{0:T(128)S(1)} %copy-done, bf16[16,32768]{1,0:T(8,128)(2,1)} %amp_ref.1), custom_call_target="tpu_custom_call" | custom-call | bytes 1048576 | tf_op jit(solution)/shard_map/pallas_call | solution.py:242
  2.0 15.9 %all_to_all.20.in_ref = bf16[16,16,256]{2,1,0:T(8,128)(2,1)S(1)} all-to-all(bf16[16,16,256]{2,1,0:T(8,128)(2,1)S(1)} %shard_map.73), channel_id=1, replica_groups=mesh['blk'=16,'pair'=8] {'blk'}, dimensions={0} | all-to-all | bytes 262144 | tf_op jit(solution)/shard_map/all_to_all | solution.py:245
  17.9 0.8 shard_map.74
  18.8 6.6 %all-to-all-start.1 = ((bf16[64,16,256]{2,1,0:T(8,128)(2,1)}), bf16[64,16,256]{2,1,0:T(8,128)(2,1)S(1)}, u32[]{:S(2)}, u32[]{:S(2)}) async-start(bf16[64,16,256]{2,1,0:T(8,128)(2,1)} %shard_map.74), calls=%async_computation.1 | async-start | bytes 1048576 | tf_op jit(solution)/shard_map/all_to_all | solution.py:250
  25.4 0.7 broadcast_compare_fusion
  26.2 0.7 broadcast_add_fusion
  26.9 10.7 %all-to-all-done.1.after_ref.mine_ref = bf16[64,16,256]{2,1,0:T(8,128)(2,1)S(1)} async-done(((bf16[64,16,256]{2,1,0:T(8,128)(2,1)}), bf16[64,16,256]{2,1,0:T(8,128)(2,1)S(1)}, u32[]{:S(2)}, u32[]{:S(2)}) %all-to-all-start.1) | async-done | bytes 524320 | tf_op jit(solution)/shard_map/all_to_all | solution.py:250
  37.6 0.1 convolution_convert_fusion
  37.8 0.2 select_reduce_fusion.2
  38.2 1.7 %shard_map.75.first_ref = bf16[20,4,128,128]{3,2,1,0:T(8,128)(2,1)S(1)} custom-call(bf16[80,4,128,128]{3,2,1,0:T(8,128)(2,1)} %tiles_ref.3, bf16[64,16,256]{2,1,0:T(8,128)(2,1)S(1)} %all-to-all-done.1.after_ref.mine_ref), custom_call_target="tpu_custom_call" | custom-call | bytes 5242880 | tf_op jit(solution)/shard_map/pallas_call | solution.py:216
  39.9 7.6 %shard_map.76 = (s32[16,8,5,8,128]{4,3,2,1,0:T(8,128)}, s32[8,128]{1,0:T(8,128)S(1)}) custom-call(s32[80]{0:T(128)S(1)} %sub.19.irrep_ref, bf16[64,16,256]{2,1,0:T(8,128)(2,1)S(1)} %all-to-all-done.1.after_ref.mine_ref, bf16[64,16,256]{2,1,0:T(8,128)(2,1)S(1)} %collective-permute-done.other_ref, bf16[20,4,128,128]{3,2,1,0:T(8,128)(2,1)S(1)} %shard_map.75.first_ref, ...), custom_call_target="tpu_custom_call" | custom-call | flops 1342177280 | bytes 14680064 | tf_op jit(solution)/shard_map/pallas_call | solution.py:199
  47.5 4.7 %all-to-all-start.2 = ((s32[128,40,128]{2,1,0:T(8,128)}), s32[128,40,128]{2,1,0:T(8,128)S(1)}, u32[]{:S(2)}, u32[]{:S(2)}) async-start(s32[128,40,128]{2,1,0:T(8,128)} %bitcast.8), calls=%async_computation.2 | async-start | bytes 5242880 | tf_op jit(solution)/shard_map/all_to_all | solution.py:280
  52.2 0.8 iota_add_fusion
  53.0 0.2 convert_reduce_fusion
  53.3 1.1 collective-permute-done.1
  54.4 0.8 collective-permute-start.2
  55.2 0.2 convert_reduce_fusion.2.own_ref
  55.4 26.1 %collective-permute-done.2 = s32[2,128]{1,0:T(2,128)S(1)} collective-permute-done((s32[2,128]{1,0:T(2,128)S(1)}, s32[2,128]{1,0:T(2,128)S(1)}, u32[]{:S(2)}, u32[]{:S(2)}) %collective-permute-start.2) | collective-permute-done | bytes 1056 | tf_op jit(solution)/shard_map/ppermute | solution.py:232
  81.5 2.8 %collective-permute-start.3 = (s32[4,128]{1,0:T(4,128)S(1)}, s32[4,128]{1,0:T(4,128)S(1)}, u32[]{:S(2)}, u32[]{:S(2)}) collective-permute-start(s32[4,128]{1,0:T(4,128)S(1)} %pad_add_fusion.1), channel_id=1, source_target_pairs={{0,4},{1,5},{2,6},{3,7},{4,0},{5,1},{6,2},{7,3},{8,12},{9,13},{10,... | collective-permute-start | bytes 6152 | tf_op jit(solution)/shard_map/ppermute | solution.py:232
  84.4 2.3 %collective-permute-done.3 = s32[4,128]{1,0:T(4,128)S(1)} collective-permute-done((s32[4,128]{1,0:T(4,128)S(1)}, s32[4,128]{1,0:T(4,128)S(1)}, u32[]{:S(2)}, u32[]{:S(2)}) %collective-permute-start.3) | collective-permute-done | bytes 2080 | tf_op jit(solution)/shard_map/ppermute | solution.py:232
  86.7 1.6 %all-to-all-done.2 = s32[128,40,128]{2,1,0:T(8,128)S(1)} async-done(((s32[128,40,128]{2,1,0:T(8,128)}), s32[128,40,128]{2,1,0:T(8,128)S(1)}, u32[]{:S(2)}, u32[]{:S(2)}) %all-to-all-start.2) | async-done | bytes 2621472 | tf_op jit(solution)/shard_map/all_to_all | solution.py:280
  88.2 2.1 %shard_map.77 = (s32[16,17,8,128]{3,2,1,0:T(8,128)}, s32[16,16,8,128]{3,2,1,0:T(8,128)}) custom-call(s32[256]{0:T(256)S(1)} %select_reduce_fusion.1.from_ref, s32[640,8,128]{2,1,0:T(8,128)S(1)} %bitcast.5, s32[8,128]{1,0:T(8,128)S(1)} %pad_add_fusion.level_ref), custom_call_target="tpu_custom_call" | custom-call | bytes 4194304 | tf_op jit(solution)/shard_map/pallas_call | solution.py:285
  90.3 1.2 %collective-permute-start.4 = (s32[16,16,8,128]{3,2,1,0:T(8,128)}, s32[16,16,8,128]{3,2,1,0:T(8,128)S(1)}, u32[]{:S(2)}, u32[]{:S(2)}) collective-permute-start(s32[16,16,8,128]{3,2,1,0:T(8,128)} %get-tuple-element.11), channel_id=1, source_target_pairs={{0,4},{1,5},{2,6},{3,7},{4,0},{5,1},{6,2},{7,3},{8,12},{9,13},{10,... | collective-permute-start | bytes 3145736 | tf_op jit(solution)/shard_map/ppermute | solution.py:232
  91.5 7.4 %all-to-all-start.3 = ((s32[16,17,8,128]{3,2,1,0:T(8,128)}), s32[16,17,8,128]{3,2,1,0:T(8,128)S(1)}, u32[]{:S(2)}, u32[]{:S(2)}) async-start(s32[16,17,8,128]{3,2,1,0:T(8,128)} %get-tuple-element.12), calls=%async_computation.3 | async-start | bytes 2228224 | tf_op jit(solution)/shard_map/all_to_all | solution.py:291
  99.0 0.7 select_reduce_fusion
  99.6 0.8 dynamic-slice_convert_fusion
  100.4 0.2 convert_reduce_fusion.1
  100.6 0.1 fusion.1.pick_ref
  100.8 14.9 %all-to-all-done.3 = s32[16,17,8,128]{3,2,1,0:T(8,128)S(1)} async-done(((s32[16,17,8,128]{3,2,1,0:T(8,128)}), s32[16,17,8,128]{3,2,1,0:T(8,128)S(1)}, u32[]{:S(2)}, u32[]{:S(2)}) %all-to-all-start.3) | async-done | bytes 1114144 | tf_op jit(solution)/shard_map/all_to_all | solution.py:291
  115.7 0.9 collective-permute-done.4
  116.7 2.5 %shard_map.78 = bf16[16,32768]{1,0:T(8,128)(2,1)} custom-call(s32[256]{0:T(256)S(1)} %convert_reduce_fusion.2.own_ref, s32[256]{0:T(256)S(1)} %fusion.3.face_ref, s32[256,8,128]{2,1,0:T(8,128)S(1)} %bitcast.7, s32[272,8,128]{2,1,0:T(8,128)S(1)} %bitcast.6, bf16[512,128]{1,0:T(8,128)(2,1)S(1)} %fusion.1.pick_ref, f32[256,128]{1,0:T(8,128)S(1)} %broadcast_in_dim.44.sign_ref), custom_call_target="tpu_custom_call" | custom-call | bytes 4194304 | tf_op jit(solution)/shard_map/pallas_call | solution.py:226
  (21 shorter events, 0.6 us)
Async XLA Ops:
  0.0 0.7 copy-start
  18.8 18.9 %all-to-all-start.1 = ((bf16[64,16,256]{2,1,0:T(8,128)(2,1)}), bf16[64,16,256]{2,1,0:T(8,128)(2,1)S(1)}, u32[]{:S(2)}, u32[]{:S(2)}) async-start(bf16[64,16,256]{2,1,0:T(8,128)(2,1)} %shard_map.74), calls=%async_computation.1 | async-start | bytes 1048576 | tf_op jit(solution)/shard_map/all_to_all | solution.py:250
  37.6 2.3 %collective-permute-start = (bf16[64,16,256]{2,1,0:T(8,128)(2,1)S(1)}, bf16[64,16,256]{2,1,0:T(8,128)(2,1)S(1)}, u32[]{:S(2)}, u32[]{:S(2)}) collective-permute-start(bf16[64,16,256]{2,1,0:T(8,128)(2,1)S(1)} %all-to-all-done.1.after_ref.mine_ref), channel_id=1, source_target_pairs={{0,1},{1,0},{2,3},{3,2},{4,5},{5,4},{6,7},{7,6},{8,9},{9,8},{10,11... | collective-permute-start | bytes 1572872 | tf_op jit(solution)/shard_map/ppermute | solution.py:232
  47.5 4.7 %copy-start.1 = (s32[4096]{0:T(1024)S(1)}, s32[4096]{0:T(1024)}, u32[]{:S(2)}) copy-start(s32[4096]{0:T(1024)} %param.11) | copy-start | bytes 49156
  47.5 40.7 %all-to-all-start.2 = ((s32[128,40,128]{2,1,0:T(8,128)}), s32[128,40,128]{2,1,0:T(8,128)S(1)}, u32[]{:S(2)}, u32[]{:S(2)}) async-start(s32[128,40,128]{2,1,0:T(8,128)} %bitcast.8), calls=%async_computation.2 | async-start | bytes 5242880 | tf_op jit(solution)/shard_map/all_to_all | solution.py:280
  53.2 1.2 %collective-permute-start.1 = (s32[1,128]{1,0:T(1,128)S(1)}, s32[1,128]{1,0:T(1,128)S(1)}, u32[]{:S(2)}, u32[]{:S(2)}) collective-permute-start(s32[1,128]{1,0:T(1,128)S(1)} %slice.3), channel_id=1, source_target_pairs={{0,1},{1,0},{2,3},{3,2},{4,5},{5,4},{6,7},{7,6},{8,9},{9,8},{10,11... | collective-permute-start | bytes 1544 | tf_op jit(solution)/shard_map/ppermute | solution.py:232
  54.4 27.1 %collective-permute-start.2 = (s32[2,128]{1,0:T(2,128)S(1)}, s32[2,128]{1,0:T(2,128)S(1)}, u32[]{:S(2)}, u32[]{:S(2)}) collective-permute-start(s32[2,128]{1,0:T(2,128)S(1)} %pad_add_fusion.3), channel_id=1, source_target_pairs={{0,2},{1,3},{2,0},{3,1},{4,6},{5,7},{6,4},{7,5},{8,10},{9,11},{10,... | collective-permute-start | bytes 3080 | tf_op jit(solution)/shard_map/ppermute | solution.py:232
  81.5 5.2 %collective-permute-start.3 = (s32[4,128]{1,0:T(4,128)S(1)}, s32[4,128]{1,0:T(4,128)S(1)}, u32[]{:S(2)}, u32[]{:S(2)}) collective-permute-start(s32[4,128]{1,0:T(4,128)S(1)} %pad_add_fusion.1), channel_id=1, source_target_pairs={{0,4},{1,5},{2,6},{3,7},{4,0},{5,1},{6,2},{7,3},{8,12},{9,13},{10,... | collective-permute-start | bytes 6152 | tf_op jit(solution)/shard_map/ppermute | solution.py:232
  90.3 26.3 %collective-permute-start.4 = (s32[16,16,8,128]{3,2,1,0:T(8,128)}, s32[16,16,8,128]{3,2,1,0:T(8,128)S(1)}, u32[]{:S(2)}, u32[]{:S(2)}) collective-permute-start(s32[16,16,8,128]{3,2,1,0:T(8,128)} %get-tuple-element.11), channel_id=1, source_target_pairs={{0,4},{1,5},{2,6},{3,7},{4,0},{5,1},{6,2},{7,3},{8,12},{9,13},{10,... | collective-permute-start | bytes 3145736 | tf_op jit(solution)/shard_map/ppermute | solution.py:232
  91.5 24.1 %all-to-all-start.3 = ((s32[16,17,8,128]{3,2,1,0:T(8,128)}), s32[16,17,8,128]{3,2,1,0:T(8,128)S(1)}, u32[]{:S(2)}, u32[]{:S(2)}) async-start(s32[16,17,8,128]{3,2,1,0:T(8,128)} %get-tuple-element.12), calls=%async_computation.3 | async-start | bytes 2228224 | tf_op jit(solution)/shard_map/all_to_all | solution.py:291

commit v9 on v8

--- a/solution.py
+++ b/solution.py
@@ -148,7 +148,7 @@
         return carry
 
     for c in range(8):
-        lax.fori_loop(c * 2, c * 2 + 2, one, 0)
+        lax.fori_loop(c * 2, c * 2 + 2, one, 0, unroll=2)
         store_words(c).start()
         store(c).start()
     for c in range(8):
@@ -187,7 +187,7 @@
         return carry
 
     for c in range(8):
-        lax.fori_loop(c * 4, c * 4 + 4, one, 0)
+        lax.fori_loop(c * 4, c * 4 + 4, one, 0, unroll=4)
         store(c).start()
     for c in range(8):
         store(c).wait()

time: 120 us -> 120 us (level)
  no operation moved by 1% of the time
where the time goes in v9:
time: 120 us; the launch traced here: 119 us
  waiting for transfers between devices  57.5 us (48%)
  starting transfers between devices  23.7 us (20%)
  blocking collectives  15.9 us (13%)
  Pallas kernels  15.8 us (13%)
  other arithmetic  4.71 us (4%)
    ppermute x5, waiting for transfers between devices, swap(): return lax.ppermute(value, 'pair', [(i, i ^ mask) for i in range(8)])  30.3 us
    all_to_all x1, blocking collectives, local(): lax.all_to_all(parts, 'blk', split_axis=0, concat_axis=0, tiled=True)  15.9 us
    all_to_all x1, waiting for transfers between devices, local(): lax.all_to_all(outgoing, 'blk', split_axis=0, concat_axis=0, tiled=True)  14.9 us
    all_to_all x1, waiting for transfers between devices, local(): lax.all_to_all(copies, BOTH, split_axis=0, concat_axis=0, tiled=True, axi...  10.7 us
    pallas_call x1, Pallas kernels, call_product(): call(product_body, [SMEM, VMEM, VMEM, VMEM, HBM], [HBM, VMEM], [pltpu.HBM...  7.6 us
    all_to_all x1, starting transfers between devices, local(): lax.all_to_all(outgoing, 'blk', split_axis=0, concat_axis=0, tiled=True)  7.43 us
    all_to_all x1, starting transfers between devices, local(): lax.all_to_all(copies, BOTH, split_axis=0, concat_axis=0, tiled=True, axi...  6.64 us
    ppermute x5, starting transfers between devices, swap(): return lax.ppermute(value, 'pair', [(i, i ^ mask) for i in range(8)])  4.93 us
  transfers between devices with their start and end apart: 8, of which 7 were waited for; matrix products, arithmetic and copies ran while one was open for 4% of the time, Pallas kernels for 1%

profile of v9, /device:TPU:0, one launch (start us, length us, event | category | flops | bytes accessed | tf_op | source)
XLA Modules:
  0.0 118.9 jit_solution(9819030055057911466)
XLA Ops:
  0.0 0.7 copy-done
  0.7 1.3 %shard_map.73 = bf16[16,16,256]{2,1,0:T(8,128)(2,1)S(1)} custom-call(s32[32]{0:T(128)S(1)} %copy-done, bf16[16,32768]{1,0:T(8,128)(2,1)} %amp_ref.1), custom_call_target="tpu_custom_call" | custom-call | bytes 1048576 | tf_op jit(solution)/shard_map/pallas_call | solution.py:242
  2.0 15.9 %all_to_all.20.in_ref = bf16[16,16,256]{2,1,0:T(8,128)(2,1)S(1)} all-to-all(bf16[16,16,256]{2,1,0:T(8,128)(2,1)S(1)} %shard_map.73), channel_id=1, replica_groups=mesh['blk'=16,'pair'=8] {'blk'}, dimensions={0} | all-to-all | bytes 262144 | tf_op jit(solution)/shard_map/all_to_all | solution.py:245
  17.9 0.8 shard_map.74
  18.8 6.6 %all-to-all-start.1 = ((bf16[64,16,256]{2,1,0:T(8,128)(2,1)}), bf16[64,16,256]{2,1,0:T(8,128)(2,1)S(1)}, u32[]{:S(2)}, u32[]{:S(2)}) async-start(bf16[64,16,256]{2,1,0:T(8,128)(2,1)} %shard_map.74), calls=%async_computation.1 | async-start | bytes 1048576 | tf_op jit(solution)/shard_map/all_to_all | solution.py:250
  25.4 0.7 broadcast_compare_fusion
  26.2 0.7 broadcast_add_fusion
  26.9 10.7 %all-to-all-done.1.after_ref.mine_ref = bf16[64,16,256]{2,1,0:T(8,128)(2,1)S(1)} async-done(((bf16[64,16,256]{2,1,0:T(8,128)(2,1)}), bf16[64,16,256]{2,1,0:T(8,128)(2,1)S(1)}, u32[]{:S(2)}, u32[]{:S(2)}) %all-to-all-start.1) | async-done | bytes 524320 | tf_op jit(solution)/shard_map/all_to_all | solution.py:250
  37.6 0.1 convolution_convert_fusion
  37.8 0.2 select_reduce_fusion.2
  38.2 1.7 %shard_map.75.first_ref = bf16[20,4,128,128]{3,2,1,0:T(8,128)(2,1)S(1)} custom-call(bf16[80,4,128,128]{3,2,1,0:T(8,128)(2,1)} %tiles_ref.3, bf16[64,16,256]{2,1,0:T(8,128)(2,1)S(1)} %all-to-all-done.1.after_ref.mine_ref), custom_call_target="tpu_custom_call" | custom-call | bytes 5242880 | tf_op jit(solution)/shard_map/pallas_call | solution.py:216
  39.9 7.6 %shard_map.76 = (s32[16,8,5,8,128]{4,3,2,1,0:T(8,128)}, s32[8,128]{1,0:T(8,128)S(1)}) custom-call(s32[80]{0:T(128)S(1)} %sub.19.irrep_ref, bf16[64,16,256]{2,1,0:T(8,128)(2,1)S(1)} %all-to-all-done.1.after_ref.mine_ref, bf16[64,16,256]{2,1,0:T(8,128)(2,1)S(1)} %collective-permute-done.other_ref, bf16[20,4,128,128]{3,2,1,0:T(8,128)(2,1)S(1)} %shard_map.75.first_ref, ...), custom_call_target="tpu_custom_call" | custom-call | flops 1342177280 | bytes 14680064 | tf_op jit(solution)/shard_map/pallas_call | solution.py:199
  47.5 4.7 %all-to-all-start.2 = ((s32[128,40,128]{2,1,0:T(8,128)}), s32[128,40,128]{2,1,0:T(8,128)S(1)}, u32[]{:S(2)}, u32[]{:S(2)}) async-start(s32[128,40,128]{2,1,0:T(8,128)} %bitcast.8), calls=%async_computation.2 | async-start | bytes 5242880 | tf_op jit(solution)/shard_map/all_to_all | solution.py:280
  52.2 0.8 iota_add_fusion
  53.0 0.2 convert_reduce_fusion
  53.3 1.1 collective-permute-done.1
  54.4 0.8 collective-permute-start.2
  55.2 0.2 convert_reduce_fusion.2.own_ref
  55.4 26.1 %collective-permute-done.2 = s32[2,128]{1,0:T(2,128)S(1)} collective-permute-done((s32[2,128]{1,0:T(2,128)S(1)}, s32[2,128]{1,0:T(2,128)S(1)}, u32[]{:S(2)}, u32[]{:S(2)}) %collective-permute-start.2) | collective-permute-done | bytes 1056 | tf_op jit(solution)/shard_map/ppermute | solution.py:232
  81.5 2.8 %collective-permute-start.3 = (s32[4,128]{1,0:T(4,128)S(1)}, s32[4,128]{1,0:T(4,128)S(1)}, u32[]{:S(2)}, u32[]{:S(2)}) collective-permute-start(s32[4,128]{1,0:T(4,128)S(1)} %pad_add_fusion.1), channel_id=1, source_target_pairs={{0,4},{1,5},{2,6},{3,7},{4,0},{5,1},{6,2},{7,3},{8,12},{9,13},{10,... | collective-permute-start | bytes 6152 | tf_op jit(solution)/shard_map/ppermute | solution.py:232
  84.4 2.3 %collective-permute-done.3 = s32[4,128]{1,0:T(4,128)S(1)} collective-permute-done((s32[4,128]{1,0:T(4,128)S(1)}, s32[4,128]{1,0:T(4,128)S(1)}, u32[]{:S(2)}, u32[]{:S(2)}) %collective-permute-start.3) | collective-permute-done | bytes 2080 | tf_op jit(solution)/shard_map/ppermute | solution.py:232
  86.7 1.6 %all-to-all-done.2 = s32[128,40,128]{2,1,0:T(8,128)S(1)} async-done(((s32[128,40,128]{2,1,0:T(8,128)}), s32[128,40,128]{2,1,0:T(8,128)S(1)}, u32[]{:S(2)}, u32[]{:S(2)}) %all-to-all-start.2) | async-done | bytes 2621472 | tf_op jit(solution)/shard_map/all_to_all | solution.py:280
  88.2 2.0 %shard_map.77 = (s32[16,17,8,128]{3,2,1,0:T(8,128)}, s32[16,16,8,128]{3,2,1,0:T(8,128)}) custom-call(s32[256]{0:T(256)S(1)} %select_reduce_fusion.1.from_ref, s32[640,8,128]{2,1,0:T(8,128)S(1)} %bitcast.5, s32[8,128]{1,0:T(8,128)S(1)} %pad_add_fusion.level_ref), custom_call_target="tpu_custom_call" | custom-call | bytes 4194304 | tf_op jit(solution)/shard_map/pallas_call | solution.py:285
  90.3 1.2 %collective-permute-start.4 = (s32[16,16,8,128]{3,2,1,0:T(8,128)}, s32[16,16,8,128]{3,2,1,0:T(8,128)S(1)}, u32[]{:S(2)}, u32[]{:S(2)}) collective-permute-start(s32[16,16,8,128]{3,2,1,0:T(8,128)} %get-tuple-element.11), channel_id=1, source_target_pairs={{0,4},{1,5},{2,6},{3,7},{4,0},{5,1},{6,2},{7,3},{8,12},{9,13},{10,... | collective-permute-start | bytes 3145736 | tf_op jit(solution)/shard_map/ppermute | solution.py:232
  91.5 7.4 %all-to-all-start.3 = ((s32[16,17,8,128]{3,2,1,0:T(8,128)}), s32[16,17,8,128]{3,2,1,0:T(8,128)S(1)}, u32[]{:S(2)}, u32[]{:S(2)}) async-start(s32[16,17,8,128]{3,2,1,0:T(8,128)} %get-tuple-element.12), calls=%async_computation.3 | async-start | bytes 2228224 | tf_op jit(solution)/shard_map/all_to_all | solution.py:291
  98.9 0.7 select_reduce_fusion
  99.6 0.8 dynamic-slice_convert_fusion
  100.4 0.2 convert_reduce_fusion.1
  100.6 0.1 fusion.1.pick_ref
  100.7 14.9 %all-to-all-done.3 = s32[16,17,8,128]{3,2,1,0:T(8,128)S(1)} async-done(((s32[16,17,8,128]{3,2,1,0:T(8,128)}), s32[16,17,8,128]{3,2,1,0:T(8,128)S(1)}, u32[]{:S(2)}, u32[]{:S(2)}) %all-to-all-start.3) | async-done | bytes 1114144 | tf_op jit(solution)/shard_map/all_to_all | solution.py:291
  115.6 0.9 collective-permute-done.4
  116.6 2.3 %shard_map.78 = bf16[16,32768]{1,0:T(8,128)(2,1)} custom-call(s32[256]{0:T(256)S(1)} %convert_reduce_fusion.2.own_ref, s32[256]{0:T(256)S(1)} %fusion.3.face_ref, s32[256,8,128]{2,1,0:T(8,128)S(1)} %bitcast.7, s32[272,8,128]{2,1,0:T(8,128)S(1)} %bitcast.6, bf16[512,128]{1,0:T(8,128)(2,1)S(1)} %fusion.1.pick_ref, f32[256,128]{1,0:T(8,128)S(1)} %broadcast_in_dim.44.sign_ref), custom_call_target="tpu_custom_call" | custom-call | bytes 4194304 | tf_op jit(solution)/shard_map/pallas_call | solution.py:226
  (21 shorter events, 0.6 us)
Async XLA Ops:
  0.0 0.7 copy-start
  18.8 18.9 %all-to-all-start.1 = ((bf16[64,16,256]{2,1,0:T(8,128)(2,1)}), bf16[64,16,256]{2,1,0:T(8,128)(2,1)S(1)}, u32[]{:S(2)}, u32[]{:S(2)}) async-start(bf16[64,16,256]{2,1,0:T(8,128)(2,1)} %shard_map.74), calls=%async_computation.1 | async-start | bytes 1048576 | tf_op jit(solution)/shard_map/all_to_all | solution.py:250
  37.6 2.3 %collective-permute-start = (bf16[64,16,256]{2,1,0:T(8,128)(2,1)S(1)}, bf16[64,16,256]{2,1,0:T(8,128)(2,1)S(1)}, u32[]{:S(2)}, u32[]{:S(2)}) collective-permute-start(bf16[64,16,256]{2,1,0:T(8,128)(2,1)S(1)} %all-to-all-done.1.after_ref.mine_ref), channel_id=1, source_target_pairs={{0,1},{1,0},{2,3},{3,2},{4,5},{5,4},{6,7},{7,6},{8,9},{9,8},{10,11... | collective-permute-start | bytes 1572872 | tf_op jit(solution)/shard_map/ppermute | solution.py:232
  47.5 4.7 %copy-start.1 = (s32[4096]{0:T(1024)S(1)}, s32[4096]{0:T(1024)}, u32[]{:S(2)}) copy-start(s32[4096]{0:T(1024)} %param.11) | copy-start | bytes 49156
  47.5 40.7 %all-to-all-start.2 = ((s32[128,40,128]{2,1,0:T(8,128)}), s32[128,40,128]{2,1,0:T(8,128)S(1)}, u32[]{:S(2)}, u32[]{:S(2)}) async-start(s32[128,40,128]{2,1,0:T(8,128)} %bitcast.8), calls=%async_computation.2 | async-start | bytes 5242880 | tf_op jit(solution)/shard_map/all_to_all | solution.py:280
  53.2 1.2 %collective-permute-start.1 = (s32[1,128]{1,0:T(1,128)S(1)}, s32[1,128]{1,0:T(1,128)S(1)}, u32[]{:S(2)}, u32[]{:S(2)}) collective-permute-start(s32[1,128]{1,0:T(1,128)S(1)} %slice.3), channel_id=1, source_target_pairs={{0,1},{1,0},{2,3},{3,2},{4,5},{5,4},{6,7},{7,6},{8,9},{9,8},{10,11... | collective-permute-start | bytes 1544 | tf_op jit(solution)/shard_map/ppermute | solution.py:232
  54.4 27.1 %collective-permute-start.2 = (s32[2,128]{1,0:T(2,128)S(1)}, s32[2,128]{1,0:T(2,128)S(1)}, u32[]{:S(2)}, u32[]{:S(2)}) collective-permute-start(s32[2,128]{1,0:T(2,128)S(1)} %pad_add_fusion.3), channel_id=1, source_target_pairs={{0,2},{1,3},{2,0},{3,1},{4,6},{5,7},{6,4},{7,5},{8,10},{9,11},{10,... | collective-permute-start | bytes 3080 | tf_op jit(solution)/shard_map/ppermute | solution.py:232
  81.5 5.2 %collective-permute-start.3 = (s32[4,128]{1,0:T(4,128)S(1)}, s32[4,128]{1,0:T(4,128)S(1)}, u32[]{:S(2)}, u32[]{:S(2)}) collective-permute-start(s32[4,128]{1,0:T(4,128)S(1)} %pad_add_fusion.1), channel_id=1, source_target_pairs={{0,4},{1,5},{2,6},{3,7},{4,0},{5,1},{6,2},{7,3},{8,12},{9,13},{10,... | collective-permute-start | bytes 6152 | tf_op jit(solution)/shard_map/ppermute | solution.py:232
  90.3 26.3 %collective-permute-start.4 = (s32[16,16,8,128]{3,2,1,0:T(8,128)}, s32[16,16,8,128]{3,2,1,0:T(8,128)S(1)}, u32[]{:S(2)}, u32[]{:S(2)}) collective-permute-start(s32[16,16,8,128]{3,2,1,0:T(8,128)} %get-tuple-element.11), channel_id=1, source_target_pairs={{0,4},{1,5},{2,6},{3,7},{4,0},{5,1},{6,2},{7,3},{8,12},{9,13},{10,... | collective-permute-start | bytes 3145736 | tf_op jit(solution)/shard_map/ppermute | solution.py:232
  91.5 24.1 %all-to-all-start.3 = ((s32[16,17,8,128]{3,2,1,0:T(8,128)}), s32[16,17,8,128]{3,2,1,0:T(8,128)S(1)}, u32[]{:S(2)}, u32[]{:S(2)}) async-start(s32[16,17,8,128]{3,2,1,0:T(8,128)} %get-tuple-element.12), calls=%async_computation.3 | async-start | bytes 2228224 | tf_op jit(solution)/shard_map/all_to_all | solution.py:291
